TPU v7x, 32 devices: a whole 2x2x4 slice. The times are simulated.
32 devices in a mesh: fsdp: 4 (over x, core), sp: 8 (over z, y).
Axes of the slice: x: 2, y: 2, z: 4, core: 2. Of those that a mesh axis runs over, the one named last changes fastest.
Arguments:
- tokens: bfloat16 [2, 2048, 2048], P(None, ('fsdp', 'sp')), may hold values from -6 to 6
- cotangent: bfloat16 [2, 2048, 2048], P(None, ('fsdp', 'sp')), may hold values from -6 to 6
- seq_len: int32 [16], replicated, may hold values from 0 to 512, as said below
- slot_order: int32 [16], replicated, may hold values from 0 to 15, as said below
- norm1_gain: bfloat16 [2048], P('fsdp'), may hold values from 0.5 to 1.5
- query_weight: bfloat16 [2048, 2048], P('fsdp'), may hold values from -0.125 to 0.125
- key_weight: bfloat16 [2048, 256], P('fsdp'), may hold values from -0.125 to 0.125
- value_weight: bfloat16 [2048, 256], P('fsdp'), may hold values from -0.125 to 0.125
- output_weight: bfloat16 [2048, 2048], P('fsdp'), may hold values from -2 to 2
- norm2_gain: bfloat16 [2048], P('fsdp'), may hold values from 0.5 to 1.5
- gate_weight: bfloat16 [2048, 5632], P('fsdp'), may hold values from -0.125 to 0.125
- up_weight: bfloat16 [2048, 5632], P('fsdp'), may hold values from -0.125 to 0.125
- down_weight: bfloat16 [2048, 5632], P('fsdp'), may hold values from -0.078125 to 0.078125
Outputs:
- block_out: float32 [2, 2048, 2048], P(None, ('fsdp', 'sp'))
- input_grad: float32 [2, 2048, 2048], P(None, ('fsdp', 'sp'))
- norm1_grad: float32 [2048], P(('fsdp', 'sp'))
- query_grad: float32 [2048, 2048], P(('fsdp', 'sp'))
- key_grad: float32 [2048, 256], P(('fsdp', 'sp'))
- value_grad: float32 [2048, 256], P(('fsdp', 'sp'))
- output_grad: float32 [2048, 2048], P(('fsdp', 'sp'))
- norm2_grad: float32 [2048], P(('fsdp', 'sp'))
- gate_grad: float32 [2048, 5632], P(('fsdp', 'sp'))
- up_grad: float32 [2048, 5632], P(('fsdp', 'sp'))
- down_grad: float32 [2048, 5632], P(('fsdp', 'sp'))
Inputs may be any that keep to these rules, and one draw needn't show every extreme that they name: `seq_len`: window w = f * 2 + m holds from its first row sequence slot_order[2w], then sequence slot_order[2w + 1], then padding. For every fsdp index f one of its 2 windows holds one sequence of 512 tokens and one of length 0; every other window holds two sequences of 128 to 256 tokens. `slot_order`: A permutation of the 16 sequences.
All inputs are finite; a program needn't handle non-finite values.
Results may differ from a plain program's by a relative error of at most 0.013.
The roundings to bfloat16 on the way count: a program that leaves them out, or rounds other values in their place, can miss the bound.
Values may be sent and summed in bfloat16 or wider, within the bound.
A program may use at most 288 MiB of HBM per device.

v0:
```python
import jax
import jax.numpy as jnp
from jax import lax
from jax.sharding import PartitionSpec as P

D = 2048
HEADS = 32
KV = 4
HDIM = 64
FF = 5632
MB = 2


EPSILON = 1e-05
ROPE_BASE = 10000.0


def plain_dot(left_side, right_side):
    return jnp.dot(left_side, right_side, preferred_element_type=jnp.float32)


def contract_rows(left_side, right_side):
    return lax.dot_general(
        left_side, right_side, (((0,), (0,)), ((), ())), preferred_element_type=jnp.float32
    )


def contract_cols(left_side, right_side):
    return lax.dot_general(
        left_side, right_side, (((1,), (1,)), ((), ())), preferred_element_type=jnp.float32
    )


def window_layout(seq_len, slot_order, window_index, window):
    first_len = seq_len[slot_order[2 * window_index]]
    second_len = seq_len[slot_order[2 * window_index + 1]]
    places = jnp.arange(window, dtype=jnp.int32)
    segment = jnp.where(
        places < first_len, 0, jnp.where(places < first_len + second_len, 1, 2)
    ).astype(jnp.int32)
    anchor = jnp.where(segment == 0, 0, jnp.where(segment == 1, first_len, first_len + second_len))
    return (segment, places - anchor)


def rope_tables(position, head_size):
    half_size = head_size // 2
    inverse = ROPE_BASE ** (-2.0 * jnp.arange(half_size, dtype=jnp.float32) / head_size)
    angles = position.astype(jnp.float32)[:, None] * inverse[None, :]
    angles = jnp.concatenate([angles, angles], axis=1)
    return (jnp.cos(angles)[:, None, :], jnp.sin(angles)[:, None, :])


def apply_rope(vectors, cosine, sine):
    half_size = vectors.shape[-1] // 2
    turned = jnp.concatenate([-vectors[..., half_size:], vectors[..., :half_size]], axis=-1)
    return vectors * cosine + turned * sine


def rope_back(grad_in, cosine, sine):
    half_size = grad_in.shape[-1] // 2
    rotated = grad_in * sine
    return grad_in * cosine + jnp.concatenate(
        [rotated[..., half_size:], -rotated[..., :half_size]], axis=-1
    )


def rms_scale(inputs):
    return lax.rsqrt(jnp.mean(inputs * inputs, axis=-1, keepdims=True) + EPSILON)


def norm_back(inputs, scale_rows, gain_full, upstream):
    through = upstream * gain_full
    gain_term = jnp.sum(upstream * inputs * scale_rows, axis=0)
    grad_in = scale_rows * through - inputs * scale_rows**3 * jnp.mean(
        through * inputs, axis=-1, keepdims=True
    )
    return (grad_in, gain_term)


def score_block(query_block, key_rot, segment, row_start):
    block_rows = query_block.shape[0]
    places = jnp.arange(key_rot.shape[0], dtype=jnp.int32)
    row_place = row_start + jnp.arange(block_rows, dtype=jnp.int32)
    block_segment = lax.dynamic_slice_in_dim(segment, row_start, block_rows, 0)
    allowed = (block_segment[:, None] == segment[None, :]) & (places[None, :] <= row_place[:, None])
    raw_scores = jnp.einsum(
        "qhd,khd->hqk", query_block, key_rot, preferred_element_type=jnp.float32
    ) * query_block.shape[2] ** (-0.5)
    return jnp.where(allowed[None], raw_scores, -1e30)


def attend_forward(query_rot, key_rot, value_heads, segment):
    window = query_rot.shape[0]
    block_rows = min(512, window)

    def step(carry, block_index):
        row_start = block_index * block_rows
        query_block = lax.dynamic_slice_in_dim(query_rot, row_start, block_rows, 0)
        scores = score_block(query_block, key_rot, segment, row_start)
        row_top = jnp.max(scores, axis=-1, keepdims=True)
        weights_exp = jnp.exp(scores - row_top)
        row_total = jnp.sum(weights_exp, axis=-1, keepdims=True)
        probs = (weights_exp / row_total).astype(jnp.bfloat16)
        block_out = jnp.einsum(
            "hqk,khd->qhd", probs, value_heads, preferred_element_type=jnp.float32
        )
        log_total = (row_top + jnp.log(row_total))[:, :, 0].T
        return (carry, (block_out, log_total))

    block_ids = jnp.arange(window // block_rows, dtype=jnp.int32)
    _, (outputs, log_totals) = lax.scan(step, jnp.zeros((), jnp.int32), block_ids)
    return (outputs.reshape(query_rot.shape), log_totals.reshape(window, query_rot.shape[1]))


def attend_backward(query_rot, key_rot, value_heads, grad_heads, log_totals, segment):
    window = query_rot.shape[0]
    block_rows = min(512, window)
    scale_factor = query_rot.shape[2] ** (-0.5)

    def step(carry, block_index):
        key_acc, value_acc = carry
        row_start = block_index * block_rows
        query_block = lax.dynamic_slice_in_dim(query_rot, row_start, block_rows, 0)
        grad_block = lax.dynamic_slice_in_dim(grad_heads, row_start, block_rows, 0)
        total_block = lax.dynamic_slice_in_dim(log_totals, row_start, block_rows, 0)
        scores = score_block(query_block, key_rot, segment, row_start)
        probs = jnp.exp(scores - total_block.T[:, :, None])
        grad_probs = jnp.einsum(
            "qhd,khd->hqk", grad_block, value_heads, preferred_element_type=jnp.float32
        )
        inner_sum = jnp.sum(probs * grad_probs, axis=-1, keepdims=True)
        grad_scores = (probs * (grad_probs - inner_sum)).astype(jnp.bfloat16)
        query_part = (
            jnp.einsum("hqk,khd->qhd", grad_scores, key_rot, preferred_element_type=jnp.float32)
            * scale_factor
        )
        key_acc = (
            key_acc
            + jnp.einsum(
                "hqk,qhd->khd", grad_scores, query_block, preferred_element_type=jnp.float32
            )
            * scale_factor
        )
        value_acc = value_acc + jnp.einsum(
            "hqk,qhd->khd",
            probs.astype(jnp.bfloat16),
            grad_block,
            preferred_element_type=jnp.float32,
        )
        return ((key_acc, value_acc), query_part)

    start_acc = (jnp.zeros(key_rot.shape, jnp.float32), jnp.zeros(value_heads.shape, jnp.float32))
    block_ids = jnp.arange(window // block_rows, dtype=jnp.int32)
    (key_acc, value_acc), query_parts = lax.scan(step, start_acc, block_ids)
    return (query_parts.reshape(query_rot.shape), key_acc, value_acc)


def weight_terms(stored):
    joined = [jnp.concatenate(pieces, axis=0) for pieces in zip(*stored)]
    (
        normed,
        query_low,
        key_low,
        value_low,
        attn_rows,
        middle_low,
        normed_two,
        gate_low,
        up_low,
        upstream_low,
        hidden,
    ) = joined
    return jnp.concatenate(
        [
            contract_rows(normed, query_low),
            contract_rows(normed, key_low),
            contract_rows(normed, value_low),
            contract_rows(attn_rows, middle_low),
            contract_rows(normed_two, gate_low),
            contract_rows(normed_two, up_low),
            contract_rows(upstream_low, hidden),
        ],
        axis=1,
    )


def body(
    tokens,
    cotangent,
    seq_len,
    slot_order,
    norm1_gain,
    query_weight,
    key_weight,
    value_weight,
    output_weight,
    norm2_gain,
    gate_weight,
    up_weight,
    down_weight,
):
    seq_devices = lax.axis_size("sp")
    seq_rank = lax.axis_index("sp")
    shard_rank = lax.axis_index("fsdp")
    tok_rows = tokens.shape[1]
    window = seq_devices * tok_rows
    group_size = HEADS // KV
    kept = []
    outputs = []
    input_grads = []
    gain_sum = jnp.zeros((2, D), jnp.float32)
    grad_shards = None
    for micro_step in range(MB):
        gathered = (
            lax.all_gather(norm1_gain, "fsdp", axis=0, tiled=True),
            lax.all_gather(query_weight, "fsdp", axis=0, tiled=True),
            lax.all_gather(key_weight, "fsdp", axis=0, tiled=True),
            lax.all_gather(value_weight, "fsdp", axis=0, tiled=True),
            lax.all_gather(output_weight, "fsdp", axis=0, tiled=True),
            lax.all_gather(norm2_gain, "fsdp", axis=0, tiled=True),
            lax.all_gather(gate_weight, "fsdp", axis=0, tiled=True),
            lax.all_gather(up_weight, "fsdp", axis=0, tiled=True),
            lax.all_gather(down_weight, "fsdp", axis=0, tiled=True),
        )
        gain_one, w_query, w_key, w_value, w_output, gain_two, w_gate, w_up, w_down = gathered
        gain_one = gain_one.astype(jnp.float32)
        gain_two = gain_two.astype(jnp.float32)
        inputs = tokens[micro_step].astype(jnp.float32)
        window_index = shard_rank * MB + micro_step
        segment, position = window_layout(seq_len, slot_order, window_index, window)
        own_segment = lax.dynamic_slice_in_dim(segment, seq_rank * tok_rows, tok_rows, 0)
        valid_rows = (own_segment < 2).astype(jnp.float32)
        scale_one = rms_scale(inputs)
        normed = (inputs * scale_one * gain_one).astype(jnp.bfloat16)
        query_proj = plain_dot(normed, w_query).astype(jnp.bfloat16).reshape(tok_rows, HEADS, HDIM)
        key_proj = plain_dot(normed, w_key).astype(jnp.bfloat16).reshape(tok_rows, KV, HDIM)
        value_proj = plain_dot(normed, w_value).astype(jnp.bfloat16).reshape(tok_rows, KV, HDIM)
        packed = jnp.concatenate(
            [
                query_proj,
                jnp.repeat(key_proj, group_size, axis=1),
                jnp.repeat(value_proj, group_size, axis=1),
            ],
            axis=2,
        )
        head_side = lax.all_to_all(packed, "sp", split_axis=1, concat_axis=0, tiled=True)
        cosine, sine = rope_tables(position, HDIM)
        query_rot = apply_rope(head_side[:, :, :HDIM].astype(jnp.float32), cosine, sine).astype(
            jnp.bfloat16
        )
        key_rot = apply_rope(
            head_side[:, :, HDIM : 2 * HDIM].astype(jnp.float32), cosine, sine
        ).astype(jnp.bfloat16)
        value_heads = head_side[:, :, 2 * HDIM :]
        attended, log_totals = attend_forward(query_rot, key_rot, value_heads, segment)
        token_side = lax.all_to_all(
            attended.astype(jnp.bfloat16), "sp", split_axis=0, concat_axis=1, tiled=True
        )
        attn_rows = token_side.reshape(tok_rows, D)
        middle = inputs + plain_dot(attn_rows, w_output)
        scale_two = rms_scale(middle)
        normed_two = (middle * scale_two * gain_two).astype(jnp.bfloat16)
        gate_proj = plain_dot(normed_two, w_gate)
        up_proj = plain_dot(normed_two, w_up)
        gate_sig = jax.nn.sigmoid(gate_proj)
        hidden = (gate_proj * gate_sig * up_proj).astype(jnp.bfloat16)
        outputs.append(middle + contract_cols(hidden, w_down))
        upstream = cotangent[micro_step].astype(jnp.float32) * valid_rows[:, None]
        upstream_low = upstream.astype(jnp.bfloat16)
        hidden_grad = plain_dot(upstream_low, w_down)
        up_low = (hidden_grad * gate_proj * gate_sig).astype(jnp.bfloat16)
        gate_low = (hidden_grad * up_proj * gate_sig * (1.0 + gate_proj * (1.0 - gate_sig))).astype(
            jnp.bfloat16
        )
        normed_two_grad = contract_cols(gate_low, w_gate) + contract_cols(up_low, w_up)
        middle_grad, gain_two_term = norm_back(middle, scale_two, gain_two, normed_two_grad)
        middle_grad = middle_grad + upstream
        middle_low = middle_grad.astype(jnp.bfloat16)
        attn_grad = (
            contract_cols(middle_low, w_output).astype(jnp.bfloat16).reshape(tok_rows, HEADS, HDIM)
        )
        grad_heads = lax.all_to_all(attn_grad, "sp", split_axis=1, concat_axis=0, tiled=True)
        query_part, key_acc, value_acc = attend_backward(
            query_rot, key_rot, value_heads, grad_heads, log_totals, segment
        )
        packed_grad = jnp.concatenate(
            [rope_back(query_part, cosine, sine), rope_back(key_acc, cosine, sine), value_acc],
            axis=2,
        )
        grad_tokens = lax.all_to_all(packed_grad, "sp", split_axis=0, concat_axis=1, tiled=True)
        query_low = grad_tokens[:, :, :HDIM].reshape(tok_rows, D).astype(jnp.bfloat16)
        key_low = (
            grad_tokens[:, :, HDIM : 2 * HDIM]
            .reshape(tok_rows, KV, group_size, HDIM)
            .sum(axis=2)
            .reshape(tok_rows, KV * HDIM)
            .astype(jnp.bfloat16)
        )
        value_low = (
            grad_tokens[:, :, 2 * HDIM :]
            .reshape(tok_rows, KV, group_size, HDIM)
            .sum(axis=2)
            .reshape(tok_rows, KV * HDIM)
            .astype(jnp.bfloat16)
        )
        normed_grad = (
            contract_cols(query_low, w_query)
            + contract_cols(key_low, w_key)
            + contract_cols(value_low, w_value)
        )
        inputs_grad, gain_one_term = norm_back(inputs, scale_one, gain_one, normed_grad)
        input_grads.append(inputs_grad + middle_grad)
        gain_sum = gain_sum + jnp.stack([gain_one_term, gain_two_term])
        kept.append(
            (
                normed,
                query_low,
                key_low,
                value_low,
                attn_rows,
                middle_low,
                normed_two,
                gate_low,
                up_low,
                upstream_low,
                hidden,
            )
        )
        grad_shards = None
    grad_shards = lax.psum_scatter(
        weight_terms(kept), ("fsdp", "sp"), scatter_dimension=0, tiled=True
    )
    gain_shards = lax.psum_scatter(gain_sum, ("fsdp", "sp"), scatter_dimension=1, tiled=True)
    kv_width = KV * HDIM
    edges = [
        0,
        D,
        D + kv_width,
        D + 2 * kv_width,
        2 * D + 2 * kv_width,
        2 * D + 2 * kv_width + FF,
        2 * D + 2 * kv_width + 2 * FF,
        2 * D + 2 * kv_width + 3 * FF,
    ]
    pieces = [grad_shards[:, edges[slot] : edges[slot + 1]] for slot in range(7)]
    return (
        jnp.stack(outputs),
        jnp.stack(input_grads),
        gain_shards[0],
        pieces[0],
        pieces[1],
        pieces[2],
        pieces[3],
        gain_shards[1],
        pieces[4],
        pieces[5],
        pieces[6],
    )


def solution(mesh):
    placed = (
        P(None, ("fsdp", "sp"), None),
        P(None, ("fsdp", "sp"), None),
        P(),
        P(),
        P("fsdp"),
        P("fsdp", None),
        P("fsdp", None),
        P("fsdp", None),
        P("fsdp", None),
        P("fsdp"),
        P("fsdp", None),
        P("fsdp", None),
        P("fsdp", None),
    )
    return jax.shard_map(
        body,
        mesh=mesh,
        in_specs=placed,
        out_specs=(
            P(None, ("fsdp", "sp"), None),
            P(None, ("fsdp", "sp"), None),
            P(("fsdp", "sp")),
            P(("fsdp", "sp"), None),
            P(("fsdp", "sp"), None),
            P(("fsdp", "sp"), None),
            P(("fsdp", "sp"), None),
            P(("fsdp", "sp")),
            P(("fsdp", "sp"), None),
            P(("fsdp", "sp"), None),
            P(("fsdp", "sp"), None),
        ),
        check_vma=False,
    )
```

profile of v0, /device:TPU:0, one launch (start us, length us, event | category | flops | bytes accessed | tf_op | source)
XLA Modules:
  0.0 2476.1 jit_solution(10302331865943642928)
XLA Ops:
  11.9 6.1 all-gather
  19.0 10.0 all-gather.14.cloned.1.call-done
  30.7 16.7 all-gather.12.cloned.1.call-done
  49.0 58.2 %all-gather.10.cloned.1.call-done = bf16[2048,2048]{1,0:T(8,128)(2,1)} async-done(((bf16[512,2048]{1,0:T(8,128)(2,1)}), bf16[2048,2048]{1,0:T(8,128)(2,1)}) %all-gather.10.cloned.1.call-update) | async-done | bytes 8388624 | tf_op jit(solution)/shard_map/all_gather | solution.py:216
  160.5 15.6 all-to-all-done
  226.2 85.5 %all-gather.20.cloned.1.call-done = bf16[2048,5632]{1,0:T(8,128)(2,1)} async-done(((bf16[512,5632]{1,0:T(8,128)(2,1)}), bf16[2048,5632]{1,0:T(8,128)(2,1)}) %all-gather.20.cloned.1.call-update) | async-done | bytes 23068688 | tf_op jit(solution)/shard_map/all_gather | solution.py:222
  311.7 11.6 fusion.119
  323.3 133.1 %all-gather.18.cloned.1.call-done = bf16[2048,5632]{1,0:T(8,128)(2,1)} async-done(((bf16[512,5632]{1,0:T(8,128)(2,1)}), bf16[2048,5632]{1,0:T(8,128)(2,1)}) %all-gather.18.cloned.1.call-update) | async-done | bytes 23068688 | tf_op jit(solution)/shard_map/all_gather | solution.py:221
  456.4 10.8 fusion.118
  467.2 134.1 %all-gather.22.cloned.1.call-done = bf16[2048,5632]{1,0:T(8,128)(2,1)} async-done(((bf16[512,5632]{1,0:T(8,128)(2,1)}), bf16[2048,5632]{1,0:T(8,128)(2,1)}) %all-gather.22.cloned.1.call-update) | async-done | bytes 23068688 | tf_op jit(solution)/shard_map/all_gather | solution.py:223
  601.2 13.5 multiply_convert_fusion.4
  614.7 11.9 fusion.122
  626.7 12.6 multiply_reduce_fusion.3
  639.3 9.7 fusion.121
  649.0 9.9 fusion.120
  658.9 12.6 multiply_convert_fusion.2
  671.5 11.9 fusion.124
  683.5 12.2 multiply_reduce_fusion.2
  697.9 6.1 convolution_convert_fusion
  713.6 6.0 convolution_convert_fusion.1
  764.2 38.4 %all-to-all-done.7 = f32[512,4,192]{2,1,0:T(4,128)} async-done(((f32[512,4,192]{2,1,0:T(4,128)}), f32[512,4,192]{2,1,0:T(4,128)}, u32[]{:S(2)}, u32[]{:S(2)}) %all-to-all-start.7) | async-done | bytes 1572896 | tf_op jit(solution)/shard_map/all_to_all | solution.py:290
  809.7 44.9 %all-to-all-done.5 = f32[512,4,192]{2,1,0:T(4,128)S(1)} async-done(((f32[512,4,192]{2,1,0:T(4,128)}), f32[512,4,192]{2,1,0:T(4,128)S(1)}, u32[]{:S(2)}, u32[]{:S(2)}) %all-to-all-start.5) | async-done | bytes 1572896 | tf_op jit(solution)/shard_map/all_to_all | solution.py:290
  858.0 8.3 convolution_dynamic-update-slice_fusion.4
  872.4 6.2 fusion.123
  886.8 9.4 convolution_dynamic-update-slice_fusion.3
  896.3 18.3 convolution_dynamic-update-slice_fusion.2
  914.6 18.0 convolution_dynamic-update-slice_fusion.1
  932.6 18.0 convolution_dynamic-update-slice_fusion
  951.7 11.5 fusion.4
  963.3 11.9 fusion.5
  977.8 38.5 %reduce-scatter.7.cloned.1.call-done = f32[64,2]{1,0:T(8,128)} async-done(((f32[2048,2]{1,0:T(8,128)}), f32[64,2]{1,0:T(8,128)}) %reduce-scatter.7.cloned.1.call-update) | async-done | bytes 528
  1018.4 1442.7 %reduce-scatter.5.cloned.1.call-done = f32[64,21504]{1,0:T(8,128)} async-done(((f32[2048,21504]{1,0:T(8,128)}), f32[64,21504]{1,0:T(8,128)}) %reduce-scatter.5.cloned.1.call-update) | async-done | bytes 5505040 | tf_op jit(solution)/shard_map/reduce_scatter | solution.py:330
  (359 shorter events, 195.7 us)
Async XLA Ops:
  7.2 21.8 all-gather.14.cloned.1.call-start
  7.9 39.4 %all-gather.12.cloned.1.call-start = ((), (), s32[]{:S(2)}) async-start(), calls=%async_computation.11 | async-start | bytes 1310720 | tf_op jit(solution)/shard_map/all_gather | solution.py:217
  8.7 98.6 %all-gather.10.cloned.1.call-start = ((), (), s32[]{:S(2)}) async-start(), calls=%async_computation.10 | async-start | bytes 10485760 | tf_op jit(solution)/shard_map/all_gather | solution.py:216
  9.4 209.0 %all-gather.16.cloned.1.call-start = ((), (), s32[]{:S(2)}) async-start(), calls=%async_computation.13 | async-start | bytes 10485760 | tf_op jit(solution)/shard_map/all_gather | solution.py:219
  10.0 301.7 %all-gather.20.cloned.1.call-start = ((), (), s32[]{:S(2)}) async-start(), calls=%async_computation.15 | async-start | bytes 28835840 | tf_op jit(solution)/shard_map/all_gather | solution.py:222
  10.6 445.8 %all-gather.18.cloned.1.call-start = ((), (), s32[]{:S(2)}) async-start(), calls=%async_computation.14 | async-start | bytes 28835840 | tf_op jit(solution)/shard_map/all_gather | solution.py:221
  11.2 590.1 %all-gather.22.cloned.1.call-start = ((), (), s32[]{:S(2)}) async-start(), calls=%async_computation.16 | async-start | bytes 28835840 | tf_op jit(solution)/shard_map/all_gather | solution.py:223
  18.1 89.2 %copy-start.70 = (f32[4,1,512]{2,1,0:T(1,128)}, f32[4,1,512]{2,1,0:T(1,128)S(1)}, u32[]{:S(2)}) copy-start(f32[4,1,512]{2,1,0:T(1,128)S(1)} %convert_element_type.278) | copy-start | bytes 24580
  18.8 88.4 %copy-start.75 = (f32[64]{0:T(128)}, f32[64]{0:T(128)S(1)}, u32[]{:S(2)}) copy-start(f32[64]{0:T(128)S(1)} %get-tuple-element.200) | copy-start | bytes 772
  18.8 88.4 %copy-start.78 = (f32[64]{0:T(128)}, f32[64]{0:T(128)S(1)}, u32[]{:S(2)}) copy-start(f32[64]{0:T(128)S(1)} %get-tuple-element.232) | copy-start | bytes 772
  19.0 88.2 %copy-start.11 = (bf16[64,2048]{1,0:T(8,128)(2,1)}, bf16[64,2048]{1,0:T(8,128)(2,1)S(1)}, u32[]{:S(2)}) copy-start(bf16[64,2048]{1,0:T(8,128)(2,1)S(1)} %get-tuple-element.167) | copy-start | bytes 786436
  19.0 114.3 %copy-start.9 = (bf16[64,2048]{1,0:T(8,128)(2,1)}, bf16[64,2048]{1,0:T(8,128)(2,1)S(1)}, u32[]{:S(2)}) copy-start(bf16[64,2048]{1,0:T(8,128)(2,1)S(1)} %get-tuple-element.166) | copy-start | bytes 786436
  112.2 20.3 copy-start.5
  112.8 20.2 copy-start.7
  114.7 31.7 %all-to-all-start.2 = ((bf16[64,32,192]{2,0,1:T(8,128)(2,1)}), bf16[64,32,192]{2,0,1:T(8,128)(2,1)S(1)}, u32[]{:S(2)}, u32[]{:S(2)}) async-start(bf16[64,32,192]{2,0,1:T(8,128)(2,1)} %pad_maximum_fusion.3), calls=%async_computation.2 | async-start | bytes 2097152 | tf_op jit(solution)/shard_map/all_to_all | solution.py:246
  146.4 29.8 %all-to-all-start = ((bf16[64,32,192]{2,0,1:T(8,128)(2,1)}), bf16[64,32,192]{2,0,1:T(8,128)(2,1)S(1)}, u32[]{:S(2)}, u32[]{:S(2)}) async-start(bf16[64,32,192]{2,0,1:T(8,128)(2,1)} %pad_maximum_fusion.2), calls=%async_computation | async-start | bytes 2097152 | tf_op jit(solution)/shard_map/all_to_all | solution.py:246
  184.1 14.7 all-to-all-start.3
  194.5 23.9 copy-start.18
  198.7 15.1 all-to-all-start.1
  223.7 472.0 %copy-start.13 = (f32[64,2048]{1,0:T(8,128)}, f32[64,2048]{1,0:T(8,128)S(1)}, u32[]{:S(2)}) copy-start(f32[64,2048]{1,0:T(8,128)S(1)} %get-tuple-element.222) | copy-start | bytes 1572868
  226.0 469.7 %copy-start.15 = (f32[64,2048]{1,0:T(8,128)}, f32[64,2048]{1,0:T(8,128)S(1)}, u32[]{:S(2)}) copy-start(f32[64,2048]{1,0:T(8,128)S(1)} %get-tuple-element.220) | copy-start | bytes 1572868
  226.2 230.2 %copy-start.31 = (bf16[64,2048]{1,0:T(8,128)(2,1)}, bf16[64,2048]{1,0:T(8,128)(2,1)S(1)}, u32[]{:S(2)}) copy-start(bf16[64,2048]{1,0:T(8,128)(2,1)S(1)} %multiply_convert_fusion.9) | copy-start | bytes 786436
  707.6 15.4 all-to-all-start.6
  723.0 13.4 all-to-all-start.4
  749.1 53.5 %all-to-all-start.7 = ((f32[512,4,192]{2,1,0:T(4,128)}), f32[512,4,192]{2,1,0:T(4,128)}, u32[]{:S(2)}, u32[]{:S(2)}) async-start(f32[512,4,192]{2,1,0:T(4,128)} %copy.212), calls=%async_computation.7 | async-start | bytes 4194304 | tf_op jit(solution)/shard_map/all_to_all | solution.py:290
  802.6 52.1 %all-to-all-start.5 = ((f32[512,4,192]{2,1,0:T(4,128)}), f32[512,4,192]{2,1,0:T(4,128)S(1)}, u32[]{:S(2)}, u32[]{:S(2)}) async-start(f32[512,4,192]{2,1,0:T(4,128)} %copy.199), calls=%async_computation.5 | async-start | bytes 4194304 | tf_op jit(solution)/shard_map/all_to_all | solution.py:290
  806.2 210.1 %reduce-scatter.7.cloned.1.call-start = ((), (), s32[]{:S(2)}) async-start(), calls=%async_computation.18 | async-start | bytes 1081344
  882.9 1578.2 %reduce-scatter.5.cloned.1.call-start = ((), (), s32[]{:S(2)}) async-start(), calls=%async_computation.17 | async-start | bytes 181665792 | tf_op jit(solution)/shard_map/reduce_scatter | solution.py:330
  896.3 18.3 copy-start.22
  896.3 18.3 copy-start.26
  914.5 18.0 copy-start.23
  914.5 18.0 copy-start.24
  (70 other events, 463.7 us)
Sparse Core Ops, SparseCore 0:
  9.6 19.4 all-gather.13
  30.6 16.7 all-gather.11
  48.9 58.2 all-gather.9
  108.6 58.2 all-gather.15
  168.4 143.2 all-gather.19
  313.1 143.2 all-gather.17
  457.9 143.2 all-gather.21
  883.0 133.2 reduce-scatter.6
  1023.9 1437.1 reduce-scatter.4
where the time goes:
time: 2480 us
  waiting for transfers between devices  2030 us (82%)
  matrix products  281 us (11%)
  local copies, waits for them, and re-layouts  59.4 us (2%)
  starting transfers between devices  39.6 us (2%)
  other arithmetic  29.4 us (1%)
  between operations  26.1 us (1%)
    reduce_scatter x1, waiting for transfers between devices, body(): lax.psum_scatter(weight_terms(kept), ('fsdp', 'sp'), scatter_dimension=0,...  1440 us
    all_gather x1, waiting for transfers between devices, body(): lax.all_gather(down_weight, 'fsdp', axis=0, tiled=True)  134 us
    all_gather x1, waiting for transfers between devices, body(): lax.all_gather(gate_weight, 'fsdp', axis=0, tiled=True)  133 us
    dot_general x14, matrix products, contract_cols(): lax.dot_general(left_side, right_side, (((1,), (1,)), ((), ())), preferre...  99.1 us
    dot_general x14, matrix products, plain_dot(): return jnp.dot(left_side, right_side, preferred_element_type=jnp.float32)  88.5 us
    all_gather x1, waiting for transfers between devices, body(): lax.all_gather(up_weight, 'fsdp', axis=0, tiled=True)  85.5 us
    all_to_all x2, waiting for transfers between devices, body(): lax.all_to_all(packed_grad, 'sp', split_axis=0, concat_axis=1, tiled=True)  83.3 us
    dot_general x7, matrix products, contract_rows(): lax.dot_general(left_side, right_side, (((0,), (0,)), ((), ())), preferre...  75.9 us
  transfers between devices with their start and end apart: 17, of which 14 were waited for; matrix products, arithmetic and copies ran while one was open for 8% of the time, Pallas kernels for 0%

commit v1 on v0

--- a/solution.py
+++ b/solution.py
@@ -358,7 +358,224 @@
     )
 
 
+def silu_parts(gate_proj):
+    gate_sig = jax.nn.sigmoid(gate_proj)
+    return gate_sig, gate_proj * gate_sig
+
+
+def turned(vectors):
+    half_size = vectors.shape[-1] // 2
+    return jnp.concatenate([-vectors[..., half_size:], vectors[..., :half_size]], axis=-1)
+
+
+def group_body(
+    tokens,
+    cotangent,
+    seq_len,
+    slot_order,
+    norm1_gain,
+    query_weight,
+    key_weight,
+    value_weight,
+    output_weight,
+    norm2_gain,
+    gate_weight,
+    up_weight,
+    down_weight,
+):
+    n_sp = lax.axis_size("sp")
+    n_fsdp = lax.axis_size("fsdp")
+    group = n_sp // MB
+    rank = lax.axis_index("sp")
+    shard = lax.axis_index("fsdp")
+    micro = rank // group
+    member = rank % group
+    tok_rows = tokens.shape[1]
+    window = n_sp * tok_rows
+    own_rows = MB * tok_rows
+    groups = [[m * group + t for t in range(group)] for m in range(MB)]
+    flat = lambda f, s: f * n_sp + s
+
+    def swap(array):
+        return lax.ppermute(array, "sp", [(s, (s + group) % n_sp) for s in range(n_sp)])
+
+    def pick(pair, index):
+        return lax.dynamic_index_in_dim(pair, index, 0, keepdims=False)
+
+    def in_order(mine, theirs):
+        return jnp.where(micro == 0, jnp.concatenate([mine, theirs]), jnp.concatenate([theirs, mine]))
+
+    def gather_rows(array):
+        return lax.all_gather(array, "sp", axis=0, tiled=True, axis_index_groups=groups)
+
+    def sum_rows(partial):
+        pieces = lax.all_to_all(
+            partial.astype(jnp.bfloat16).reshape(group, own_rows, D),
+            "sp", split_axis=0, concat_axis=0, tiled=True, axis_index_groups=groups,
+        )
+        return jnp.sum(pieces.astype(jnp.float32), axis=0)
+
+    def gather_weight(weight):
+        width = weight.shape[1] // group
+        part = lax.dynamic_slice_in_dim(weight, member * width, width, 1)
+        return lax.all_gather(part, "fsdp", axis=0, tiled=True)
+
+    def reduce_weight(partial):
+        width = partial.shape[1]
+        rows = partial.reshape(2, 2, MB, group, tok_rows, width)
+
+        def halve(array, axis, index, axis_name, perm):
+            keep = lax.dynamic_index_in_dim(array, index, axis, keepdims=False)
+            send = lax.dynamic_index_in_dim(array, 1 - index, axis, keepdims=False)
+            got = lax.ppermute(send.astype(jnp.bfloat16), axis_name, perm)
+            return keep + got.astype(jnp.float32)
+
+        rows = halve(rows, 1, shard % 2, "fsdp", [(f, f ^ 1) for f in range(n_fsdp)])
+        rows = halve(rows, 0, shard // 2, "fsdp", [(f, f ^ 2) for f in range(n_fsdp)])
+        rows = halve(rows, 0, micro, "sp", [(s, (s + group) % n_sp) for s in range(n_sp)])
+        rows = lax.all_to_all(
+            rows.astype(jnp.bfloat16), "sp", split_axis=0, concat_axis=0, tiled=True, axis_index_groups=groups
+        )
+        return rows.astype(jnp.float32).transpose(1, 0, 2).reshape(tok_rows, group * width)
+
+    w_query = gather_weight(query_weight)
+    w_key = gather_weight(key_weight)
+    w_value = gather_weight(value_weight)
+    both = ("fsdp", "sp")
+    members = [(m * group + t, t) for m in range(MB) for t in range(group)]
+    over_x = lax.ppermute(output_weight, both, [(flat(t, s), flat(t ^ 2, s)) for s, t in members])
+    held = jnp.where(shard == member, output_weight, over_x)
+    over_core = lax.ppermute(
+        held, both, [(flat(t ^ k, s), flat(t ^ k ^ 1, s)) for s, t in members for k in (0, 2)]
+    )
+    w_output = jnp.where((shard & 1) == (member & 1), held, over_core)
+    w_gate = gather_weight(gate_weight)
+    w_up = gather_weight(up_weight)
+    w_down = gather_weight(down_weight)
+    gain_one = lax.all_gather(norm1_gain, "fsdp", axis=0, tiled=True).astype(jnp.float32)
+    gain_two = lax.all_gather(norm2_gain, "fsdp", axis=0, tiled=True).astype(jnp.float32)
+
+    ids = jnp.arange(window, dtype=jnp.int32)
+    owner, half, inner = ids // own_rows, (ids // tok_rows) % MB, ids % tok_rows
+    place = (half * group + owner) * tok_rows + inner
+    window_index = shard * MB + micro
+    first_len = seq_len[slot_order[2 * window_index]]
+    second_len = seq_len[slot_order[2 * window_index + 1]]
+    segment = jnp.where(place < first_len, 0, jnp.where(place < first_len + second_len, 1, 2))
+    anchor = jnp.where(segment == 0, 0, jnp.where(segment == 1, first_len, first_len + second_len))
+    position = place - anchor
+    allowed = (segment[:, None] == segment[None, :]) & (place[None, :] <= place[:, None])
+    valid = (segment < 2).astype(jnp.float32)
+    own_valid = lax.dynamic_slice_in_dim(valid, member * own_rows, own_rows, 0)
+    cosine, sine = rope_tables(position, HDIM)
+
+    own_tokens = in_order(pick(tokens, micro), swap(pick(tokens, 1 - micro)))
+    own_cot = in_order(pick(cotangent, micro), swap(pick(cotangent, 1 - micro)))
+    inputs = own_tokens.astype(jnp.float32)
+    upstream = own_cot.astype(jnp.float32) * own_valid[:, None]
+    upstream_low = gather_rows(upstream.astype(jnp.bfloat16))
+
+    scale_one = rms_scale(inputs)
+    normed = gather_rows((inputs * scale_one * gain_one).astype(jnp.bfloat16))
+    heads = HEADS // group
+    query = plain_dot(normed, w_query).astype(jnp.bfloat16).astype(jnp.float32).reshape(window, heads, HDIM)
+    key = plain_dot(normed, w_key).astype(jnp.bfloat16).astype(jnp.float32).reshape(window, 1, HDIM)
+    value = plain_dot(normed, w_value).astype(jnp.bfloat16)
+    query_rot = apply_rope(query, cosine, sine).astype(jnp.bfloat16)
+    key_rot = apply_rope(key, cosine, sine).astype(jnp.bfloat16)[:, 0]
+
+    scale = HDIM**-0.5
+    scores = jnp.einsum("qhd,kd->hqk", query_rot, key_rot, preferred_element_type=jnp.float32) * scale
+    scores = jnp.where(allowed[None], scores, -1e30)
+    top = jnp.max(scores, axis=-1, keepdims=True)
+    weights_exp = jnp.exp(scores - top)
+    probs = weights_exp / jnp.sum(weights_exp, axis=-1, keepdims=True)
+    probs_low = probs.astype(jnp.bfloat16)
+    attended = jnp.einsum("hqk,kd->qhd", probs_low, value, preferred_element_type=jnp.float32)
+    attended = attended.astype(jnp.bfloat16).reshape(window, heads * HDIM)
+
+    middle = inputs + sum_rows(plain_dot(attended, w_output))
+    scale_two = rms_scale(middle)
+    normed_two = gather_rows((middle * scale_two * gain_two).astype(jnp.bfloat16))
+    gate = plain_dot(normed_two, w_gate)
+    up = plain_dot(normed_two, w_up)
+    sig, silu = silu_parts(gate)
+    hidden = (silu * up).astype(jnp.bfloat16)
+    block = middle + sum_rows(contract_cols(hidden, w_down))
+    d_hidden = plain_dot(upstream_low, w_down)
+    d_up = (d_hidden * silu).astype(jnp.bfloat16)
+    d_gate = (d_hidden * up * sig * (1.0 + gate * (1.0 - sig))).astype(jnp.bfloat16)
+    d_normed_two = sum_rows(contract_cols(d_gate, w_gate) + contract_cols(d_up, w_up))
+    d_middle, gain_two_term = norm_back(middle, scale_two, gain_two, d_normed_two)
+    d_middle = d_middle + upstream
+    middle_low = gather_rows(d_middle.astype(jnp.bfloat16))
+
+    d_attended = contract_cols(middle_low, w_output).astype(jnp.bfloat16).reshape(window, heads, HDIM)
+    d_probs = jnp.einsum("qhd,kd->hqk", d_attended, value, preferred_element_type=jnp.float32)
+    inner_sum = jnp.sum(probs * d_probs, axis=-1, keepdims=True)
+    d_scores = (probs * (d_probs - inner_sum)).astype(jnp.bfloat16)
+    d_query_rot = jnp.einsum("hqk,kd->qhd", d_scores, key_rot, preferred_element_type=jnp.float32) * scale
+    d_key_rot = jnp.einsum("hqk,qhd->kd", d_scores, query_rot, preferred_element_type=jnp.float32) * scale
+    d_value = jnp.einsum("hqk,qhd->kd", probs_low, d_attended, preferred_element_type=jnp.float32)
+    d_query = rope_back(d_query_rot, cosine, sine).astype(jnp.bfloat16).reshape(window, heads * HDIM)
+    d_key = rope_back(d_key_rot[:, None], cosine, sine)[:, 0].astype(jnp.bfloat16)
+    d_value = d_value.astype(jnp.bfloat16)
+    d_normed = sum_rows(
+        contract_cols(d_query, w_query) + contract_cols(d_key, w_key) + contract_cols(d_value, w_value)
+    )
+    d_inputs, gain_one_term = norm_back(inputs, scale_one, gain_one, d_normed)
+    d_inputs = d_inputs + d_middle
+
+    def to_owner(rows):
+        halves = rows.reshape(MB, tok_rows, D)
+        mine, theirs = pick(halves, micro), swap(pick(halves, 1 - micro))
+        return jnp.where(micro == 0, jnp.stack([mine, theirs]), jnp.stack([theirs, mine]))
+
+    gate_grad = reduce_weight(contract_rows(normed_two, d_gate))
+    up_grad = reduce_weight(contract_rows(normed_two, d_up))
+    down_grad = reduce_weight(contract_rows(upstream_low, hidden))
+    query_grad = reduce_weight(contract_rows(normed, d_query))
+    key_grad = reduce_weight(contract_rows(normed, d_key))
+    value_grad = reduce_weight(contract_rows(normed, d_value))
+
+    output_part = contract_rows(attended, middle_low)
+    got = lax.ppermute(
+        output_part.astype(jnp.bfloat16), both,
+        [(flat(t ^ k ^ 1, s), flat(t ^ k, s)) for s, t in members for k in (0, 2)],
+    )
+    output_part = output_part + got.astype(jnp.float32)
+    got = lax.ppermute(
+        output_part.astype(jnp.bfloat16), both, [(flat(t ^ 2, s), flat(t, s)) for s, t in members]
+    )
+    output_part = (output_part + got.astype(jnp.float32)).reshape(MB, group * tok_rows, D)
+    got = swap(pick(output_part, 1 - micro).astype(jnp.bfloat16))
+    output_part = pick(output_part, micro) + got.astype(jnp.float32)
+    pieces = lax.all_to_all(
+        output_part.astype(jnp.bfloat16).reshape(group, tok_rows, D),
+        "sp", split_axis=0, concat_axis=0, tiled=True, axis_index_groups=groups,
+    )
+    output_grad = pick(pieces, shard).astype(jnp.float32)
+
+    gains = lax.psum_scatter(
+        jnp.stack([gain_one_term, gain_two_term]), both, scatter_dimension=1, tiled=True
+    )
+    return (
+        to_owner(block),
+        to_owner(d_inputs),
+        gains[0],
+        query_grad,
+        key_grad,
+        value_grad,
+        output_grad,
+        gains[1],
+        gate_grad,
+        up_grad,
+        down_grad,
+    )
+
+
 def solution(mesh):
+    fits = mesh.shape["fsdp"] == KV and mesh.shape["sp"] == MB * KV
     placed = (
         P(None, ("fsdp", "sp"), None),
         P(None, ("fsdp", "sp"), None),
@@ -375,7 +592,7 @@
         P("fsdp", None),
     )
     return jax.shard_map(
-        body,
+        group_body if fits else body,
         mesh=mesh,
         in_specs=placed,
         out_specs=(

time: 2480 us -> 931 us (0.38)
  waiting for transfers between devices: 2030 us -> 502 us
  matrix products: 281 us -> 111 us
  other arithmetic: 29.4 us -> 85.7 us
  starting transfers between devices: 39.6 us -> 91 us
    reduce_scatter x1 -> x0, waiting for transfers between devices: 1440 us -> none  [body(): lax.psum_scatter(weight_terms(kept), ('fsdp', 'sp'), scatter_dimension=0,...]
    all_gather x7 -> x8, waiting for transfers between devices: 438 us -> 152 us  [the longest x4 99.8 us: gather_weight(): return lax.all_gather(part, 'fsdp', axis=0, tiled=True)]
    ppermute x0 -> x27, waiting for transfers between devices: none -> 181 us  [the longest x18 126 us: halve(): got = lax.ppermute(send.astype(jnp.bfloat16), axis_name, perm)]
    unnamed x10, waiting for transfers between devices: 42.9 us -> 142 us
    all_to_all x8 -> x11, waiting for transfers between devices: 106 us -> 26.2 us  [the longest x4 20.4 us: sum_rows(): lax.all_to_all(partial.astype(jnp.bfloat16).reshape(group, own_rows, D),...]
    dot_general x14 -> x7, matrix products: 99.1 us -> 31 us  [contract_cols(): lax.dot_general(left_side, right_side, (((1,), (1,)), ((), ())), preferre...]
    dot_general x7, matrix products: 75.9 us -> 21.9 us  [contract_rows(): lax.dot_general(left_side, right_side, (((0,), (0,)), ((), ())), preferre...]
    dot_general x14 -> x7, matrix products: 88.5 us -> 37.5 us  [plain_dot(): return jnp.dot(left_side, right_side, preferred_element_type=jnp.float32)]
  transfers between devices with their start and end apart: 17 -> 47, of which waited for: 14 -> 21; matrix products, arithmetic and copies ran while one was open for 8% -> 25% of each run, Pallas kernels for 0% -> 0%
where the time goes in v1:
time: 931 us; the launch traced here: 920 us
  waiting for transfers between devices  502 us (54%)
  matrix products  111 us (12%)
  starting transfers between devices  91 us (10%)
  other arithmetic  85.7 us (9%)
  local copies, waits for them, and re-layouts  74.5 us (8%)
  blocking collectives  35.7 us (4%)
  between operations  20.6 us (2%)
    unnamed x10, waiting for transfers between devices  142 us
    ppermute x18, waiting for transfers between devices, halve(): got = lax.ppermute(send.astype(jnp.bfloat16), axis_name, perm)  126 us
    all_gather x4, waiting for transfers between devices, gather_weight(): return lax.all_gather(part, 'fsdp', axis=0, tiled=True)  99.8 us
    ppermute x5, waiting for transfers between devices, swap(): lax.ppermute(array, 'sp', [(s, (s + group) % n_sp) for s in range(n_sp)])  55.1 us
    all_gather x4, waiting for transfers between devices, gather_rows(): lax.all_gather(array, 'sp', axis=0, tiled=True, axis_index_groups=groups)  52.4 us
    dot_general x7, matrix products, plain_dot(): return jnp.dot(left_side, right_side, preferred_element_type=jnp.float32)  37.5 us
    dot_general x7, matrix products, contract_cols(): lax.dot_general(left_side, right_side, (((1,), (1,)), ((), ())), preferre...  31 us
    all_to_all x6, starting transfers between devices, reduce_weight(): lax.all_to_all(rows.astype(jnp.bfloat16), 'sp', split_axis=0, concat_axis...  27.7 us
  transfers between devices with their start and end apart: 47, of which 21 were waited for; matrix products, arithmetic and copies ran while one was open for 25% of the time, Pallas kernels for 0%

profile of v1, /device:TPU:0, one launch (start us, length us, event | category | flops | bytes accessed | tf_op | source)
XLA Modules:
  0.0 920.0 jit_solution(9054507240444045993)
XLA Ops:
  13.3 5.1 all-gather
  18.4 6.1 collective-permute-done
  40.9 15.9 %all_gather.38 = bf16[2048,64]{1,0:T(8,128)(2,1)} all-gather(bf16[512,64]{1,0:T(8,128)(2,1)S(1)} %constant_dynamic-slice_fusion.9), channel_id=1, replica_groups=mesh['fsdp'=4,'sp'=8] {'fsdp'}, dimensions={0}, use_global_device_ids=true | all-gather | bytes 327680 | tf_op jit(solution)/shard_map/all_gather | solution.py:421
  56.9 9.5 %all_gather.39 = bf16[2048,64]{1,0:T(8,128)(2,1)S(1)} all-gather(bf16[512,64]{1,0:T(8,128)(2,1)S(1)} %constant_dynamic-slice_fusion.8), channel_id=1, replica_groups=mesh['fsdp'=4,'sp'=8] {'fsdp'}, dimensions={0}, use_global_device_ids=true | all-gather | bytes 327680 | tf_op jit(solution)/shard_map/all_gather | solution.py:421
  70.4 5.2 collective-permute-start.2
  78.1 17.7 %all-gather.13.cloned.1.call-done = bf16[2048,512]{1,0:T(8,128)(2,1)} async-done(((bf16[512,512]{1,0:T(8,128)(2,1)}), bf16[2048,512]{1,0:T(8,128)(2,1)}) %all-gather.13.cloned.1.call-update) | async-done | bytes 2097168 | tf_op jit(solution)/shard_map/all_gather | solution.py:421
  101.3 6.2 fusion.95
  121.3 5.2 all-gather.1
  126.5 20.4 %all-to-all-done = bf16[4,128,2048]{2,1,0:T(8,128)(2,1)} async-done(((bf16[4,128,2048]{2,1,0:T(8,128)(2,1)}), bf16[4,128,2048]{2,1,0:T(8,128)(2,1)}, u32[]{:S(2)}, u32[]{:S(2)}) %all-to-all-start) | async-done | bytes 2097184 | tf_op jit(solution)/shard_map/all_to_all | solution.py:412
  156.4 11.1 %collective-permute-done.4 = bf16[64,2048]{1,0:T(8,128)(2,1)S(1)} collective-permute-done((bf16[64,2048]{1,0:T(8,128)(2,1)S(1)}, bf16[64,2048]{1,0:T(8,128)(2,1)S(1)}, u32[]{:S(2)}, u32[]{:S(2)}) %collective-permute-start.4) | collective-permute-done | bytes 262176 | tf_op jit(solution)/shard_map/ppermute | solution.py:400
  179.7 14.4 %all-gather.15.cloned.1.call-done = bf16[512,2048]{1,0:T(8,128)(2,1)} async-done(((bf16[128,2048]{1,0:T(8,128)(2,1)}), bf16[512,2048]{1,0:T(8,128)(2,1)}) %all-gather.15.cloned.1.call-update) | async-done | bytes 2097168 | tf_op jit(solution)/shard_map/all_gather | solution.py:409
  194.0 8.3 fusion.98
  202.3 36.8 %all-gather.19.cloned.1.call-done = bf16[2048,1408]{1,0:T(8,128)(2,1)} async-done(((bf16[512,1408]{1,0:T(8,128)(2,1)}), bf16[2048,1408]{1,0:T(8,128)(2,1)}) %all-gather.19.cloned.1.call-update) | async-done | bytes 5767184 | tf_op jit(solution)/shard_map/all_gather | solution.py:421
  239.2 8.2 fusion.99
  247.4 38.0 %all-gather.23.cloned.1.call-done = bf16[512,2048]{1,0:T(8,128)(2,1)} async-done(((bf16[128,2048]{1,0:T(8,128)(2,1)}), bf16[512,2048]{1,0:T(8,128)(2,1)}) %all-gather.23.cloned.1.call-update) | async-done | bytes 2097168 | tf_op jit(solution)/shard_map/all_gather | solution.py:409
  285.4 45.3 %all-gather.21.cloned.1.call-done = bf16[2048,1408]{1,0:T(8,128)(2,1)} async-done(((bf16[512,1408]{1,0:T(8,128)(2,1)}), bf16[2048,1408]{1,0:T(8,128)(2,1)}) %all-gather.21.cloned.1.call-update) | async-done | bytes 5767184 | tf_op jit(solution)/shard_map/all_gather | solution.py:421
  330.7 10.4 %multiply_convert_fusion = (bf16[512,1408]{1,0:T(8,128)(2,1)S(1)}, bf16[512,1408]{1,0:T(8,128)(2,1)S(1)}, bf16[512,1408]{1,0:T(8,128)(2,1)}) fusion(f32[512,1408]{1,0:T(8,128)} %fusion.98, f32[512,1408]{1,0:T(8,128)} %fusion.99, bf16[512,2048]{1,0:T(8,128)(2,1)} %all-gather.23.cloned.1.call-done, bf16[2048,1408]{1,0:T(8,128)(2,1)} %all-gather.21.cloned.1.call-done), kind=kOutput, calls=%fused_computation.39 | convolution fusion | flops 2963603456 | bytes 17956864 | tf_op jit(solution)/shard_map/dot_general | solution.py:19
  373.7 5.6 fusion.106
  384.7 7.5 convolution_convert_fusion.1
  420.3 12.4 %collective-permute-done.19 = bf16[2,4,64,1408]{3,2,1,0:T(8,128)(2,1)} collective-permute-done((bf16[2,4,64,1408]{3,2,1,0:T(8,128)(2,1)}, bf16[2,4,64,1408]{3,2,1,0:T(8,128)(2,1)}, u32[]{:S(2)}, u32[]{:S(2)}) %collective-permute-start.19) | collective-permute-done | bytes 1441824 | tf_op jit(solution)/shard_map/ppermute | solution.py:430
  437.9 25.6 %collective-permute-done.22 = bf16[2,4,64,1408]{3,2,1,0:T(8,128)(2,1)} collective-permute-done((bf16[2,4,64,1408]{3,2,1,0:T(8,128)(2,1)}, bf16[2,4,64,1408]{3,2,1,0:T(8,128)(2,1)}, u32[]{:S(2)}, u32[]{:S(2)}) %collective-permute-start.22) | collective-permute-done | bytes 1441824 | tf_op jit(solution)/shard_map/ppermute | solution.py:430
  469.6 24.2 %collective-permute-done.25 = bf16[2,4,64,1408]{3,2,1,0:T(8,128)(2,1)} collective-permute-done((bf16[2,4,64,1408]{3,2,1,0:T(8,128)(2,1)}, bf16[2,4,64,1408]{3,2,1,0:T(8,128)(2,1)}, u32[]{:S(2)}, u32[]{:S(2)}) %collective-permute-start.25) | collective-permute-done | bytes 1441824 | tf_op jit(solution)/shard_map/ppermute | solution.py:430
  508.7 11.2 %collective-permute-done.23 = bf16[4,64,1408]{2,1,0:T(8,128)(2,1)} collective-permute-done((bf16[4,64,1408]{2,1,0:T(8,128)(2,1)}, bf16[4,64,1408]{2,1,0:T(8,128)(2,1)}, u32[]{:S(2)}, u32[]{:S(2)}) %collective-permute-start.23) | collective-permute-done | bytes 720928 | tf_op jit(solution)/shard_map/ppermute | solution.py:430
  522.6 12.3 %collective-permute-done.26 = bf16[4,64,1408]{2,1,0:T(8,128)(2,1)} collective-permute-done((bf16[4,64,1408]{2,1,0:T(8,128)(2,1)}, bf16[4,64,1408]{2,1,0:T(8,128)(2,1)}, u32[]{:S(2)}, u32[]{:S(2)}) %collective-permute-start.26) | collective-permute-done | bytes 720928 | tf_op jit(solution)/shard_map/ppermute | solution.py:430
  537.0 5.9 all-to-all-start.9
  572.6 5.8 fusion.96
  590.3 6.5 all-to-all-start.10
  622.3 5.6 add_convert_fusion
  650.6 27.1 %collective-permute-done.7 = bf16[2,4,64,512]{3,2,1,0:T(8,128)(2,1)} collective-permute-done((bf16[2,4,64,512]{3,2,1,0:T(8,128)(2,1)S(1)}, bf16[2,4,64,512]{3,2,1,0:T(8,128)(2,1)}, u32[]{:S(2)}, u32[]{:S(2)}) %collective-permute-start.7) | collective-permute-done | bytes 524320 | tf_op jit(solution)/shard_map/ppermute | solution.py:430
  682.8 7.3 collective-permute-done.8
  709.5 38.0 %collective-permute-done.17 = bf16[256,2048]{1,0:T(8,128)(2,1)} collective-permute-done((bf16[256,2048]{1,0:T(8,128)(2,1)}, bf16[256,2048]{1,0:T(8,128)(2,1)}, u32[]{:S(2)}, u32[]{:S(2)}) %collective-permute-start.17) | collective-permute-done | bytes 1048608 | tf_op jit(solution)/shard_map/ppermute | solution.py:400
  762.8 142.1 %reduce-scatter.4.cloned.1.call-done = f32[64,2]{1,0:T(8,128)} async-done(((f32[2048,2]{1,0:T(8,128)}), f32[64,2]{1,0:T(8,128)}) %reduce-scatter.4.cloned.1.call-update) | async-done | bytes 528
  (396 shorter events, 298.5 us)
Async XLA Ops:
  7.2 68.4 %all-gather.11.cloned.1.call-start = ((), (), s32[]{:S(2)}) async-start(), calls=%async_computation.12 | async-start | bytes 2621440 | tf_op jit(solution)/shard_map/all_gather | solution.py:409
  25.8 70.1 %all-gather.13.cloned.1.call-start = ((), (), s32[]{:S(2)}) async-start(), calls=%async_computation.13 | async-start | bytes 2621440 | tf_op jit(solution)/shard_map/all_gather | solution.py:421
  26.8 152.9 %all-gather.17.cloned.1.call-start = ((), (), s32[]{:S(2)}) async-start(), calls=%async_computation.15 | async-start | bytes 7208960 | tf_op jit(solution)/shard_map/all_gather | solution.py:421
  26.8 42.1 %collective-permute-start.1 = (bf16[512,2048]{1,0:T(8,128)(2,1)}, bf16[512,2048]{1,0:T(8,128)(2,1)}, u32[]{:S(2)}, u32[]{:S(2)}) collective-permute-start(bf16[512,2048]{1,0:T(8,128)(2,1)} %param.21), channel_id=1, source_target_pairs={{0,16},{9,25},{18,2},{27,11},{4,20},{13,29},{22,6},{31,15}} | collective-permute-start | bytes 6291464 | tf_op jit(solution)/shard_map/ppermute | solution.py:446
  70.4 41.9 %collective-permute-start.2 = (bf16[512,2048]{1,0:T(8,128)(2,1)}, bf16[512,2048]{1,0:T(8,128)(2,1)}, u32[]{:S(2)}, u32[]{:S(2)}) collective-permute-start(bf16[512,2048]{1,0:T(8,128)(2,1)} %broadcast_select_fusion), channel_id=1, source_target_pairs={{0,8},{16,24},{9,1},{25,17},{18,26},{2,10},{27,19},{11,3},{4,12},{... | collective-permute-start | bytes 6291464 | tf_op jit(solution)/shard_map/ppermute | solution.py:448
  121.3 72.8 %all-gather.15.cloned.1.call-start = ((), (), s32[]{:S(2)}) async-start(), calls=%async_computation.14 | async-start | bytes 2621440 | tf_op jit(solution)/shard_map/all_gather | solution.py:409
  150.4 88.8 %all-gather.19.cloned.1.call-start = ((), (), s32[]{:S(2)}) async-start(), calls=%async_computation.16 | async-start | bytes 7208960 | tf_op jit(solution)/shard_map/all_gather | solution.py:421
  153.1 132.3 %all-gather.23.cloned.1.call-start = ((), (), s32[]{:S(2)}) async-start(), calls=%async_computation.18 | async-start | bytes 2621440 | tf_op jit(solution)/shard_map/all_gather | solution.py:409
  168.5 162.2 %all-gather.21.cloned.1.call-start = ((), (), s32[]{:S(2)}) async-start(), calls=%async_computation.17 | async-start | bytes 7208960 | tf_op jit(solution)/shard_map/all_gather | solution.py:421
  346.6 45.7 %collective-permute-start.18 = (bf16[2,2,4,64,1408]{4,3,2,1,0:T(8,128)(2,1)}, bf16[2,2,4,64,1408]{4,3,2,1,0:T(8,128)(2,1)}, u32[]{:S(2)}, u32[]{:S(2)}) collective-permute-start(bf16[2,2,4,64,1408]{4,3,2,1,0:T(8,128)(2,1)} %fusion.9), channel_id=1, source_target_pairs={{0,8},{8,0},{16,24},{24,16},{1,9},{9,1},{17,25},{25,17},{2,10},{10... | collective-permute-start | bytes 8650760 | tf_op jit(solution)/shard_map/ppermute | solution.py:430
  360.8 37.4 %collective-permute-start.21 = (bf16[2,2,4,64,1408]{4,3,2,1,0:T(8,128)(2,1)}, bf16[2,2,4,64,1408]{4,3,2,1,0:T(8,128)(2,1)}, u32[]{:S(2)}, u32[]{:S(2)}) collective-permute-start(bf16[2,2,4,64,1408]{4,3,2,1,0:T(8,128)(2,1)} %fusion.10), channel_id=1, source_target_pairs={{0,8},{8,0},{16,24},{24,16},{1,9},{9,1},{17,25},{25,17},{2,10},{10... | collective-permute-start | bytes 8650760 | tf_op jit(solution)/shard_map/ppermute | solution.py:430
  369.3 42.6 %all-to-all-start.2 = ((bf16[4,128,2048]{2,1,0:T(8,128)(2,1)}), bf16[4,128,2048]{2,1,0:T(8,128)(2,1)}, u32[]{:S(2)}, u32[]{:S(2)}) async-start(bf16[4,128,2048]{2,1,0:T(8,128)(2,1)} %bitcast.313), calls=%async_computation.2 | async-start | bytes 4194304 | tf_op jit(solution)/shard_map/all_to_all | solution.py:412
  397.9 34.7 %collective-permute-start.19 = (bf16[2,4,64,1408]{3,2,1,0:T(8,128)(2,1)}, bf16[2,4,64,1408]{3,2,1,0:T(8,128)(2,1)}, u32[]{:S(2)}, u32[]{:S(2)}) collective-permute-start(bf16[2,4,64,1408]{3,2,1,0:T(8,128)(2,1)} %fusion.18), channel_id=1, source_target_pairs={{0,16},{8,24},{16,0},{24,8},{1,17},{9,25},{17,1},{25,9},{2,18},{10... | collective-permute-start | bytes 4325384 | tf_op jit(solution)/shard_map/ppermute | solution.py:430
  402.8 60.8 %collective-permute-start.22 = (bf16[2,4,64,1408]{3,2,1,0:T(8,128)(2,1)}, bf16[2,4,64,1408]{3,2,1,0:T(8,128)(2,1)}, u32[]{:S(2)}, u32[]{:S(2)}) collective-permute-start(bf16[2,4,64,1408]{3,2,1,0:T(8,128)(2,1)} %fusion.19), channel_id=1, source_target_pairs={{0,16},{8,24},{16,0},{24,8},{1,17},{9,25},{17,1},{25,9},{2,18},{10... | collective-permute-start | bytes 4325384 | tf_op jit(solution)/shard_map/ppermute | solution.py:430
  410.9 82.9 %collective-permute-start.25 = (bf16[2,4,64,1408]{3,2,1,0:T(8,128)(2,1)}, bf16[2,4,64,1408]{3,2,1,0:T(8,128)(2,1)}, u32[]{:S(2)}, u32[]{:S(2)}) collective-permute-start(bf16[2,4,64,1408]{3,2,1,0:T(8,128)(2,1)} %fusion.20), channel_id=1, source_target_pairs={{0,16},{8,24},{16,0},{24,8},{1,17},{9,25},{17,1},{25,9},{2,18},{10... | collective-permute-start | bytes 4325384 | tf_op jit(solution)/shard_map/ppermute | solution.py:430
  411.8 89.0 %all-to-all-start.1 = ((bf16[4,128,2048]{2,1,0:T(8,128)(2,1)}), bf16[4,128,2048]{2,1,0:T(8,128)(2,1)}, u32[]{:S(2)}, u32[]{:S(2)}) async-start(bf16[4,128,2048]{2,1,0:T(8,128)(2,1)} %bitcast.312), calls=%async_computation.1 | async-start | bytes 4194304 | tf_op jit(solution)/shard_map/all_to_all | solution.py:412
  416.4 127.9 %all-gather.25.cloned.1.call-start = ((), (), s32[]{:S(2)}) async-start(), calls=%async_computation.19 | async-start | bytes 2621440 | tf_op jit(solution)/shard_map/all_gather | solution.py:409
  435.4 64.4 %collective-permute-start.20 = (bf16[4,64,1408]{2,1,0:T(8,128)(2,1)S(1)}, bf16[4,64,1408]{2,1,0:T(8,128)(2,1)S(1)}, u32[]{:S(2)}, u32[]{:S(2)}) collective-permute-start(bf16[4,64,1408]{2,1,0:T(8,128)(2,1)S(1)} %fusion.49), channel_id=1, source_target_pairs={{0,4},{1,5},{2,6},{3,7},{4,0},{5,1},{6,2},{7,3},{8,12},{9,13},{10,... | collective-permute-start | bytes 2162696 | tf_op jit(solution)/shard_map/ppermute | solution.py:430
  467.1 52.8 %collective-permute-start.23 = (bf16[4,64,1408]{2,1,0:T(8,128)(2,1)}, bf16[4,64,1408]{2,1,0:T(8,128)(2,1)}, u32[]{:S(2)}, u32[]{:S(2)}) collective-permute-start(bf16[4,64,1408]{2,1,0:T(8,128)(2,1)} %fusion.50), channel_id=1, source_target_pairs={{0,4},{1,5},{2,6},{3,7},{4,0},{5,1},{6,2},{7,3},{8,12},{9,13},{10,... | collective-permute-start | bytes 2162696 | tf_op jit(solution)/shard_map/ppermute | solution.py:430
  497.4 37.5 %collective-permute-start.26 = (bf16[4,64,1408]{2,1,0:T(8,128)(2,1)}, bf16[4,64,1408]{2,1,0:T(8,128)(2,1)}, u32[]{:S(2)}, u32[]{:S(2)}) collective-permute-start(bf16[4,64,1408]{2,1,0:T(8,128)(2,1)} %fusion.51), channel_id=1, source_target_pairs={{0,4},{1,5},{2,6},{3,7},{4,0},{5,1},{6,2},{7,3},{8,12},{9,13},{10,... | collective-permute-start | bytes 2162696 | tf_op jit(solution)/shard_map/ppermute | solution.py:430
  500.8 36.2 %all-to-all-start.8 = ((bf16[4,64,1408]{2,1,0:T(8,128)(2,1)}), bf16[4,64,1408]{2,1,0:T(8,128)(2,1)S(1)}, u32[]{:S(2)}, u32[]{:S(2)}) async-start(bf16[4,64,1408]{2,1,0:T(8,128)(2,1)} %fusion.23), calls=%async_computation.8 | async-start | bytes 1441792 | tf_op jit(solution)/shard_map/all_to_all | solution.py:436
  537.0 53.3 %all-to-all-start.9 = ((bf16[4,64,1408]{2,1,0:T(8,128)(2,1)}), bf16[4,64,1408]{2,1,0:T(8,128)(2,1)}, u32[]{:S(2)}, u32[]{:S(2)}) async-start(bf16[4,64,1408]{2,1,0:T(8,128)(2,1)} %fusion.22), calls=%async_computation.9 | async-start | bytes 1441792 | tf_op jit(solution)/shard_map/all_to_all | solution.py:436
  564.5 75.7 %collective-permute-start.6 = (bf16[2,2,4,64,512]{4,3,2,1,0:T(8,128)(2,1)}, bf16[2,2,4,64,512]{4,3,2,1,0:T(8,128)(2,1)}, u32[]{:S(2)}, u32[]{:S(2)}) collective-permute-start(bf16[2,2,4,64,512]{4,3,2,1,0:T(8,128)(2,1)} %fusion.43), channel_id=1, source_target_pairs={{0,8},{8,0},{16,24},{24,16},{1,9},{9,1},{17,25},{25,17},{2,10},{10... | collective-permute-start | bytes 3145736 | tf_op jit(solution)/shard_map/ppermute | solution.py:430
  578.4 56.5 %collective-permute-start.15 = (bf16[512,2048]{1,0:T(8,128)(2,1)}, bf16[512,2048]{1,0:T(8,128)(2,1)}, u32[]{:S(2)}, u32[]{:S(2)}) collective-permute-start(bf16[512,2048]{1,0:T(8,128)(2,1)} %get-tuple-element.67), channel_id=1, source_target_pairs={{8,0},{24,16},{1,9},{17,25},{26,18},{10,2},{19,27},{3,11},{12,4},{... | collective-permute-start | bytes 6291464 | tf_op jit(solution)/shard_map/ppermute | solution.py:542
  627.9 64.0 %all-to-all-start.3 = ((bf16[4,128,2048]{2,1,0:T(8,128)(2,1)}), bf16[4,128,2048]{2,1,0:T(8,128)(2,1)}, u32[]{:S(2)}, u32[]{:S(2)}) async-start(bf16[4,128,2048]{2,1,0:T(8,128)(2,1)} %bitcast.297), calls=%async_computation.3 | async-start | bytes 4194304 | tf_op jit(solution)/shard_map/all_to_all | solution.py:412
  638.9 59.3 %collective-permute-start.16 = (bf16[512,2048]{1,0:T(8,128)(2,1)}, bf16[512,2048]{1,0:T(8,128)(2,1)}, u32[]{:S(2)}, u32[]{:S(2)}) collective-permute-start(bf16[512,2048]{1,0:T(8,128)(2,1)} %fusion.8), channel_id=1, source_target_pairs={{16,0},{25,9},{2,18},{11,27},{20,4},{29,13},{6,22},{15,31}} | collective-permute-start | bytes 6291464 | tf_op jit(solution)/shard_map/ppermute | solution.py:547
  692.0 58.0 %all-to-all-start.4 = ((bf16[4,64,512]{2,1,0:T(8,128)(2,1)}), bf16[4,64,512]{2,1,0:T(8,128)(2,1)}, u32[]{:S(2)}, u32[]{:S(2)}) async-start(bf16[4,64,512]{2,1,0:T(8,128)(2,1)} %fusion.54), calls=%async_computation.4 | async-start | bytes 524288 | tf_op jit(solution)/shard_map/all_to_all | solution.py:436
  704.4 43.1 %collective-permute-start.17 = (bf16[256,2048]{1,0:T(8,128)(2,1)}, bf16[256,2048]{1,0:T(8,128)(2,1)}, u32[]{:S(2)}, u32[]{:S(2)}) collective-permute-start(bf16[256,2048]{1,0:T(8,128)(2,1)} %fusion.44), channel_id=1, source_target_pairs={{0,4},{1,5},{2,6},{3,7},{4,0},{5,1},{6,2},{7,3},{8,12},{9,13},{10,... | collective-permute-start | bytes 3145736 | tf_op jit(solution)/shard_map/ppermute | solution.py:400
  750.0 161.6 %all-to-all-start.7 = ((bf16[4,64,2048]{2,1,0:T(8,128)(2,1)}), bf16[4,64,2048]{2,1,0:T(8,128)(2,1)}, u32[]{:S(2)}, u32[]{:S(2)}) async-start(bf16[4,64,2048]{2,1,0:T(8,128)(2,1)} %bitcast.79), calls=%async_computation.7 | async-start | bytes 2097152 | tf_op jit(solution)/shard_map/all_to_all | solution.py:553
  754.2 150.6 %reduce-scatter.4.cloned.1.call-start = ((), (), s32[]{:S(2)}) async-start(), calls=%async_computation.20 | async-start | bytes 1081344
  755.4 151.6 %collective-permute-start.3 = (f32[64,2048]{1,0:T(8,128)}, f32[64,2048]{1,0:T(8,128)}, u32[]{:S(2)}, u32[]{:S(2)}) collective-permute-start(f32[64,2048]{1,0:T(8,128)} %get-tuple-element.36), channel_id=1, source_target_pairs={{0,4},{1,5},{2,6},{3,7},{4,0},{5,1},{6,2},{7,3},{8,12},{9,13},{10,... | collective-permute-start | bytes 1572872 | tf_op jit(solution)/shard_map/ppermute | solution.py:400
  757.2 152.0 %collective-permute-start.5 = (f32[64,2048]{1,0:T(8,128)}, f32[64,2048]{1,0:T(8,128)}, u32[]{:S(2)}, u32[]{:S(2)}) collective-permute-start(f32[64,2048]{1,0:T(8,128)} %get-tuple-element.32), channel_id=1, source_target_pairs={{0,4},{1,5},{2,6},{3,7},{4,0},{5,1},{6,2},{7,3},{8,12},{9,13},{10,... | collective-permute-start | bytes 1572872 | tf_op jit(solution)/shard_map/ppermute | solution.py:400
  (94 other events, 2068.3 us)
Sparse Core Ops, SparseCore 0:
  25.9 45.3 all-gather.10
  73.5 22.3 all-gather.12
  98.0 43.3 all-gather.16
  150.5 43.4 all-gather.14
  196.0 43.0 all-gather.18
  241.2 44.2 all-gather.22
  287.5 43.0 all-gather.20
  420.4 58.2 all-gather.24
  760.9 143.9 reduce-scatter.3

commit v2 on v1

--- a/solution.py
+++ b/solution.py
@@ -1,6 +1,11 @@
+import functools
+
 import jax
 import jax.numpy as jnp
+import numpy as np
 from jax import lax
+from jax.experimental import pallas as pl
+from jax.experimental.pallas import tpu as pltpu
 from jax.sharding import PartitionSpec as P
 
 D = 2048
@@ -9,6 +14,8 @@
 HDIM = 64
 FF = 5632
 MB = 2
+MESH = pl.DeviceIdType.MESH
+VMEM_BYTES = 56 * 2**20
 
 
 EPSILON = 1e-05
@@ -358,14 +365,364 @@
     )
 
 
-def silu_parts(gate_proj):
-    gate_sig = jax.nn.sigmoid(gate_proj)
-    return gate_sig, gate_proj * gate_sig
-
-
-def turned(vectors):
-    half_size = vectors.shape[-1] // 2
-    return jnp.concatenate([-vectors[..., half_size:], vectors[..., :half_size]], axis=-1)
+def mesh_place(n_sp):
+    shard = lax.axis_index("fsdp")
+    rank = lax.axis_index("sp")
+    group = n_sp // MB
+    chip, core = shard // 2, shard % 2
+    micro, member = rank // group, rank % group
+    high, low = member // 2, member % 2
+    base = micro * group
+    peers = (
+        (shard, base + high * 2 + (1 - low)),
+        (shard, base + (1 - high) * 2 + low),
+        (shard, base + (1 - high) * 2 + (1 - low)),
+    )
+    members = (high * 2 + (1 - low), (1 - high) * 2 + low, (1 - high) * 2 + (1 - low))
+    partner = (shard, (1 - micro) * group + member)
+    core_mate = (chip * 2 + (1 - core), rank)
+    chip_mate = ((1 - chip) * 2 + core, rank)
+    far_mate = ((1 - chip) * 2 + (1 - core), rank)
+    return shard, rank, micro, member, peers, members, partner, core_mate, chip_mate, far_mate
+
+
+def greet(devices):
+    barrier = pltpu.get_barrier_semaphore()
+    for device in devices:
+        pl.semaphore_signal(barrier, inc=1, device_id=device, device_id_type=MESH)
+    pl.semaphore_wait(barrier, len(devices))
+
+
+def lane_ids(shape):
+    return lax.broadcasted_iota(jnp.int32, shape, len(shape) - 1)
+
+
+def turn(vectors):
+    width = vectors.shape[-1]
+    ahead = pltpu.roll(vectors, width - HDIM // 2, 1)
+    behind = pltpu.roll(vectors, HDIM // 2, 1)
+    first = lane_ids(vectors.shape) % HDIM < HDIM // 2
+    return jnp.where(first, -ahead, behind)
+
+
+def turn_back(vectors):
+    return -turn(vectors)
+
+
+def softmax_rows(query_pair, key_twice, bias, lower):
+    lanes = lane_ids(query_pair.shape)
+    query = jnp.where((lanes < HDIM) == lower, query_pair, jnp.zeros_like(query_pair))
+    scores = contract_cols(query, key_twice) * HDIM**-0.5 + bias
+    top = jnp.max(scores, axis=-1, keepdims=True)
+    weights_exp = jnp.exp(scores - top)
+    return weights_exp * (1.0 / jnp.sum(weights_exp, axis=-1, keepdims=True))
+
+
+def row_places(shape, dim, group, tok_rows):
+    ids = lax.broadcasted_iota(jnp.int32, shape, dim)
+    own_rows = MB * tok_rows
+    return ((ids % own_rows) // tok_rows) * (group * tok_rows) + (ids // own_rows) * tok_rows + ids % tok_rows
+
+
+def pair_bias(window, group, tok_rows, first_len, both_len):
+    place = row_places((window, 1), 0, group, tok_rows)
+    key_place = row_places((1, window), 1, group, tok_rows)
+    anchor = jnp.where(place < first_len, 0, jnp.where(place < both_len, first_len, both_len))
+    return jnp.where((key_place <= place) & (key_place >= anchor), 0.0, -1e30)
+
+
+def front_kernel(
+    n_sp,
+    tokens,
+    cotangent,
+    seq_len,
+    slot_order,
+    gains,
+    wq_in,
+    wkv_in,
+    wo_in,
+    wg_in,
+    wu_in,
+    wd_in,
+    cosine,
+    sine,
+    xs,
+    upstream,
+    normed,
+    query_rot,
+    keys,
+    values,
+    attended,
+    middle,
+    normed_two,
+    wq,
+    wkv,
+    wo,
+    wg,
+    wu,
+    wd,
+    gains_all,
+    gs,
+    sent,
+    got,
+    bias,
+    local_sem,
+    send_sem,
+    recv_sem,
+):
+    place = mesh_place(n_sp)
+    shard, rank, micro, member, peers, members, partner, core_mate, chip_mate, far_mate = place
+    group = n_sp // MB
+    tok_rows = tokens.shape[1]
+    own_rows = MB * tok_rows
+    window = group * own_rows
+    greet((*peers, partner, core_mate, chip_mate, far_mate))
+
+    def send(index, source, target, device):
+        copy = pltpu.make_async_remote_copy(
+            src_ref=source,
+            dst_ref=target,
+            send_sem=send_sem.at[index],
+            recv_sem=recv_sem.at[index],
+            device_id=device,
+            device_id_type=MESH,
+        )
+        copy.start()
+        return copy
+
+    def move(index, source, target):
+        copy = pltpu.make_async_copy(source, target, local_sem.at[index])
+        copy.start()
+        return copy
+
+    swap_x = send(0, tokens.at[1 - micro], xs.at[micro], partner)
+    swap_g = send(1, cotangent.at[1 - micro], gs.at[micro], partner)
+    own_x = move(0, tokens.at[micro], xs.at[micro])
+    own_g = move(1, cotangent.at[micro], gs.at[micro])
+    gain_sends = [
+        send(2 + i, gains, gains_all.at[shard], device) for i, device in enumerate((core_mate, chip_mate, far_mate))
+    ]
+    own_gain = move(2, gains, gains_all.at[shard])
+
+    def columns(ref, width):
+        return ref.at[:, pl.ds(pl.multiple_of(member * width, 128), width)]
+
+    chip_shard = (1 - shard // 2) * 2 + shard % 2
+    width_q, width_f = wq.shape[2], wg.shape[2]
+    parts = (
+        (columns(wq_in, width_q), wq),
+        (wkv_in, wkv),
+        (columns(wg_in, width_f), wg),
+        (columns(wu_in, width_f), wu),
+        (columns(wd_in, width_f), wd),
+    )
+
+    def weight_out(i):
+        source, target = parts[i]
+        over_chip = send(5 + 3 * i, source, target.at[shard], chip_mate)
+        over_core = send(6 + 3 * i, source, target.at[shard], core_mate)
+        here = move(3 + i, source, target.at[shard])
+        return over_chip, over_core, here
+
+    def weight_on(i):
+        target = parts[i][1]
+        return send(7 + 3 * i, target.at[chip_shard], target.at[chip_shard], core_mate)
+
+    started = {i: weight_out(i) for i in (0, 1)}
+    wo_x, wo_core, wo_on = 20, 21, 22
+
+    def wo_copy(index, source, device):
+        return pltpu.make_async_remote_copy(
+            src_ref=source,
+            dst_ref=wo,
+            send_sem=send_sem.at[index],
+            recv_sem=recv_sem.at[index],
+            device_id=device,
+            device_id_type=MESH,
+        )
+
+    same_chip = shard // 2 == member // 2
+    same_core = shard % 2 == member % 2
+    wo_here = pltpu.make_async_copy(wo_in, wo, local_sem.at[8])
+
+    @pl.when(same_chip & same_core)
+    def _():
+        wo_copy(wo_x, wo_in, chip_mate).start()
+        wo_copy(wo_core, wo_in, core_mate).start()
+        wo_here.start()
+
+    first_len = seq_len[slot_order[2 * (shard * MB + micro)]]
+    both_len = first_len + seq_len[slot_order[2 * (shard * MB + micro) + 1]]
+
+    own_gain.wait()
+    for copy in gain_sends:
+        copy.wait()
+    gain_one = jnp.concatenate([gains_all[f, 0:1, :] for f in range(KV)], axis=1)
+    gain_two = jnp.concatenate([gains_all[f, 1:2, :] for f in range(KV)], axis=1)
+    own_x.wait()
+    swap_x.wait()
+    inputs = xs[...].reshape(own_rows, D).astype(jnp.float32)
+    normed[member] = (inputs * rms_scale(inputs) * gain_one).astype(jnp.bfloat16)
+    gather = [send(23 + i, normed.at[member], normed.at[member], device) for i, device in enumerate(peers)]
+
+    own_g.wait()
+    swap_g.wait()
+    ids = lax.broadcasted_iota(jnp.int32, (own_rows, 1), 0)
+    own_place = (ids // tok_rows) * (group * tok_rows) + member * tok_rows + ids % tok_rows
+    valid = jnp.where(own_place < both_len, 1.0, 0.0)
+    upstream[member] = (gs[...].reshape(own_rows, D).astype(jnp.float32) * valid).astype(jnp.bfloat16)
+
+    on = []
+    for i in (0, 1):
+        started[i][0].wait()
+        on.append(weight_on(i))
+    for i in (2, 3, 4):
+        started[i] = weight_out(i)
+    for i in (0, 1):
+        started[i][1].wait()
+        started[i][2].wait()
+    for copy in on:
+        copy.wait()
+
+    def project(rows):
+        block = normed[rows]
+        place_rows = pl.ds(pl.multiple_of(rows * own_rows, own_rows), own_rows)
+        query = jnp.zeros((own_rows, width_q), jnp.float32)
+        pair = jnp.zeros((own_rows, 2 * HDIM), jnp.float32)
+        for f in range(KV):
+            part = block[:, f * (D // KV) : (f + 1) * (D // KV)]
+            query += plain_dot(part, wq[f])
+            pair += plain_dot(part, wkv[f])
+        cos, sin = cosine[place_rows, :], sine[place_rows, :]
+        for j in range(width_q // 128):
+            lanes = slice(j * 128, (j + 1) * 128)
+            head = query[:, lanes].astype(jnp.bfloat16).astype(jnp.float32)
+            query_rot[place_rows, lanes] = (head * cos + turn(head) * sin).astype(jnp.bfloat16)
+        pair = pair.astype(jnp.bfloat16).astype(jnp.float32)
+        turned_key = pair * cos + turn(pair) * sin
+        lower = lane_ids(pair.shape) < HDIM
+        keys[place_rows, :] = jnp.where(lower, turned_key, pltpu.roll(turned_key, HDIM, 1)).astype(jnp.bfloat16)
+        values[place_rows, :] = jnp.where(lower, pltpu.roll(pair, HDIM, 1), pair).astype(jnp.bfloat16)
+
+    project(member)
+    for i, copy in enumerate(gather):
+        copy.wait()
+        project(members[i])
+    gather_g = [send(26 + i, upstream.at[member], upstream.at[member], device) for i, device in enumerate(peers)]
+
+    bias[...] = pair_bias(window, group, tok_rows, first_len, both_len)
+    key_twice = keys[...]
+    value_twice = values[...]
+    lower = lane_ids(value_twice.shape) < HDIM
+    value_low = jnp.where(lower, value_twice, jnp.zeros_like(value_twice))
+    value_high = jnp.where(lower, jnp.zeros_like(value_twice), value_twice)
+
+    @pl.loop(0, width_q // 128)
+    def _(j):
+        lanes = pl.ds(pl.multiple_of(j * 128, 128), 128)
+        pair = query_rot[:, lanes]
+        low_probs = softmax_rows(pair, key_twice, bias[...], True).astype(jnp.bfloat16)
+        total = plain_dot(low_probs, value_low)
+        high_probs = softmax_rows(pair, key_twice, bias[...], False).astype(jnp.bfloat16)
+        total += plain_dot(high_probs, value_high)
+        attended[:, lanes] = total.astype(jnp.bfloat16)
+
+    @pl.when(same_chip & same_core)
+    def _():
+        wo_copy(wo_x, wo_in, chip_mate).wait_send()
+        wo_copy(wo_core, wo_in, core_mate).wait_send()
+        wo_here.wait()
+
+    @pl.when(jnp.logical_not(same_chip) & same_core)
+    def _():
+        wo_copy(wo_x, wo_in, chip_mate).wait_recv()
+        forward = wo_copy(wo_on, wo, core_mate)
+        forward.start()
+        forward.wait_send()
+
+    @pl.when(same_chip & jnp.logical_not(same_core))
+    def _():
+        wo_copy(wo_core, wo_in, core_mate).wait_recv()
+
+    @pl.when(jnp.logical_not(same_chip) & jnp.logical_not(same_core))
+    def _():
+        wo_copy(wo_on, wo, core_mate).wait_recv()
+
+    def project_out(rows):
+        place_rows = pl.ds(pl.multiple_of(rows * own_rows, own_rows), own_rows)
+        return plain_dot(attended[place_rows, :], wo[...])
+
+    sums = {}
+    for i in (2, 0, 1):
+        sent[i] = project_out(members[i]).astype(jnp.bfloat16)
+        sums[i] = send(29 + i, sent.at[i], got.at[i], peers[i])
+    total = inputs + project_out(member)
+    for i in (0, 1, 2):
+        sums[i].wait()
+        total += got[i].astype(jnp.float32)
+    middle[...] = total
+    normed_two[member] = (total * rms_scale(total) * gain_two).astype(jnp.bfloat16)
+    gather_two = [
+        send(32 + i, normed_two.at[member], normed_two.at[member], device) for i, device in enumerate(peers)
+    ]
+    on = []
+    for i in (2, 3, 4):
+        started[i][0].wait()
+        on.append(weight_on(i))
+        started[i][1].wait()
+        started[i][2].wait()
+    for copy in (*on, *gather_g, *gather_two):
+        copy.wait()
+
+
+def front(n_sp, tok_rows, heads, *operands):
+    group = n_sp // MB
+    own_rows = MB * tok_rows
+    window = group * own_rows
+    width_q = heads * HDIM
+    width_f = FF // group
+    low = jnp.bfloat16
+    vmem = pl.BlockSpec(memory_space=pltpu.VMEM)
+    anywhere = pl.BlockSpec(memory_space=pl.ANY)
+    smem = pl.BlockSpec(memory_space=pltpu.SMEM)
+    shape = jax.ShapeDtypeStruct
+    return pl.pallas_call(
+        functools.partial(front_kernel, n_sp),
+        out_shape=(
+            shape((MB, tok_rows, D), low),
+            shape((group, own_rows, D), low),
+            shape((group, own_rows, D), low),
+            shape((window, width_q), low),
+            shape((window, 2 * HDIM), low),
+            shape((window, 2 * HDIM), low),
+            shape((window, width_q), low),
+            shape((own_rows, D), jnp.float32),
+            shape((group, own_rows, D), low),
+            shape((KV, D // KV, width_q), low),
+            shape((KV, D // KV, 2 * HDIM), low),
+            shape((width_q, D), low),
+            shape((KV, D // KV, width_f), low),
+            shape((KV, D // KV, width_f), low),
+            shape((KV, D // KV, width_f), low),
+            shape((KV, 8, D // KV), jnp.float32),
+        ),
+        in_specs=[anywhere, anywhere, smem, smem, vmem, anywhere, anywhere, anywhere, anywhere, anywhere, anywhere, vmem, vmem],
+        out_specs=tuple([vmem] * 12 + [anywhere] * 3 + [vmem]),
+        scratch_shapes=[
+            pltpu.VMEM((MB, tok_rows, D), low),
+            pltpu.VMEM((group - 1, own_rows, D), low),
+            pltpu.VMEM((group - 1, own_rows, D), low),
+            pltpu.VMEM((window, window), jnp.float32),
+            pltpu.SemaphoreType.DMA((9,)),
+            pltpu.SemaphoreType.DMA((35,)),
+            pltpu.SemaphoreType.DMA((35,)),
+        ],
+        compiler_params=pltpu.CompilerParams(
+            collective_id=0, has_side_effects=True, vmem_limit_bytes=VMEM_BYTES
+        ),
+        cost_estimate=pl.CostEstimate(flops=8 * 10**9, bytes_accessed=40 * 10**6, transcendentals=2 * 10**6),
+        name="front",
+    )(*operands)
 
 
 def group_body(
@@ -394,6 +751,8 @@
     window = n_sp * tok_rows
     own_rows = MB * tok_rows
     groups = [[m * group + t for t in range(group)] for m in range(MB)]
+    both = ("fsdp", "sp")
+    members = [(m * group + t, t) for m in range(MB) for t in range(group)]
     flat = lambda f, s: f * n_sp + s
 
     def swap(array):
@@ -438,68 +797,65 @@
         )
         return rows.astype(jnp.float32).transpose(1, 0, 2).reshape(tok_rows, group * width)
 
-    w_query = gather_weight(query_weight)
-    w_key = gather_weight(key_weight)
-    w_value = gather_weight(value_weight)
-    both = ("fsdp", "sp")
-    members = [(m * group + t, t) for m in range(MB) for t in range(group)]
-    over_x = lax.ppermute(output_weight, both, [(flat(t, s), flat(t ^ 2, s)) for s, t in members])
-    held = jnp.where(shard == member, output_weight, over_x)
-    over_core = lax.ppermute(
-        held, both, [(flat(t ^ k, s), flat(t ^ k ^ 1, s)) for s, t in members for k in (0, 2)]
-    )
-    w_output = jnp.where((shard & 1) == (member & 1), held, over_core)
-    w_gate = gather_weight(gate_weight)
-    w_up = gather_weight(up_weight)
-    w_down = gather_weight(down_weight)
-    gain_one = lax.all_gather(norm1_gain, "fsdp", axis=0, tiled=True).astype(jnp.float32)
-    gain_two = lax.all_gather(norm2_gain, "fsdp", axis=0, tiled=True).astype(jnp.float32)
-
-    ids = jnp.arange(window, dtype=jnp.int32)
-    owner, half, inner = ids // own_rows, (ids // tok_rows) % MB, ids % tok_rows
-    place = (half * group + owner) * tok_rows + inner
-    window_index = shard * MB + micro
-    first_len = seq_len[slot_order[2 * window_index]]
-    second_len = seq_len[slot_order[2 * window_index + 1]]
-    segment = jnp.where(place < first_len, 0, jnp.where(place < first_len + second_len, 1, 2))
-    anchor = jnp.where(segment == 0, 0, jnp.where(segment == 1, first_len, first_len + second_len))
-    position = place - anchor
-    allowed = (segment[:, None] == segment[None, :]) & (place[None, :] <= place[:, None])
-    valid = (segment < 2).astype(jnp.float32)
-    own_valid = lax.dynamic_slice_in_dim(valid, member * own_rows, own_rows, 0)
-    cosine, sine = rope_tables(position, HDIM)
-
-    own_tokens = in_order(pick(tokens, micro), swap(pick(tokens, 1 - micro)))
-    own_cot = in_order(pick(cotangent, micro), swap(pick(cotangent, 1 - micro)))
-    inputs = own_tokens.astype(jnp.float32)
-    upstream = own_cot.astype(jnp.float32) * own_valid[:, None]
-    upstream_low = gather_rows(upstream.astype(jnp.bfloat16))
-
+    first_len = seq_len[slot_order[2 * (shard * MB + micro)]]
+    second_len = seq_len[slot_order[2 * (shard * MB + micro) + 1]]
+    place = row_places((window,), 0, group, tok_rows)
+    anchor = jnp.where(place < first_len, 0, jnp.where(place < first_len + second_len, first_len, first_len + second_len))
+    inverse = ROPE_BASE ** (-2.0 * jnp.arange(HDIM // 2, dtype=jnp.float32) / HDIM)
+    angles = (place - anchor).astype(jnp.float32)[:, None] * jnp.tile(inverse, 4)[None, :]
+    cosine, sine = jnp.cos(angles), jnp.sin(angles)
+
+    def columns(weight):
+        width = weight.shape[1] // group
+        return lax.dynamic_slice_in_dim(weight, member * width, width, 1)
+
+    gains = jnp.concatenate(
+        [norm1_gain[None], norm2_gain[None], jnp.zeros((6, norm1_gain.shape[0]), jnp.bfloat16)]
+    ).astype(jnp.float32)
+    kv_weight = jnp.concatenate([columns(key_weight), columns(value_weight)], axis=1)
+    heads = HEADS // group
+    (
+        own_tokens,
+        upstream_low,
+        normed,
+        query_rot,
+        keys,
+        values,
+        attended,
+        middle,
+        normed_two,
+        w_query,
+        w_kv,
+        w_output,
+        w_gate,
+        w_up,
+        w_down,
+        gains,
+    ) = front(
+        n_sp, tok_rows, heads,
+        tokens, cotangent, seq_len, slot_order, gains,
+        query_weight, kv_weight, output_weight, gate_weight, up_weight, down_weight, cosine, sine,
+    )
+    gain_one, gain_two = gains[:, 0].reshape(D), gains[:, 1].reshape(D)
+    upstream_low, normed, normed_two = (rows.reshape(window, D) for rows in (upstream_low, normed, normed_two))
+    w_query, w_kv, w_gate, w_up, w_down = (w.reshape(D, -1) for w in (w_query, w_kv, w_gate, w_up, w_down))
+    w_key, w_value = w_kv[:, :HDIM], w_kv[:, HDIM:]
+    inputs = own_tokens.reshape(own_rows, D).astype(jnp.float32)
+    upstream = lax.dynamic_slice_in_dim(upstream_low, member * own_rows, own_rows, 0).astype(jnp.float32)
     scale_one = rms_scale(inputs)
-    normed = gather_rows((inputs * scale_one * gain_one).astype(jnp.bfloat16))
-    heads = HEADS // group
-    query = plain_dot(normed, w_query).astype(jnp.bfloat16).astype(jnp.float32).reshape(window, heads, HDIM)
-    key = plain_dot(normed, w_key).astype(jnp.bfloat16).astype(jnp.float32).reshape(window, 1, HDIM)
-    value = plain_dot(normed, w_value).astype(jnp.bfloat16)
-    query_rot = apply_rope(query, cosine, sine).astype(jnp.bfloat16)
-    key_rot = apply_rope(key, cosine, sine).astype(jnp.bfloat16)[:, 0]
-
+    scale_two = rms_scale(middle)
+    cosine, sine = cosine[:, None, :HDIM], sine[:, None, :HDIM]
+    query_rot = query_rot.reshape(window, heads, HDIM)
+    key_rot, value = keys[:, :HDIM], values[:, :HDIM]
     scale = HDIM**-0.5
     scores = jnp.einsum("qhd,kd->hqk", query_rot, key_rot, preferred_element_type=jnp.float32) * scale
-    scores = jnp.where(allowed[None], scores, -1e30)
-    top = jnp.max(scores, axis=-1, keepdims=True)
-    weights_exp = jnp.exp(scores - top)
-    probs = weights_exp / jnp.sum(weights_exp, axis=-1, keepdims=True)
+    scores = scores + pair_bias(window, group, tok_rows, first_len, first_len + second_len)[None]
+    probs = jax.nn.softmax(scores, axis=-1)
     probs_low = probs.astype(jnp.bfloat16)
-    attended = jnp.einsum("hqk,kd->qhd", probs_low, value, preferred_element_type=jnp.float32)
-    attended = attended.astype(jnp.bfloat16).reshape(window, heads * HDIM)
-
-    middle = inputs + sum_rows(plain_dot(attended, w_output))
-    scale_two = rms_scale(middle)
-    normed_two = gather_rows((middle * scale_two * gain_two).astype(jnp.bfloat16))
     gate = plain_dot(normed_two, w_gate)
     up = plain_dot(normed_two, w_up)
-    sig, silu = silu_parts(gate)
+    sig = jax.nn.sigmoid(gate)
+    silu = gate * sig
     hidden = (silu * up).astype(jnp.bfloat16)
     block = middle + sum_rows(contract_cols(hidden, w_down))
     d_hidden = plain_dot(upstream_low, w_down)

time: 931 us -> 798 us (0.86)
  waiting for transfers between devices: 502 us -> 287 us
  Pallas kernels: 0 us -> 169 us
  blocking collectives: 35.7 us -> 0 us
  starting transfers between devices: 91 us -> 62 us
  matrix products: 111 us -> 94.1 us
    pallas_call x0 -> x1, Pallas kernels: none -> 169 us  [front(): pl.pallas_call(functools.partial(front_kernel, n_sp), out_shape=(shape((M...]
    all_gather x4 -> x0, waiting for transfers between devices: 99.8 us -> none  [gather_weight(): return lax.all_gather(part, 'fsdp', axis=0, tiled=True)]
    all_gather x4 -> x1, waiting for transfers between devices: 52.4 us -> 0.02 us  [gather_rows(): lax.all_gather(array, 'sp', axis=0, tiled=True, axis_index_groups=groups)]
    ppermute x5 -> x3, waiting for transfers between devices: 55.1 us -> 12.5 us  [swap(): lax.ppermute(array, 'sp', [(s, (s + group) % n_sp) for s in range(n_sp)])]
    all_gather x4 -> x0, blocking collectives: 35.7 us -> none  [the longest x2 25.4 us: gather_weight(): return lax.all_gather(part, 'fsdp', axis=0, tiled=True)]
    dot_general x7 -> x3, matrix products: 37.5 us -> 16 us  [plain_dot(): return jnp.dot(left_side, right_side, preferred_element_type=jnp.float32)]
    all_to_all x4 -> x3, waiting for transfers between devices: 20.4 us -> 1.51 us  [sum_rows(): lax.all_to_all(partial.astype(jnp.bfloat16).reshape(group, own_rows, D),...]
    ppermute x18, waiting for transfers between devices: 126 us -> 138 us  [halve(): got = lax.ppermute(send.astype(jnp.bfloat16), axis_name, perm)]
  transfers between devices with their start and end apart: 47 -> 35, of which waited for: 21 -> 13; matrix products, arithmetic and copies ran while one was open for 25% -> 25% of each run, Pallas kernels for 0% -> 0%
where the time goes in v2:
time: 798 us; the launch traced here: 787 us
  waiting for transfers between devices  287 us (36%)
  Pallas kernels  169 us (21%)
  matrix products  94.1 us (12%)
  other arithmetic  79.7 us (10%)
  local copies, waits for them, and re-layouts  74.5 us (9%)
  starting transfers between devices  62 us (8%)
  between operations  20.9 us (3%)
    pallas_call x1, Pallas kernels, front(): pl.pallas_call(functools.partial(front_kernel, n_sp), out_shape=(shape((M...  169 us
    ppermute x18, waiting for transfers between devices, halve(): got = lax.ppermute(send.astype(jnp.bfloat16), axis_name, perm)  138 us
    unnamed x3, waiting for transfers between devices  135 us
    dot_general x7, matrix products, contract_cols(): lax.dot_general(left_side, right_side, (((1,), (1,)), ((), ())), preferre...  32.8 us
    all_to_all x6, starting transfers between devices, reduce_weight(): lax.all_to_all(rows.astype(jnp.bfloat16), 'sp', split_axis=0, concat_axis...  27.1 us
    unnamed x145, local copies, waits for them, and re-layouts  26.5 us
    dot_general x7, matrix products, contract_rows(): lax.dot_general(left_side, right_side, (((0,), (0,)), ((), ())), preferre...  25.2 us
    add x12, other arithmetic, halve(): return keep + got.astype(jnp.float32)  24.3 us
  transfers between devices with their start and end apart: 35, of which 13 were waited for; matrix products, arithmetic and copies ran while one was open for 25% of the time, Pallas kernels for 0%

profile of v2, /device:TPU:0, one launch (start us, length us, event | category | flops | bytes accessed | tf_op | source)
XLA Modules:
  0.0 787.0 jit_solution(2814943071900119138)
XLA Ops:
  21.6 168.8 %front.1 = (bf16[2,64,2048]{2,1,0:T(8,128)(2,1)}, bf16[4,128,2048]{2,1,0:T(8,128)(2,1)}, bf16[4,128,2048]{2,1,0:T(8,128)(2,1)}, bf16[512,512]{1,0:T(8,128)(2,1)}...) custom-call(bf16[2,64,2048]{2,1,0:T(8,128)(2,1)} %tokens.1, ...), custom_call_target="tpu_custom_call" | custom-call | flops 8000000000 | bytes 40000000 | tf_op jit(solution)/shard_map/front/pallas_call | solution.py:689
  190.5 6.9 fusion.112
  201.0 5.6 multiply_convert_fusion
  210.0 4.7 add_convert_fusion.1
  214.7 4.5 all-to-all-start.1
  223.2 9.7 %fusion.22 = f32[2,2,2,4,64,1408]{5,4,3,2,1,0:T(8,128)} fusion(bf16[2,2,2,4,64,512]{5,4,3,2,1,0:T(8,128)(2,1)} %bitcast.313, bf16[512,1408]{1,0:T(8,128)(2,1)} %copy-done.56), kind=kOutput, calls=%fused_computation.55 | convolution fusion | flops 2952790016 | bytes 15073280 | tf_op jit(solution)/shard_map/dot_general | solution.py:30
  232.8 4.7 fusion.10
  241.0 4.2 copy-done.16
  250.2 5.4 fusion.18
  270.2 8.0 %fusion.106 = (f32[8,512]{1,0:T(8,128)}, f32[8,512,512]{1,2,0:T(8,128)}) fusion(f32[512,512]{0,1:T(8,128)} %and_select_fusion, bf16[512,8,64]{0,2,1:T(8,128)(2,1)} %bitcast.323, bf16[512,128]{1,0:T(8,128)(2,1)S(1)} %copy-done.44), kind=kOutput, calls=%fused_computation.210 | convolution fusion | flops 276824576 | bytes 10108928 | tf_op jit(solution)/shard_map/sub | solution.py:853
  278.1 8.0 %convolution_convert_fusion = bf16[512,2048]{1,0:T(8,128)(2,1)} fusion(bf16[512,1408]{1,0:T(8,128)(2,1)} %get-tuple-element.51, bf16[2048,1408]{1,0:T(8,128)(2,1)} %bitcast.335), kind=kOutput, calls=%fused_computation.27 | convolution fusion | flops 2953838592 | bytes 9306112 | tf_op jit(solution)/shard_map/dot_general | solution.py:36
  286.1 4.4 all-to-all-start
  290.7 4.3 bitcast_add_fusion.6
  297.7 5.5 bitcast_add_fusion.5
  322.8 8.2 %collective-permute-done.15 = bf16[2,4,64,1408]{3,2,1,0:T(8,128)(2,1)} collective-permute-done((bf16[2,4,64,1408]{3,2,1,0:T(8,128)(2,1)}, bf16[2,4,64,1408]{3,2,1,0:T(8,128)(2,1)}, u32[]{:S(2)}, u32[]{:S(2)}) %collective-permute-start.15) | collective-permute-done | bytes 1441824 | tf_op jit(solution)/shard_map/ppermute | solution.py:789
  333.9 28.0 %collective-permute-done.18 = bf16[2,4,64,1408]{3,2,1,0:T(8,128)(2,1)} collective-permute-done((bf16[2,4,64,1408]{3,2,1,0:T(8,128)(2,1)}, bf16[2,4,64,1408]{3,2,1,0:T(8,128)(2,1)}, u32[]{:S(2)}, u32[]{:S(2)}) %collective-permute-start.18) | collective-permute-done | bytes 1441824 | tf_op jit(solution)/shard_map/ppermute | solution.py:789
  365.4 26.9 %collective-permute-done.21 = bf16[2,4,64,1408]{3,2,1,0:T(8,128)(2,1)} collective-permute-done((bf16[2,4,64,1408]{3,2,1,0:T(8,128)(2,1)}, bf16[2,4,64,1408]{3,2,1,0:T(8,128)(2,1)}, u32[]{:S(2)}, u32[]{:S(2)}) %collective-permute-start.21) | collective-permute-done | bytes 1441824 | tf_op jit(solution)/shard_map/ppermute | solution.py:789
  403.4 23.9 %collective-permute-done.19 = bf16[4,64,1408]{2,1,0:T(8,128)(2,1)} collective-permute-done((bf16[4,64,1408]{2,1,0:T(8,128)(2,1)}, bf16[4,64,1408]{2,1,0:T(8,128)(2,1)}, u32[]{:S(2)}, u32[]{:S(2)}) %collective-permute-start.19) | collective-permute-done | bytes 720928 | tf_op jit(solution)/shard_map/ppermute | solution.py:789
  429.8 11.8 %collective-permute-done.22 = bf16[4,64,1408]{2,1,0:T(8,128)(2,1)} collective-permute-done((bf16[4,64,1408]{2,1,0:T(8,128)(2,1)}, bf16[4,64,1408]{2,1,0:T(8,128)(2,1)}, u32[]{:S(2)}, u32[]{:S(2)}) %collective-permute-start.22) | collective-permute-done | bytes 720928 | tf_op jit(solution)/shard_map/ppermute | solution.py:789
  444.6 4.4 all-to-all-start.8
  453.9 5.6 fusion.33
  497.7 4.6 all-to-all-start.9
  518.1 4.2 all-to-all-start.4
  522.3 5.1 fusion.9
  528.6 6.7 all-to-all-start.5
  535.4 5.8 add_convert_fusion
  541.8 4.2 all-to-all-start.2
  558.3 8.4 %collective-permute-done.3 = bf16[2,4,64,512]{3,2,1,0:T(8,128)(2,1)S(1)} collective-permute-done((bf16[2,4,64,512]{3,2,1,0:T(8,128)(2,1)S(1)}, bf16[2,4,64,512]{3,2,1,0:T(8,128)(2,1)S(1)}, u32[]{:S(2)}, u32[]{:S(2)}) %collective-permute-start.3) | collective-permute-done | bytes 524320 | tf_op jit(solution)/shard_map/ppermute | solution.py:789
  580.1 25.6 %collective-permute-done.4 = bf16[4,64,512]{2,1,0:T(8,128)(2,1)S(1)} collective-permute-done((bf16[4,64,512]{2,1,0:T(8,128)(2,1)S(1)}, bf16[4,64,512]{2,1,0:T(8,128)(2,1)S(1)}, u32[]{:S(2)}, u32[]{:S(2)}) %collective-permute-start.4) | collective-permute-done | bytes 262176 | tf_op jit(solution)/shard_map/ppermute | solution.py:789
  614.7 12.5 %collective-permute-done.13 = bf16[256,2048]{1,0:T(8,128)(2,1)} collective-permute-done((bf16[256,2048]{1,0:T(8,128)(2,1)}, bf16[256,2048]{1,0:T(8,128)(2,1)}, u32[]{:S(2)}, u32[]{:S(2)}) %collective-permute-start.13) | collective-permute-done | bytes 1048608 | tf_op jit(solution)/shard_map/ppermute | solution.py:759
  630.4 4.2 all-to-all-start.6
  639.4 135.4 %reduce-scatter.4.cloned.1.call-done = f32[64,2]{1,0:T(8,128)} async-done(((f32[2048,2]{1,0:T(8,128)}), f32[64,2]{1,0:T(8,128)}) %reduce-scatter.4.cloned.1.call-update) | async-done | bytes 528
  (319 shorter events, 196.0 us)
Async XLA Ops:
  214.7 71.4 %all-to-all-start.1 = ((bf16[4,128,2048]{2,1,0:T(8,128)(2,1)}), bf16[4,128,2048]{2,1,0:T(8,128)(2,1)}, u32[]{:S(2)}, u32[]{:S(2)}) async-start(bf16[4,128,2048]{2,1,0:T(8,128)(2,1)} %bitcast.307), calls=%async_computation.1 | async-start | bytes 4194304 | tf_op jit(solution)/shard_map/all_to_all | solution.py:771
  237.5 53.1 %collective-permute-start.14 = (bf16[2,2,4,64,1408]{4,3,2,1,0:T(8,128)(2,1)}, bf16[2,2,4,64,1408]{4,3,2,1,0:T(8,128)(2,1)}, u32[]{:S(2)}, u32[]{:S(2)}) collective-permute-start(bf16[2,2,4,64,1408]{4,3,2,1,0:T(8,128)(2,1)} %fusion.10), channel_id=1, source_target_pairs={{0,8},{8,0},{16,24},{24,16},{1,9},{9,1},{17,25},{25,17},{2,10},{10... | collective-permute-start | bytes 8650760 | tf_op jit(solution)/shard_map/ppermute | solution.py:789
  247.2 50.5 %collective-permute-start.17 = (bf16[2,2,4,64,1408]{4,3,2,1,0:T(8,128)(2,1)}, bf16[2,2,4,64,1408]{4,3,2,1,0:T(8,128)(2,1)}, u32[]{:S(2)}, u32[]{:S(2)}) collective-permute-start(bf16[2,2,4,64,1408]{4,3,2,1,0:T(8,128)(2,1)} %fusion.11), channel_id=1, source_target_pairs={{0,8},{8,0},{16,24},{24,16},{1,9},{9,1},{17,25},{25,17},{2,10},{10... | collective-permute-start | bytes 8650760 | tf_op jit(solution)/shard_map/ppermute | solution.py:789
  261.8 44.1 %collective-permute-start.20 = (bf16[2,2,4,64,1408]{4,3,2,1,0:T(8,128)(2,1)}, bf16[2,2,4,64,1408]{4,3,2,1,0:T(8,128)(2,1)}, u32[]{:S(2)}, u32[]{:S(2)}) collective-permute-start(bf16[2,2,4,64,1408]{4,3,2,1,0:T(8,128)(2,1)} %fusion.12), channel_id=1, source_target_pairs={{0,8},{8,0},{16,24},{24,16},{1,9},{9,1},{17,25},{25,17},{2,10},{10... | collective-permute-start | bytes 8650760 | tf_op jit(solution)/shard_map/ppermute | solution.py:789
  286.1 30.5 %all-to-all-start = ((bf16[4,128,2048]{2,1,0:T(8,128)(2,1)}), bf16[4,128,2048]{2,1,0:T(8,128)(2,1)}, u32[]{:S(2)}, u32[]{:S(2)}) async-start(bf16[4,128,2048]{2,1,0:T(8,128)(2,1)} %bitcast.312), calls=%async_computation | async-start | bytes 4194304 | tf_op jit(solution)/shard_map/all_to_all | solution.py:771
  290.6 159.6 %all-gather.2.cloned.1.call-start = ((), (), s32[]{:S(2)}) async-start(), calls=%async_computation.11 | async-start | bytes 2621440 | tf_op jit(solution)/shard_map/all_gather | solution.py:768
  296.2 34.7 %collective-permute-start.15 = (bf16[2,4,64,1408]{3,2,1,0:T(8,128)(2,1)}, bf16[2,4,64,1408]{3,2,1,0:T(8,128)(2,1)}, u32[]{:S(2)}, u32[]{:S(2)}) collective-permute-start(bf16[2,4,64,1408]{3,2,1,0:T(8,128)(2,1)} %fusion.15), channel_id=1, source_target_pairs={{0,16},{8,24},{16,0},{24,8},{1,17},{9,25},{17,1},{25,9},{2,18},{10... | collective-permute-start | bytes 4325384 | tf_op jit(solution)/shard_map/ppermute | solution.py:789
  304.6 57.2 %collective-permute-start.18 = (bf16[2,4,64,1408]{3,2,1,0:T(8,128)(2,1)}, bf16[2,4,64,1408]{3,2,1,0:T(8,128)(2,1)}, u32[]{:S(2)}, u32[]{:S(2)}) collective-permute-start(bf16[2,4,64,1408]{3,2,1,0:T(8,128)(2,1)} %fusion.16), channel_id=1, source_target_pairs={{0,16},{8,24},{16,0},{24,8},{1,17},{9,25},{17,1},{25,9},{2,18},{10... | collective-permute-start | bytes 4325384 | tf_op jit(solution)/shard_map/ppermute | solution.py:789
  311.3 81.1 %collective-permute-start.21 = (bf16[2,4,64,1408]{3,2,1,0:T(8,128)(2,1)}, bf16[2,4,64,1408]{3,2,1,0:T(8,128)(2,1)}, u32[]{:S(2)}, u32[]{:S(2)}) collective-permute-start(bf16[2,4,64,1408]{3,2,1,0:T(8,128)(2,1)} %fusion.17), channel_id=1, source_target_pairs={{0,16},{8,24},{16,0},{24,8},{1,17},{9,25},{17,1},{25,9},{2,18},{10... | collective-permute-start | bytes 4325384 | tf_op jit(solution)/shard_map/ppermute | solution.py:789
  322.7 78.2 %collective-permute-start = (f32[64,2048]{1,0:T(8,128)}, f32[64,2048]{1,0:T(8,128)}, u32[]{:S(2)}, u32[]{:S(2)}) collective-permute-start(f32[64,2048]{1,0:T(8,128)} %get-tuple-element.58), channel_id=1, source_target_pairs={{0,4},{1,5},{2,6},{3,7},{4,0},{5,1},{6,2},{7,3},{8,12},{9,13},{10,... | collective-permute-start | bytes 1572872 | tf_op jit(solution)/shard_map/ppermute | solution.py:759
  333.8 62.5 %collective-permute-start.16 = (bf16[4,64,1408]{2,1,0:T(8,128)(2,1)S(1)}, bf16[4,64,1408]{2,1,0:T(8,128)(2,1)S(1)}, u32[]{:S(2)}, u32[]{:S(2)}) collective-permute-start(bf16[4,64,1408]{2,1,0:T(8,128)(2,1)S(1)} %fusion.42), channel_id=1, source_target_pairs={{0,4},{1,5},{2,6},{3,7},{4,0},{5,1},{6,2},{7,3},{8,12},{9,13},{10,... | collective-permute-start | bytes 2162696 | tf_op jit(solution)/shard_map/ppermute | solution.py:789
  365.4 61.8 %collective-permute-start.19 = (bf16[4,64,1408]{2,1,0:T(8,128)(2,1)}, bf16[4,64,1408]{2,1,0:T(8,128)(2,1)}, u32[]{:S(2)}, u32[]{:S(2)}) collective-permute-start(bf16[4,64,1408]{2,1,0:T(8,128)(2,1)} %fusion.43), channel_id=1, source_target_pairs={{0,4},{1,5},{2,6},{3,7},{4,0},{5,1},{6,2},{7,3},{8,12},{9,13},{10,... | collective-permute-start | bytes 2162696 | tf_op jit(solution)/shard_map/ppermute | solution.py:789
  395.8 45.7 %collective-permute-start.22 = (bf16[4,64,1408]{2,1,0:T(8,128)(2,1)}, bf16[4,64,1408]{2,1,0:T(8,128)(2,1)}, u32[]{:S(2)}, u32[]{:S(2)}) collective-permute-start(bf16[4,64,1408]{2,1,0:T(8,128)(2,1)} %fusion.44), channel_id=1, source_target_pairs={{0,4},{1,5},{2,6},{3,7},{4,0},{5,1},{6,2},{7,3},{8,12},{9,13},{10,... | collective-permute-start | bytes 2162696 | tf_op jit(solution)/shard_map/ppermute | solution.py:789
  397.2 46.5 %all-to-all-start.7 = ((bf16[4,64,1408]{2,1,0:T(8,128)(2,1)}), bf16[4,64,1408]{2,1,0:T(8,128)(2,1)S(1)}, u32[]{:S(2)}, u32[]{:S(2)}) async-start(bf16[4,64,1408]{2,1,0:T(8,128)(2,1)} %fusion.26), calls=%async_computation.7 | async-start | bytes 1441792 | tf_op jit(solution)/shard_map/all_to_all | solution.py:795
  444.6 53.1 %all-to-all-start.8 = ((bf16[4,64,1408]{2,1,0:T(8,128)(2,1)}), bf16[4,64,1408]{2,1,0:T(8,128)(2,1)}, u32[]{:S(2)}, u32[]{:S(2)}) async-start(bf16[4,64,1408]{2,1,0:T(8,128)(2,1)} %fusion.25), calls=%async_computation.8 | async-start | bytes 1441792 | tf_op jit(solution)/shard_map/all_to_all | solution.py:795
  482.7 67.0 %collective-permute-start.2 = (bf16[2,2,4,64,512]{4,3,2,1,0:T(8,128)(2,1)}, bf16[2,2,4,64,512]{4,3,2,1,0:T(8,128)(2,1)}, u32[]{:S(2)}, u32[]{:S(2)}) collective-permute-start(bf16[2,2,4,64,512]{4,3,2,1,0:T(8,128)(2,1)} %fusion.36), channel_id=1, source_target_pairs={{0,8},{8,0},{16,24},{24,16},{1,9},{9,1},{17,25},{25,17},{2,10},{10... | collective-permute-start | bytes 3145736 | tf_op jit(solution)/shard_map/ppermute | solution.py:789
  482.7 11.1 %collective-permute-start.5 = (bf16[2,2,4,64,64]{4,3,2,1,0:T(8,128)(2,1)S(1)}, bf16[2,2,4,64,64]{4,3,2,1,0:T(8,128)(2,1)S(1)}, u32[]{:S(2)}, u32[]{:S(2)}) collective-permute-start(bf16[2,2,4,64,64]{4,3,2,1,0:T(8,128)(2,1)S(1)} %fusion.51), channel_id=1, source_target_pairs={{0,8},{8,0},{16,24},{24,16},{1,9},{9,1},{17,25},{25,17},{2,10},{10... | collective-permute-start | bytes 393224 | tf_op jit(solution)/shard_map/ppermute | solution.py:789
  484.2 12.0 %collective-permute-start.8 = (bf16[2,2,4,64,64]{4,3,2,1,0:T(8,128)(2,1)S(1)}, bf16[2,2,4,64,64]{4,3,2,1,0:T(8,128)(2,1)S(1)}, u32[]{:S(2)}, u32[]{:S(2)}) collective-permute-start(bf16[2,2,4,64,64]{4,3,2,1,0:T(8,128)(2,1)S(1)} %fusion.52), channel_id=1, source_target_pairs={{0,8},{8,0},{16,24},{24,16},{1,9},{9,1},{17,25},{25,17},{2,10},{10... | collective-permute-start | bytes 393224 | tf_op jit(solution)/shard_map/ppermute | solution.py:789
  489.0 33.2 %collective-permute-start.11 = (bf16[512,2048]{1,0:T(8,128)(2,1)}, bf16[512,2048]{1,0:T(8,128)(2,1)S(1)}, u32[]{:S(2)}, u32[]{:S(2)}) collective-permute-start(bf16[512,2048]{1,0:T(8,128)(2,1)} %get-tuple-element.83), channel_id=1, source_target_pairs={{8,0},{24,16},{1,9},{17,25},{26,18},{10,2},{19,27},{3,11},{12,4},{... | collective-permute-start | bytes 6291464 | tf_op jit(solution)/shard_map/ppermute | solution.py:898
  497.7 20.4 %all-to-all-start.9 = ((bf16[4,64,1408]{2,1,0:T(8,128)(2,1)}), bf16[4,64,1408]{2,1,0:T(8,128)(2,1)}, u32[]{:S(2)}, u32[]{:S(2)}) async-start(bf16[4,64,1408]{2,1,0:T(8,128)(2,1)} %fusion.24), calls=%async_computation.9 | async-start | bytes 1441792 | tf_op jit(solution)/shard_map/all_to_all | solution.py:795
  503.4 9.3 %collective-permute-start.7 = (bf16[4,64,64]{2,1,0:T(8,128)(2,1)S(1)}, bf16[4,64,64]{2,1,0:T(8,128)(2,1)S(1)}, u32[]{:S(2)}, u32[]{:S(2)}) collective-permute-start(bf16[4,64,64]{2,1,0:T(8,128)(2,1)S(1)} %fusion.77), channel_id=1, source_target_pairs={{0,4},{1,5},{2,6},{3,7},{4,0},{5,1},{6,2},{7,3},{8,12},{9,13},{10,... | collective-permute-start | bytes 98312 | tf_op jit(solution)/shard_map/ppermute | solution.py:789
  518.1 10.5 %all-to-all-start.4 = ((bf16[4,2,2048]{2,1,0:T(2,128)(2,1)}), bf16[4,2,2048]{2,1,0:T(2,128)(2,1)}, u32[]{:S(2)}, u32[]{:S(2)}) async-start(bf16[4,2,2048]{2,1,0:T(2,128)(2,1)} %reshape.585), calls=%async_computation.4 | async-start | bytes 65536 | tf_op jit(solution)/shard_map/all_to_all | solution.py:795
  527.3 44.1 %collective-permute-start.12 = (bf16[512,2048]{1,0:T(8,128)(2,1)}, bf16[512,2048]{1,0:T(8,128)(2,1)}, u32[]{:S(2)}, u32[]{:S(2)}) collective-permute-start(bf16[512,2048]{1,0:T(8,128)(2,1)} %fusion.9), channel_id=1, source_target_pairs={{16,0},{25,9},{2,18},{11,27},{20,4},{29,13},{6,22},{15,31}} | collective-permute-start | bytes 6291464 | tf_op jit(solution)/shard_map/ppermute | solution.py:903
  528.6 12.5 %all-to-all-start.5 = ((bf16[4,2,2048]{2,1,0:T(2,128)(2,1)}), bf16[4,2,2048]{2,1,0:T(2,128)(2,1)S(1)}, u32[]{:S(2)}, u32[]{:S(2)}) async-start(bf16[4,2,2048]{2,1,0:T(2,128)(2,1)} %reshape.587), calls=%async_computation.5 | async-start | bytes 65536 | tf_op jit(solution)/shard_map/all_to_all | solution.py:795
  541.8 65.7 %all-to-all-start.2 = ((bf16[4,128,2048]{2,1,0:T(8,128)(2,1)}), bf16[4,128,2048]{2,1,0:T(8,128)(2,1)S(1)}, u32[]{:S(2)}, u32[]{:S(2)}) async-start(bf16[4,128,2048]{2,1,0:T(8,128)(2,1)} %bitcast.296), calls=%async_computation.2 | async-start | bytes 4194304 | tf_op jit(solution)/shard_map/all_to_all | solution.py:771
  553.4 13.3 %collective-permute-start.3 = (bf16[2,4,64,512]{3,2,1,0:T(8,128)(2,1)S(1)}, bf16[2,4,64,512]{3,2,1,0:T(8,128)(2,1)S(1)}, u32[]{:S(2)}, u32[]{:S(2)}) collective-permute-start(bf16[2,4,64,512]{3,2,1,0:T(8,128)(2,1)S(1)} %fusion.45), channel_id=1, source_target_pairs={{0,16},{8,24},{16,0},{24,8},{1,17},{9,25},{17,1},{25,9},{2,18},{10... | collective-permute-start | bytes 1572872 | tf_op jit(solution)/shard_map/ppermute | solution.py:789
  568.2 37.5 %collective-permute-start.4 = (bf16[4,64,512]{2,1,0:T(8,128)(2,1)S(1)}, bf16[4,64,512]{2,1,0:T(8,128)(2,1)S(1)}, u32[]{:S(2)}, u32[]{:S(2)}) collective-permute-start(bf16[4,64,512]{2,1,0:T(8,128)(2,1)S(1)} %fusion.50), channel_id=1, source_target_pairs={{0,4},{1,5},{2,6},{3,7},{4,0},{5,1},{6,2},{7,3},{8,12},{9,13},{10,... | collective-permute-start | bytes 786440 | tf_op jit(solution)/shard_map/ppermute | solution.py:789
  578.3 48.8 %collective-permute-start.13 = (bf16[256,2048]{1,0:T(8,128)(2,1)}, bf16[256,2048]{1,0:T(8,128)(2,1)}, u32[]{:S(2)}, u32[]{:S(2)}) collective-permute-start(bf16[256,2048]{1,0:T(8,128)(2,1)} %fusion.37), channel_id=1, source_target_pairs={{0,4},{1,5},{2,6},{3,7},{4,0},{5,1},{6,2},{7,3},{8,12},{9,13},{10,... | collective-permute-start | bytes 3145736 | tf_op jit(solution)/shard_map/ppermute | solution.py:759
  608.8 21.6 %all-to-all-start.3 = ((bf16[4,64,512]{2,1,0:T(8,128)(2,1)}), bf16[4,64,512]{2,1,0:T(8,128)(2,1)S(1)}, u32[]{:S(2)}, u32[]{:S(2)}) async-start(bf16[4,64,512]{2,1,0:T(8,128)(2,1)} %fusion.49), calls=%async_computation.3 | async-start | bytes 524288 | tf_op jit(solution)/shard_map/all_to_all | solution.py:795
  630.4 147.6 %all-to-all-start.6 = ((bf16[4,64,2048]{2,1,0:T(8,128)(2,1)}), bf16[4,64,2048]{2,1,0:T(8,128)(2,1)}, u32[]{:S(2)}, u32[]{:S(2)}) async-start(bf16[4,64,2048]{2,1,0:T(8,128)(2,1)} %bitcast.72), calls=%async_computation.6 | async-start | bytes 2097152 | tf_op jit(solution)/shard_map/all_to_all | solution.py:909
  634.6 140.2 %reduce-scatter.4.cloned.1.call-start = ((), (), s32[]{:S(2)}) async-start(), calls=%async_computation.12 | async-start | bytes 1081344
  636.4 140.4 %collective-permute-start.1 = (f32[64,2048]{1,0:T(8,128)S(1)}, f32[64,2048]{1,0:T(8,128)S(1)}, u32[]{:S(2)}, u32[]{:S(2)}) collective-permute-start(f32[64,2048]{1,0:T(8,128)S(1)} %get-tuple-element.53), channel_id=1, source_target_pairs={{0,4},{1,5},{2,6},{3,7},{4,0},{5,1},{6,2},{7,3},{8,12},{9,13},{10,... | collective-permute-start | bytes 1572872 | tf_op jit(solution)/shard_map/ppermute | solution.py:759
  (72 other events, 597.4 us)
Sparse Core Ops, SparseCore 0:
  322.9 44.7 all-gather.1
  638.6 136.1 reduce-scatter.3

commit v3 on v2

--- a/solution.py
+++ b/solution.py
@@ -15,7 +15,7 @@
 FF = 5632
 MB = 2
 MESH = pl.DeviceIdType.MESH
-VMEM_BYTES = 56 * 2**20
+VMEM_BYTES = 60 * 2**20
 
 
 EPSILON = 1e-05
@@ -409,13 +409,10 @@
     return -turn(vectors)
 
 
-def softmax_rows(query_pair, key_twice, bias, lower):
-    lanes = lane_ids(query_pair.shape)
-    query = jnp.where((lanes < HDIM) == lower, query_pair, jnp.zeros_like(query_pair))
-    scores = contract_cols(query, key_twice) * HDIM**-0.5 + bias
-    top = jnp.max(scores, axis=-1, keepdims=True)
-    weights_exp = jnp.exp(scores - top)
-    return weights_exp * (1.0 / jnp.sum(weights_exp, axis=-1, keepdims=True))
+def softmax_columns(key_side, query_pair, bias):
+    scores = contract_cols(key_side, query_pair) + bias
+    weights_exp = jnp.exp(scores - jnp.max(scores, axis=0, keepdims=True))
+    return weights_exp * (1.0 / jnp.sum(weights_exp, axis=0, keepdims=True))
 
 
 def row_places(shape, dim, group, tok_rows):
@@ -425,8 +422,8 @@
 
 
 def pair_bias(window, group, tok_rows, first_len, both_len):
-    place = row_places((window, 1), 0, group, tok_rows)
-    key_place = row_places((1, window), 1, group, tok_rows)
+    place = row_places((1, window), 1, group, tok_rows)
+    key_place = row_places((window, 1), 0, group, tok_rows)
     anchor = jnp.where(place < first_len, 0, jnp.where(place < both_len, first_len, both_len))
     return jnp.where((key_place <= place) & (key_place >= anchor), 0.0, -1e30)
 
@@ -597,7 +594,8 @@
         for j in range(width_q // 128):
             lanes = slice(j * 128, (j + 1) * 128)
             head = query[:, lanes].astype(jnp.bfloat16).astype(jnp.float32)
-            query_rot[place_rows, lanes] = (head * cos + turn(head) * sin).astype(jnp.bfloat16)
+            head = (head * cos + turn(head) * sin).astype(jnp.bfloat16)
+            query_rot[place_rows, lanes] = head * HDIM**-0.5
         pair = pair.astype(jnp.bfloat16).astype(jnp.float32)
         turned_key = pair * cos + turn(pair) * sin
         lower = lane_ids(pair.shape) < HDIM
@@ -614,18 +612,17 @@
     key_twice = keys[...]
     value_twice = values[...]
     lower = lane_ids(value_twice.shape) < HDIM
-    value_low = jnp.where(lower, value_twice, jnp.zeros_like(value_twice))
-    value_high = jnp.where(lower, jnp.zeros_like(value_twice), value_twice)
+    zero = jnp.zeros_like(key_twice)
+    key_low, key_high = jnp.where(lower, key_twice, zero), jnp.where(lower, zero, key_twice)
+    value_low, value_high = jnp.where(lower, value_twice, zero).T, jnp.where(lower, zero, value_twice).T
 
     @pl.loop(0, width_q // 128)
     def _(j):
         lanes = pl.ds(pl.multiple_of(j * 128, 128), 128)
         pair = query_rot[:, lanes]
-        low_probs = softmax_rows(pair, key_twice, bias[...], True).astype(jnp.bfloat16)
-        total = plain_dot(low_probs, value_low)
-        high_probs = softmax_rows(pair, key_twice, bias[...], False).astype(jnp.bfloat16)
-        total += plain_dot(high_probs, value_high)
-        attended[:, lanes] = total.astype(jnp.bfloat16)
+        total = plain_dot(value_low, softmax_columns(key_low, pair, bias[...]).astype(jnp.bfloat16))
+        total += plain_dot(value_high, softmax_columns(key_high, pair, bias[...]).astype(jnp.bfloat16))
+        attended[:, lanes] = total.T.astype(jnp.bfloat16)
 
     @pl.when(same_chip & same_core)
     def _():
@@ -725,6 +722,564 @@
     )(*operands)
 
 
+def back_kernel(
+    n_sp,
+    d_two_part,
+    block_part,
+    gate_part,
+    up_part,
+    down_part,
+    middle_in,
+    tokens_in,
+    upstream_in,
+    normed_in,
+    query_in,
+    keys_in,
+    values_in,
+    attended_in,
+    wq_in,
+    wkv_in,
+    wo_in,
+    seq_len,
+    slot_order,
+    gains,
+    cosine,
+    sine,
+    block_out,
+    input_grad,
+    ffn_grad,
+    qkv_grad,
+    out_grad,
+    gain_sum,
+    own_two,
+    own_block,
+    own_one,
+    middle,
+    xs,
+    upstream,
+    normed,
+    query_rot,
+    keys,
+    values,
+    attended,
+    wq,
+    wkv,
+    wo,
+    d_middle,
+    d_full,
+    d_attended,
+    d_query,
+    d_pair,
+    key_sum,
+    value_sum,
+    bias,
+    sent,
+    got_two,
+    got_one,
+    rows_out,
+    rows_got,
+    from_core,
+    from_chip,
+    from_half,
+    unit_stage,
+    late,
+    late_core,
+    late_chip,
+    late_half,
+    out_part,
+    out_core,
+    out_chip,
+    out_half,
+    gain_part,
+    gain_got,
+    local_sem,
+    send_sem,
+    recv_sem,
+):
+    place = mesh_place(n_sp)
+    shard, rank, micro, member, peers, members, partner, core_mate, chip_mate, far_mate = place
+    chip, core = shard // 2, shard % 2
+    group = n_sp // MB
+    own_rows = middle.shape[0]
+    tok_rows = own_rows // MB
+    window = group * own_rows
+    width_q = query_rot.shape[1]
+    greet((*peers, partner, core_mate, chip_mate))
+
+    def copy_to(index, source, target, device):
+        return pltpu.make_async_remote_copy(
+            src_ref=source,
+            dst_ref=target,
+            send_sem=send_sem.at[index],
+            recv_sem=recv_sem.at[index],
+            device_id=device,
+            device_id_type=MESH,
+        )
+
+    def send(index, source, target, device):
+        copy = copy_to(index, source, target, device)
+        copy.start()
+        return copy
+
+    def move(index, source, target):
+        copy = pltpu.make_async_copy(source, target, local_sem.at[index])
+        copy.start()
+        return copy
+
+    ffn_parts = (gate_part, up_part, down_part)
+    sums_two = {i: send(6 + i, d_two_part.at[members[i]], got_two.at[i], peers[i]) for i in (2, 0, 1)}
+    own_load = move(0, d_two_part.at[member], own_two)
+    core_copies = {}
+    for w in range(3):
+        for x in range(2):
+            core_copies[w, x] = send(
+                2 * w + x, ffn_parts[w].at[x, 1 - core], from_core.at[w, x], core_mate
+            )
+    inputs_in = (
+        (middle_in, middle),
+        (upstream_in.at[member], upstream),
+        (wo_in, wo),
+        (attended_in, attended),
+        (query_in, query_rot),
+        (keys_in, keys),
+        (values_in, values),
+        (wq_in, wq),
+        (wkv_in, wkv),
+        (normed_in, normed),
+        (tokens_in, xs),
+    )
+    kept = [move(4 + i, source, target) for i, (source, target) in enumerate(inputs_in)]
+
+    units = []
+    for w in range(3):
+        units.append((w, 1 - chip, 1 - micro))
+    for w in (0, 1):
+        units.append((w, chip, 1 - micro))
+        units.append((w, 1 - chip, micro))
+    units.append((2, chip, 1 - micro))
+    units.append((2, 1 - chip, micro))
+    for w in range(3):
+        units.append((w, chip, micro))
+    turn_of = {"next": 0, "load": None}
+
+    def load_unit(number):
+        w, x, m = units[number]
+        return move(15 + number % 2, ffn_parts[w].at[x, core, m], unit_stage.at[number % 2])
+
+    def next_unit():
+        number = turn_of["next"]
+        turn_of["load"].wait()
+        if number + 1 < len(units):
+            turn_of["load"] = load_unit(number + 1)
+        turn_of["next"] = number + 1
+        return unit_stage.at[number % 2]
+
+    turn_of["load"] = load_unit(0)
+    chip_copies, half_copies, last_copies, here_copies = {}, {}, [], []
+
+    def chip_unit(w, m, index):
+        part = next_unit()
+        if (w, "core") not in turn_of:
+            turn_of[w, "core"] = True
+            core_copies[w, 0].wait()
+            core_copies[w, 1].wait()
+
+        @pl.loop(0, group)
+        def _(t):
+            total = from_core[w, 1 - chip, m, t].astype(jnp.float32) + part[t].astype(jnp.float32)
+            from_core[w, 1 - chip, m, t] = total.astype(jnp.bfloat16)
+
+        chip_copies[w, index] = send(
+            9 + 2 * w + index, from_core.at[w, 1 - chip, m], from_chip.at[w, m], chip_mate
+        )
+
+    def half_unit(w):
+        part = next_unit()
+        chip_copies[w, 0].wait()
+
+        @pl.loop(0, group)
+        def _(t):
+            total = from_core[w, chip, 1 - micro, t].astype(jnp.float32) + part[t].astype(jnp.float32)
+            total += from_chip[w, 1 - micro, t].astype(jnp.float32)
+            from_chip[w, 1 - micro, t] = total.astype(jnp.bfloat16)
+
+        half_copies[w] = send(15 + w, from_chip.at[w, 1 - micro], from_half.at[w], partner)
+
+    def last_unit(w):
+        part = next_unit()
+        chip_copies[w, 1].wait()
+        half_copies[w].wait()
+
+        @pl.loop(0, group)
+        def _(t):
+            total = from_core[w, chip, micro, t].astype(jnp.float32) + part[t].astype(jnp.float32)
+            total += from_chip[w, micro, t].astype(jnp.float32) + from_half[w, t].astype(jnp.float32)
+            from_chip[w, micro, t] = total.astype(jnp.bfloat16)
+
+        for i in range(group - 1):
+            last_copies.append(
+                send(18 + 3 * w + i, from_chip.at[w, micro, members[i]], ffn_grad.at[w, member], peers[i])
+            )
+        here_copies.append(move(17 + w, from_chip.at[w, micro, member], ffn_grad.at[w, member]))
+
+    chip_unit(0, 1 - micro, 0)
+    chip_unit(1, 1 - micro, 0)
+
+    kept[0].wait()
+    kept[1].wait()
+    gain_one = jnp.concatenate([gains[f, 0:1, :] for f in range(KV)], axis=1)
+    gain_two = jnp.concatenate([gains[f, 1:2, :] for f in range(KV)], axis=1)
+    own_load.wait()
+    upstream_rows = own_two[...].astype(jnp.float32)
+    for i in range(group - 1):
+        sums_two[i].wait()
+        upstream_rows += got_two[i].astype(jnp.float32)
+    middle_rows = middle[...]
+    grad, two_term = norm_back(middle_rows, rms_scale(middle_rows), gain_two, upstream_rows)
+    grad += upstream[...].astype(jnp.float32)
+    d_middle[...] = grad
+    d_full[member] = grad.astype(jnp.bfloat16)
+    gather = [send(27 + i, d_full.at[member], d_full.at[member], device) for i, device in enumerate(peers)]
+    block_load = move(1, block_part.at[member], own_block)
+
+    first_len = seq_len[slot_order[2 * (shard * MB + micro)]]
+    both_len = first_len + seq_len[slot_order[2 * (shard * MB + micro) + 1]]
+    bias[...] = pair_bias(window, group, tok_rows, first_len, both_len)
+    chip_unit(2, 1 - micro, 0)
+
+    for i in (2, 3, 4, 5, 6):
+        kept[i].wait()
+
+    def attention_grad(rows):
+        place_rows = pl.ds(pl.multiple_of(rows * own_rows, own_rows), own_rows)
+        d_attended[place_rows, :] = contract_cols(d_full[rows], wo[...]).astype(jnp.bfloat16)
+
+    attention_grad(member)
+    for i, copy in enumerate(gather):
+        copy.wait()
+        attention_grad(members[i])
+
+    sums_block = {i: send(30 + i, block_part.at[members[i]], got_two.at[i], peers[i]) for i in (2, 0, 1)}
+
+    same_chip = chip == member // 2
+    same_core = core == member % 2
+    d_rows = d_full[...].reshape(window, D)
+    for j in range(width_q // 128):
+        part = contract_rows(attended[:, j * 128 : (j + 1) * 128], d_rows)
+        for k in range(128 // tok_rows):
+            out_part[j * (128 // tok_rows) + k] = part[k * tok_rows : (k + 1) * tok_rows].astype(jnp.bfloat16)
+    out_by_core = copy_to(33, out_part, out_core, core_mate)
+    out_by_chip = copy_to(34, out_part, out_chip, chip_mate)
+    out_by_half = copy_to(35, out_part.at[pl.ds((1 - micro) * group, group)], out_half, partner)
+
+    @pl.when(jnp.logical_not(same_core))
+    def _():
+        out_by_core.start()
+
+    half_unit(0)
+    chip_unit(0, micro, 1)
+    half_unit(1)
+    chip_unit(1, micro, 1)
+
+    @pl.when(jnp.logical_not(same_core))
+    def _():
+        out_by_core.wait_send()
+
+    @pl.when(same_core)
+    def _():
+        out_by_core.wait_recv()
+
+        @pl.loop(0, MB * group)
+        def _(t):
+            total = out_part[t].astype(jnp.float32) + out_core[t].astype(jnp.float32)
+            out_part[t] = total.astype(jnp.bfloat16)
+
+    @pl.when(same_core & jnp.logical_not(same_chip))
+    def _():
+        out_by_chip.start()
+
+    key_twice, value_twice = keys[...], values[...]
+    lower = lane_ids(key_twice.shape) < HDIM
+    zero = jnp.zeros_like(key_twice)
+    key_low, key_high = jnp.where(lower, key_twice, zero), jnp.where(lower, zero, key_twice)
+    value_low, value_high = jnp.where(lower, value_twice, zero), jnp.where(lower, zero, value_twice)
+    key_low_turned, key_high_turned = key_low.T, key_high.T
+    key_sum[...] = jnp.zeros_like(key_sum)
+    value_sum[...] = jnp.zeros_like(value_sum)
+
+    def attention_pair(j):
+        lanes = pl.ds(pl.multiple_of(j * 128, 128), 128)
+        query_pair, grad_pair = query_rot[:, lanes], d_attended[:, lanes]
+        total = jnp.zeros((2 * HDIM, window), jnp.float32)
+        for side, (key_side, value_side, key_turned) in enumerate(
+            ((key_low, value_low, key_low_turned), (key_high, value_high, key_high_turned))
+        ):
+            probs = softmax_columns(key_side, query_pair, bias[...])
+            d_probs = contract_cols(value_side, grad_pair)
+            inner = jnp.sum(probs * d_probs, axis=0, keepdims=True)
+            d_scores = (probs * (d_probs - inner)).astype(jnp.bfloat16)
+            total += plain_dot(key_turned, d_scores)
+            key_sum[side] += plain_dot(d_scores, query_pair)
+            value_sum[side] += plain_dot(probs.astype(jnp.bfloat16), grad_pair)
+        grad_rot = total.T * HDIM**-0.5
+        d_query[:, lanes] = (grad_rot * cosine[...] + turn_back(grad_rot * sine[...])).astype(jnp.bfloat16)
+
+    pl.loop(0, width_q // 256)(attention_pair)
+    half_unit(2)
+    chip_unit(2, micro, 1)
+    pl.loop(width_q // 256, width_q // 128)(attention_pair)
+
+    fold = lambda sums: jnp.where(lower, sums[0] + pltpu.roll(sums[1], HDIM, 1), 0.0)
+    key_grad, value_grad = fold(key_sum), fold(value_sum)
+    key_grad = key_grad * cosine[...] + turn_back(key_grad * sine[...])
+    d_pair[...] = jnp.where(lower, key_grad, pltpu.roll(value_grad, HDIM, 1)).astype(jnp.bfloat16)
+
+    block_load.wait()
+    block = middle[...] + own_block[...].astype(jnp.float32)
+    for i in range(group - 1):
+        sums_block[i].wait()
+        block += got_two[i].astype(jnp.float32)
+
+    for i in (7, 8, 9, 10):
+        kept[i].wait()
+
+    def project_back(rows):
+        place_rows = pl.ds(pl.multiple_of(rows * own_rows, own_rows), own_rows)
+        grad_rows, pair_rows = d_query[place_rows, :], d_pair[place_rows, :]
+        return jnp.concatenate(
+            [contract_cols(grad_rows, wq[f]) + contract_cols(pair_rows, wkv[f]) for f in range(KV)], axis=1
+        )
+
+    sums_one = {}
+    for i in (2, 0, 1):
+        sent[i] = project_back(members[i]).astype(jnp.bfloat16)
+        sums_one[i] = send(36 + i, sent.at[i], got_one.at[i], peers[i])
+    own_one[...] = project_back(member)
+
+    def give(slot, rows, target):
+        rows_out[slot] = jnp.where(micro == 0, rows[tok_rows:], rows[:tok_rows]).astype(jnp.bfloat16)
+        target[micro] = jnp.where(micro == 0, rows[:tok_rows], rows[tok_rows:])
+        return send(39 + slot, rows_out.at[slot], rows_got.at[slot], partner)
+
+    def take(slot, copy, target):
+        copy.wait()
+        target[1 - micro] = rows_got[slot].astype(jnp.float32)
+
+    give_block = give(0, block, block_out)
+
+    normed_rows = normed
+    d_all = jnp.concatenate([d_query[...], d_pair[...]], axis=1)
+    late_core_copies = []
+
+    def late_part(x, c):
+        for m in range(MB):
+            first = ((x * 2 + c) * MB + m) * (group * tok_rows)
+            columns = pl.ds(pl.multiple_of(first, group * tok_rows), group * tok_rows)
+            rows = normed_rows[:, :, columns].reshape(window, group * tok_rows)
+            part = contract_rows(rows, d_all)
+            late[x, c, m] = part.astype(jnp.bfloat16).reshape(group, tok_rows, -1)
+
+    for x in range(2):
+        late_part(x, 1 - core)
+        late_core_copies.append(send(41 + x, late.at[x, 1 - core], late_core.at[x], core_mate))
+    for x in range(2):
+        late_part(x, core)
+
+    last_unit(0)
+    for copy in late_core_copies:
+        copy.wait()
+
+    @pl.loop(0, MB * group)
+    def _(k):
+        m, t = k // group, k % group
+        total = late[1 - chip, core, m, t].astype(jnp.float32) + late_core[1 - chip, m, t].astype(jnp.float32)
+        late[1 - chip, core, m, t] = total.astype(jnp.bfloat16)
+
+    late_to_chip = send(43, late.at[1 - chip, core], late_chip, chip_mate)
+
+    @pl.when(same_core & jnp.logical_not(same_chip))
+    def _():
+        out_by_chip.wait_send()
+
+    @pl.when(same_core & same_chip)
+    def _():
+        out_by_chip.wait_recv()
+
+        @pl.loop(0, MB * group)
+        def _(t):
+            total = out_part[t].astype(jnp.float32) + out_chip[t].astype(jnp.float32)
+            out_part[t] = total.astype(jnp.bfloat16)
+
+        out_by_half.start()
+
+    inputs = xs[...].reshape(own_rows, D).astype(jnp.float32)
+    upstream_rows = own_one[...]
+    for i in range(group - 1):
+        sums_one[i].wait()
+        upstream_rows += got_one[i].astype(jnp.float32)
+    grad, one_term = norm_back(inputs, rms_scale(inputs), gain_one, upstream_rows)
+    give_grad = give(1, grad + d_middle[...], input_grad)
+    gain_part[...] = jnp.concatenate([one_term[None], two_term[None], jnp.zeros((6, D), jnp.float32)], axis=0)
+
+    gain_core = send(44, gain_part, gain_got.at[0], core_mate)
+    last_unit(1)
+    gain_core.wait()
+    gain_part[...] = gain_part[...] + gain_got[0]
+    gain_chip = send(45, gain_part, gain_got.at[1], chip_mate)
+
+    late_to_chip.wait()
+
+    @pl.loop(0, group)
+    def _(t):
+        total = late[chip, core, 1 - micro, t].astype(jnp.float32) + late_core[chip, 1 - micro, t].astype(jnp.float32)
+        total += late_chip[1 - micro, t].astype(jnp.float32)
+        late_chip[1 - micro, t] = total.astype(jnp.bfloat16)
+
+    late_to_half = send(46, late_chip.at[1 - micro], late_half, partner)
+    gain_chip.wait()
+    gain_part[...] = gain_part[...] + gain_got[1]
+    gain_half = send(47, gain_part, gain_got.at[2], partner)
+
+    last_unit(2)
+    take(0, give_block, block_out)
+
+    out_here = pltpu.make_async_copy(out_part.at[micro * group + member], out_grad, local_sem.at[24])
+
+    def out_to(i):
+        return pltpu.make_async_remote_copy(
+            src_ref=out_part.at[micro * group + members[i]],
+            dst_ref=out_grad,
+            send_sem=send_sem.at[48 + i],
+            recv_sem=recv_sem.at[48],
+            device_id=peers[i],
+            device_id_type=MESH,
+        )
+
+    @pl.when(same_core & same_chip)
+    def _():
+        out_by_half.wait()
+
+        @pl.loop(0, group)
+        def _(t):
+            total = out_part[micro * group + t].astype(jnp.float32) + out_half[t].astype(jnp.float32)
+            out_part[micro * group + t] = total.astype(jnp.bfloat16)
+
+        for i in range(group - 1):
+            out_to(i).start()
+        out_here.start()
+
+    gain_half.wait()
+    gain_part[...] = gain_part[...] + gain_got[2]
+    gain_all = [send(51 + i, gain_part, gain_got.at[3 + i], device) for i, device in enumerate(peers)]
+
+    late_to_half.wait()
+
+    @pl.loop(0, group)
+    def _(t):
+        total = late[chip, core, micro, t].astype(jnp.float32) + late_core[chip, micro, t].astype(jnp.float32)
+        total += late_chip[micro, t].astype(jnp.float32) + late_half[t].astype(jnp.float32)
+        late_chip[micro, t] = total.astype(jnp.bfloat16)
+
+    for i in range(group - 1):
+        last_copies.append(send(54 + i, late_chip.at[micro, members[i]], qkv_grad.at[member], peers[i]))
+    here_copies.append(move(25, late_chip.at[micro, member], qkv_grad.at[member]))
+    take(1, give_grad, input_grad)
+    for copy in gain_all:
+        copy.wait()
+    gain_sum[...] = gain_part[...] + gain_got[3] + gain_got[4] + gain_got[5]
+
+    @pl.when(same_core & same_chip)
+    def _():
+        for i in range(group - 1):
+            out_to(i).wait_send()
+        out_here.wait()
+
+    @pl.when(jnp.logical_not(same_core & same_chip))
+    def _():
+        out_to(0).wait_recv()
+
+    for copy in (*last_copies, *here_copies):
+        copy.wait()
+
+
+def back(n_sp, tok_rows, heads, *operands):
+    group = n_sp // MB
+    own_rows = MB * tok_rows
+    window = group * own_rows
+    width_q = heads * HDIM
+    width_f = FF // group
+    width_l = width_q + 2 * HDIM
+    low, full = jnp.bfloat16, jnp.float32
+    vmem = pl.BlockSpec(memory_space=pltpu.VMEM)
+    anywhere = pl.BlockSpec(memory_space=pl.ANY)
+    smem = pl.BlockSpec(memory_space=pltpu.SMEM)
+    shape = jax.ShapeDtypeStruct
+    return pl.pallas_call(
+        functools.partial(back_kernel, n_sp),
+        out_shape=(
+            shape((MB, tok_rows, D), full),
+            shape((MB, tok_rows, D), full),
+            shape((3, group, tok_rows, width_f), low),
+            shape((group, tok_rows, width_l), low),
+            shape((tok_rows, D), low),
+            shape((8, D), full),
+        ),
+        in_specs=[anywhere] * 16 + [smem] * 2 + [vmem] * 3,
+        out_specs=(vmem, vmem, anywhere, anywhere, anywhere, vmem),
+        scratch_shapes=[
+            pltpu.VMEM((own_rows, D), low),
+            pltpu.VMEM((own_rows, D), low),
+            pltpu.VMEM((own_rows, D), full),
+            pltpu.VMEM((own_rows, D), full),
+            pltpu.VMEM((MB, tok_rows, D), low),
+            pltpu.VMEM((own_rows, D), low),
+            pltpu.VMEM((group, own_rows, D), low),
+            pltpu.VMEM((window, width_q), low),
+            pltpu.VMEM((window, 2 * HDIM), low),
+            pltpu.VMEM((window, 2 * HDIM), low),
+            pltpu.VMEM((window, width_q), low),
+            pltpu.VMEM((KV, D // KV, width_q), low),
+            pltpu.VMEM((KV, D // KV, 2 * HDIM), low),
+            pltpu.VMEM((width_q, D), low),
+            pltpu.VMEM((own_rows, D), full),
+            pltpu.VMEM((group, own_rows, D), low),
+            pltpu.VMEM((window, width_q), low),
+            pltpu.VMEM((window, width_q), low),
+            pltpu.VMEM((window, 2 * HDIM), low),
+            pltpu.VMEM((2, window, 2 * HDIM), full),
+            pltpu.VMEM((2, window, 2 * HDIM), full),
+            pltpu.VMEM((window, window), full),
+            pltpu.VMEM((group - 1, own_rows, D), low),
+            pltpu.VMEM((group - 1, own_rows, D), low),
+            pltpu.VMEM((group - 1, own_rows, D), low),
+            pltpu.VMEM((2, tok_rows, D), low),
+            pltpu.VMEM((2, tok_rows, D), low),
+            pltpu.VMEM((3, 2, MB, group, tok_rows, width_f), low),
+            pltpu.VMEM((3, MB, group, tok_rows, width_f), low),
+            pltpu.VMEM((3, group, tok_rows, width_f), low),
+            pltpu.VMEM((2, group, tok_rows, width_f), low),
+            pltpu.VMEM((2, 2, MB, group, tok_rows, width_l), low),
+            pltpu.VMEM((2, MB, group, tok_rows, width_l), low),
+            pltpu.VMEM((MB, group, tok_rows, width_l), low),
+            pltpu.VMEM((group, tok_rows, width_l), low),
+            pltpu.VMEM((MB * group, tok_rows, D), low),
+            pltpu.VMEM((MB * group, tok_rows, D), low),
+            pltpu.VMEM((MB * group, tok_rows, D), low),
+            pltpu.VMEM((group, tok_rows, D), low),
+            pltpu.VMEM((8, D), full),
+            pltpu.VMEM((6, 8, D), full),
+            pltpu.SemaphoreType.DMA((26,)),
+            pltpu.SemaphoreType.DMA((57,)),
+            pltpu.SemaphoreType.DMA((57,)),
+        ],
+        compiler_params=pltpu.CompilerParams(
+            collective_id=1, has_side_effects=True, vmem_limit_bytes=VMEM_BYTES
+        ),
+        cost_estimate=pl.CostEstimate(flops=14 * 10**9, bytes_accessed=60 * 10**6, transcendentals=2 * 10**6),
+        name="back",
+    )(*operands)
+
+
 def group_body(
     tokens,
     cotangent,
@@ -750,53 +1305,6 @@
     tok_rows = tokens.shape[1]
     window = n_sp * tok_rows
     own_rows = MB * tok_rows
-    groups = [[m * group + t for t in range(group)] for m in range(MB)]
-    both = ("fsdp", "sp")
-    members = [(m * group + t, t) for m in range(MB) for t in range(group)]
-    flat = lambda f, s: f * n_sp + s
-
-    def swap(array):
-        return lax.ppermute(array, "sp", [(s, (s + group) % n_sp) for s in range(n_sp)])
-
-    def pick(pair, index):
-        return lax.dynamic_index_in_dim(pair, index, 0, keepdims=False)
-
-    def in_order(mine, theirs):
-        return jnp.where(micro == 0, jnp.concatenate([mine, theirs]), jnp.concatenate([theirs, mine]))
-
-    def gather_rows(array):
-        return lax.all_gather(array, "sp", axis=0, tiled=True, axis_index_groups=groups)
-
-    def sum_rows(partial):
-        pieces = lax.all_to_all(
-            partial.astype(jnp.bfloat16).reshape(group, own_rows, D),
-            "sp", split_axis=0, concat_axis=0, tiled=True, axis_index_groups=groups,
-        )
-        return jnp.sum(pieces.astype(jnp.float32), axis=0)
-
-    def gather_weight(weight):
-        width = weight.shape[1] // group
-        part = lax.dynamic_slice_in_dim(weight, member * width, width, 1)
-        return lax.all_gather(part, "fsdp", axis=0, tiled=True)
-
-    def reduce_weight(partial):
-        width = partial.shape[1]
-        rows = partial.reshape(2, 2, MB, group, tok_rows, width)
-
-        def halve(array, axis, index, axis_name, perm):
-            keep = lax.dynamic_index_in_dim(array, index, axis, keepdims=False)
-            send = lax.dynamic_index_in_dim(array, 1 - index, axis, keepdims=False)
-            got = lax.ppermute(send.astype(jnp.bfloat16), axis_name, perm)
-            return keep + got.astype(jnp.float32)
-
-        rows = halve(rows, 1, shard % 2, "fsdp", [(f, f ^ 1) for f in range(n_fsdp)])
-        rows = halve(rows, 0, shard // 2, "fsdp", [(f, f ^ 2) for f in range(n_fsdp)])
-        rows = halve(rows, 0, micro, "sp", [(s, (s + group) % n_sp) for s in range(n_sp)])
-        rows = lax.all_to_all(
-            rows.astype(jnp.bfloat16), "sp", split_axis=0, concat_axis=0, tiled=True, axis_index_groups=groups
-        )
-        return rows.astype(jnp.float32).transpose(1, 0, 2).reshape(tok_rows, group * width)
-
     first_len = seq_len[slot_order[2 * (shard * MB + micro)]]
     second_len = seq_len[slot_order[2 * (shard * MB + micro) + 1]]
     place = row_places((window,), 0, group, tok_rows)
@@ -836,97 +1344,47 @@
         tokens, cotangent, seq_len, slot_order, gains,
         query_weight, kv_weight, output_weight, gate_weight, up_weight, down_weight, cosine, sine,
     )
-    gain_one, gain_two = gains[:, 0].reshape(D), gains[:, 1].reshape(D)
-    upstream_low, normed, normed_two = (rows.reshape(window, D) for rows in (upstream_low, normed, normed_two))
-    w_query, w_kv, w_gate, w_up, w_down = (w.reshape(D, -1) for w in (w_query, w_kv, w_gate, w_up, w_down))
-    w_key, w_value = w_kv[:, :HDIM], w_kv[:, HDIM:]
-    inputs = own_tokens.reshape(own_rows, D).astype(jnp.float32)
-    upstream = lax.dynamic_slice_in_dim(upstream_low, member * own_rows, own_rows, 0).astype(jnp.float32)
-    scale_one = rms_scale(inputs)
-    scale_two = rms_scale(middle)
-    cosine, sine = cosine[:, None, :HDIM], sine[:, None, :HDIM]
-    query_rot = query_rot.reshape(window, heads, HDIM)
-    key_rot, value = keys[:, :HDIM], values[:, :HDIM]
-    scale = HDIM**-0.5
-    scores = jnp.einsum("qhd,kd->hqk", query_rot, key_rot, preferred_element_type=jnp.float32) * scale
-    scores = scores + pair_bias(window, group, tok_rows, first_len, first_len + second_len)[None]
-    probs = jax.nn.softmax(scores, axis=-1)
-    probs_low = probs.astype(jnp.bfloat16)
-    gate = plain_dot(normed_two, w_gate)
-    up = plain_dot(normed_two, w_up)
+    upstream_rows, normed_rows = upstream_low.reshape(window, D), normed_two.reshape(window, D)
+    gate_full, up_full, down_full = (w.reshape(D, -1) for w in (w_gate, w_up, w_down))
+    gate = plain_dot(normed_rows, gate_full)
+    up = plain_dot(normed_rows, up_full)
+    d_hidden = plain_dot(upstream_rows, down_full)
     sig = jax.nn.sigmoid(gate)
     silu = gate * sig
     hidden = (silu * up).astype(jnp.bfloat16)
-    block = middle + sum_rows(contract_cols(hidden, w_down))
-    d_hidden = plain_dot(upstream_low, w_down)
     d_up = (d_hidden * silu).astype(jnp.bfloat16)
     d_gate = (d_hidden * up * sig * (1.0 + gate * (1.0 - sig))).astype(jnp.bfloat16)
-    d_normed_two = sum_rows(contract_cols(d_gate, w_gate) + contract_cols(d_up, w_up))
-    d_middle, gain_two_term = norm_back(middle, scale_two, gain_two, d_normed_two)
-    d_middle = d_middle + upstream
-    middle_low = gather_rows(d_middle.astype(jnp.bfloat16))
-
-    d_attended = contract_cols(middle_low, w_output).astype(jnp.bfloat16).reshape(window, heads, HDIM)
-    d_probs = jnp.einsum("qhd,kd->hqk", d_attended, value, preferred_element_type=jnp.float32)
-    inner_sum = jnp.sum(probs * d_probs, axis=-1, keepdims=True)
-    d_scores = (probs * (d_probs - inner_sum)).astype(jnp.bfloat16)
-    d_query_rot = jnp.einsum("hqk,kd->qhd", d_scores, key_rot, preferred_element_type=jnp.float32) * scale
-    d_key_rot = jnp.einsum("hqk,qhd->kd", d_scores, query_rot, preferred_element_type=jnp.float32) * scale
-    d_value = jnp.einsum("hqk,qhd->kd", probs_low, d_attended, preferred_element_type=jnp.float32)
-    d_query = rope_back(d_query_rot, cosine, sine).astype(jnp.bfloat16).reshape(window, heads * HDIM)
-    d_key = rope_back(d_key_rot[:, None], cosine, sine)[:, 0].astype(jnp.bfloat16)
-    d_value = d_value.astype(jnp.bfloat16)
-    d_normed = sum_rows(
-        contract_cols(d_query, w_query) + contract_cols(d_key, w_key) + contract_cols(d_value, w_value)
+    d_two_part = contract_cols(d_gate, gate_full) + contract_cols(d_up, up_full)
+    block_part = contract_cols(hidden, down_full)
+    gate_part = contract_rows(normed_rows, d_gate).astype(jnp.bfloat16)
+    up_part = contract_rows(normed_rows, d_up).astype(jnp.bfloat16)
+    down_part = contract_rows(upstream_rows, hidden).astype(jnp.bfloat16)
+    by_owner = lambda part: part.reshape(2, 2, MB, group, tok_rows, -1)
+    by_member = lambda part: part.reshape(group, own_rows, D).astype(jnp.bfloat16)
+    block, d_inputs, ffn_grad, qkv_grad, output_grad, gain_sum = back(
+        n_sp, tok_rows, heads,
+        by_member(d_two_part), by_member(block_part), by_owner(gate_part), by_owner(up_part), by_owner(down_part),
+        middle, own_tokens, upstream_low, normed, query_rot, keys, values, attended,
+        w_query, w_kv, w_output, seq_len, slot_order, gains, cosine, sine,
     )
-    d_inputs, gain_one_term = norm_back(inputs, scale_one, gain_one, d_normed)
-    d_inputs = d_inputs + d_middle
-
-    def to_owner(rows):
-        halves = rows.reshape(MB, tok_rows, D)
-        mine, theirs = pick(halves, micro), swap(pick(halves, 1 - micro))
-        return jnp.where(micro == 0, jnp.stack([mine, theirs]), jnp.stack([theirs, mine]))
-
-    gate_grad = reduce_weight(contract_rows(normed_two, d_gate))
-    up_grad = reduce_weight(contract_rows(normed_two, d_up))
-    down_grad = reduce_weight(contract_rows(upstream_low, hidden))
-    query_grad = reduce_weight(contract_rows(normed, d_query))
-    key_grad = reduce_weight(contract_rows(normed, d_key))
-    value_grad = reduce_weight(contract_rows(normed, d_value))
-
-    output_part = contract_rows(attended, middle_low)
-    got = lax.ppermute(
-        output_part.astype(jnp.bfloat16), both,
-        [(flat(t ^ k ^ 1, s), flat(t ^ k, s)) for s, t in members for k in (0, 2)],
-    )
-    output_part = output_part + got.astype(jnp.float32)
-    got = lax.ppermute(
-        output_part.astype(jnp.bfloat16), both, [(flat(t ^ 2, s), flat(t, s)) for s, t in members]
-    )
-    output_part = (output_part + got.astype(jnp.float32)).reshape(MB, group * tok_rows, D)
-    got = swap(pick(output_part, 1 - micro).astype(jnp.bfloat16))
-    output_part = pick(output_part, micro) + got.astype(jnp.float32)
-    pieces = lax.all_to_all(
-        output_part.astype(jnp.bfloat16).reshape(group, tok_rows, D),
-        "sp", split_axis=0, concat_axis=0, tiled=True, axis_index_groups=groups,
-    )
-    output_grad = pick(pieces, shard).astype(jnp.float32)
-
-    gains = lax.psum_scatter(
-        jnp.stack([gain_one_term, gain_two_term]), both, scatter_dimension=1, tiled=True
-    )
+    gain_own = lax.dynamic_slice_in_dim(gain_sum, (shard * n_sp + rank) * tok_rows, tok_rows, 1)
+
+    def side_by_side(pieces):
+        return jnp.swapaxes(pieces, 0, 1).reshape(tok_rows, -1).astype(jnp.float32)
+
+    width_q = heads * HDIM
     return (
-        to_owner(block),
-        to_owner(d_inputs),
-        gains[0],
-        query_grad,
-        key_grad,
-        value_grad,
-        output_grad,
-        gains[1],
-        gate_grad,
-        up_grad,
-        down_grad,
+        block,
+        d_inputs,
+        gain_own[0],
+        side_by_side(qkv_grad[:, :, :width_q]),
+        side_by_side(qkv_grad[:, :, width_q : width_q + HDIM]),
+        side_by_side(qkv_grad[:, :, width_q + HDIM :]),
+        output_grad.astype(jnp.float32),
+        gain_own[1],
+        side_by_side(ffn_grad[0]),
+        side_by_side(ffn_grad[1]),
+        side_by_side(ffn_grad[2]),
     )
 
 

time: 798 us -> 462 us (0.58)
  waiting for transfers between devices: 287 us -> 0 us
  Pallas kernels: 169 us -> 382 us
  other arithmetic: 79.7 us -> 7.16 us
  starting transfers between devices: 62 us -> 0 us
  local copies, waits for them, and re-layouts: 74.5 us -> 15.3 us
  matrix products: 94.1 us -> 43.2 us
  between operations: 20.9 us -> 6.55 us
    pallas_call x0 -> x1, Pallas kernels: none -> 213 us  [back(): pl.pallas_call(functools.partial(back_kernel, n_sp), out_shape=(shape((MB...]
    ppermute x23 -> x0, waiting for transfers between devices: 150 us -> none  [the longest x18 138 us: halve(): got = lax.ppermute(send.astype(jnp.bfloat16), axis_name, perm)]
    unnamed x3 -> x0, waiting for transfers between devices: 135 us -> none
    all_to_all x10 -> x0, starting transfers between devices: 44.4 us -> none  [the longest x6 27.1 us: reduce_weight(): lax.all_to_all(rows.astype(jnp.bfloat16), 'sp', split_axis=0, concat_axis...]
    add x15 -> x0, other arithmetic: 30.4 us -> none  [the longest x12 24.3 us: halve(): return keep + got.astype(jnp.float32)]
    unnamed x145 -> x24, local copies, waits for them, and re-layouts: 26.5 us -> 2.41 us
    convert_element_type x13 -> x3, other arithmetic: 26.1 us -> 2.5 us  [the longest x1 1 us: side_by_side(): return jnp.swapaxes(pieces, 0, 1).reshape(tok_rows, -1).astype(jnp.float32)]
    dot_general x7 -> x3, matrix products: 32.8 us -> 12.8 us  [contract_cols(): lax.dot_general(left_side, right_side, (((1,), (1,)), ((), ())), preferre...]
  transfers between devices with their start and end apart: 35 -> 0, of which waited for: 13 -> 0; matrix products, arithmetic and copies ran while one was open for 25% -> 0% of each run, Pallas kernels for 0% -> 0%
where the time goes in v3:
time: 462 us; the launch traced here: 454 us
  Pallas kernels  382 us (83%)
  matrix products  43.2 us (9%)
  local copies, waits for them, and re-layouts  15.3 us (3%)
  other arithmetic  7.16 us (2%)
  between operations  6.55 us (1%)
    pallas_call x1, Pallas kernels, back(): pl.pallas_call(functools.partial(back_kernel, n_sp), out_shape=(shape((MB...  213 us
    pallas_call x1, Pallas kernels, front(): pl.pallas_call(functools.partial(front_kernel, n_sp), out_shape=(shape((M...  169 us
    dot_general x3, matrix products, contract_rows(): lax.dot_general(left_side, right_side, (((0,), (0,)), ((), ())), preferre...  16 us
    dot_general x3, matrix products, plain_dot(): return jnp.dot(left_side, right_side, preferred_element_type=jnp.float32)  14.4 us
    dot_general x3, matrix products, contract_cols(): lax.dot_general(left_side, right_side, (((1,), (1,)), ((), ())), preferre...  12.8 us

profile of v3, /device:TPU:0, one launch (start us, length us, event | category | flops | bytes accessed | tf_op | source)
XLA Modules:
  0.0 453.8 jit_solution(8556100842485037636)
XLA Ops:
  0.7 1.3 fusion.20
  5.9 1.3 fusion.19
  8.6 0.7 subtract_convert_fusion
  9.4 0.7 broadcast_in_dim.16
  10.1 0.7 broadcast_in_dim.17
  10.7 0.7 maximum_convert_fusion.gains
  11.4 1.1 constant_dynamic-slice_fusion.1
  12.5 0.8 pad_maximum_fusion.wkv_in
  13.3 1.8 multiply_sine_fusion
  15.1 169.0 %front.1 = (bf16[2,64,2048]{2,1,0:T(8,128)(2,1)}, bf16[4,128,2048]{2,1,0:T(8,128)(2,1)}, bf16[4,128,2048]{2,1,0:T(8,128)(2,1)}, bf16[512,512]{1,0:T(8,128)(2,1)}...) custom-call(bf16[2,64,2048]{2,1,0:T(8,128)(2,1)} %tokens.1, ...), custom_call_target="tpu_custom_call" | custom-call | flops 8000000000 | bytes 40000000 | tf_op jit(solution)/shard_map/front/pallas_call | solution.py:686
  184.2 6.7 %fusion.22 = f32[512,1408]{1,0:T(8,128)S(1)} fusion(bf16[512,2048]{1,0:T(8,128)(2,1)} %bitcast.86, bf16[2048,1408]{1,0:T(8,128)(2,1)} %bitcast.79), kind=kOutput, calls=%fused_computation.58 | convolution fusion | flops 2952790016 | bytes 10747904 | tf_op jit(solution)/shard_map/dot_general | solution.py:26
  190.9 3.4 fusion.21
  194.4 4.3 multiply_convert_fusion
  198.7 3.4 fusion.23
  202.1 4.7 %add_convert_fusion = bf16[512,2048]{1,0:T(8,128)(2,1)} fusion(f32[512,2048]{1,0:T(8,128)S(1)} %fusion.23, bf16[512,1408]{1,0:T(8,128)(2,1)S(1)} %get-tuple-element.57, bf16[2048,1408]{1,0:T(8,128)(2,1)S(1)} %bitcast.77), kind=kOutput, calls=%fused_computation.3 | convolution fusion | flops 2954887168 | bytes 13500416 | tf_op jit(solution)/shard_map/dot_general | solution.py:36
  206.9 4.7 %convolution_convert_fusion.3.block_part = bf16[4,128,2048]{2,1,0:T(8,128)(2,1)} fusion(bf16[4,128,1408]{2,1,0:T(8,128)(2,1)S(1)} %bitcast.91, bf16[2048,1408,1]{1,0,2:T(8,128)(2,1)S(1)} %bitcast.72), kind=kOutput, calls=%fused_computation.4 | convolution fusion | flops 2953838592 | bytes 9306112 | tf_op jit(solution)/shard_map/dot_general | solution.py:36
  211.5 5.2 %convolution_convert_fusion = bf16[2048,1408]{1,0:T(8,128)(2,1)} fusion(bf16[512,2048]{1,0:T(8,128)(2,1)S(1)} %bitcast.85, bf16[512,1408]{1,0:T(8,128)(2,1)S(1)} %get-tuple-element.55), kind=kOutput, calls=%fused_computation | convolution fusion | flops 2955673600 | bytes 9306112 | tf_op jit(solution)/shard_map/dot_general | solution.py:30
  216.8 5.5 %convolution_convert_fusion.2 = bf16[2048,1408]{1,0:T(8,128)(2,1)} fusion(bf16[512,2048]{1,0:T(8,128)(2,1)S(1)} %bitcast.88, bf16[512,1408]{1,0:T(8,128)(2,1)S(1)} %get-tuple-element.56), kind=kOutput, calls=%fused_computation.2 | convolution fusion | flops 2955673600 | bytes 9306112 | tf_op jit(solution)/shard_map/dot_general | solution.py:30
  222.2 5.3 %convolution_convert_fusion.1 = bf16[2048,1408]{1,0:T(8,128)(2,1)} fusion(bf16[512,2048]{1,0:T(8,128)(2,1)S(1)} %bitcast.89, bf16[512,1408]{1,0:T(8,128)(2,1)S(1)} %get-tuple-element.57), kind=kOutput, calls=%fused_computation.1 | convolution fusion | flops 2955673600 | bytes 9306112 | tf_op jit(solution)/shard_map/dot_general | solution.py:30
  227.5 212.5 %back.1 = (f32[2,64,2048]{2,1,0:T(8,128)}, f32[2,64,2048]{2,1,0:T(8,128)}, bf16[3,4,64,1408]{3,2,1,0:T(8,128)(2,1)}, bf16[4,64,640]{2,1,0:T(8,128)(2,1)}, bf16[64,2048]{1,0:T(8,128)(2,1)}, /*index=5*/f32[8,2048]{1,0:T(8,128)}) custom-call(bf16[4,128,2048]{2,1,0:T(8,128)(2,1)} %bitcast.90, bf16[4,128,2048]{2,1,0:T(8,128)(2,1)} %convolution_convert_fusion.3.block_part, ...), custom_call_target="tpu_custom_call" | custom-call | flops 14000000000 | bytes 60000000 | tf_op jit(solution)/shard_map/back/pallas_call | solution.py:1217
  440.0 0.9 constant_dynamic-slice_fusion
  441.4 1.0 convert_bitcast_fusion.4
  442.5 0.8 reshape.142
  443.4 0.8 reshape.141
  444.2 1.0 convert_bitcast_fusion.3
  445.2 0.8 copy.30
  446.0 0.8 convert_element_type.122
  447.3 1.2 copy.33
  448.5 1.2 copy.32
  449.7 1.2 copy.31
  451.4 1.0 copy.36
  452.3 1.0 copy.37
  (33 shorter events, 1.8 us)
Async XLA Ops:
  184.1 6.7 %copy-start.4 = (bf16[4,512,1408]{2,1,0:T(8,128)(2,1)S(1)}, bf16[4,512,1408]{2,1,0:T(8,128)(2,1)}, u32[]{:S(2)}) copy-start(bf16[4,512,1408]{2,1,0:T(8,128)(2,1)} %get-tuple-element.34) | copy-start | bytes 17301508
  184.1 6.7 %copy-start.5 = (bf16[4,128,2048]{2,1,0:T(8,128)(2,1)S(1)}, bf16[4,128,2048]{2,1,0:T(8,128)(2,1)}, u32[]{:S(2)}) copy-start(bf16[4,128,2048]{2,1,0:T(8,128)(2,1)} %get-tuple-element.33.upstream_in) | copy-start | bytes 6291460
  184.2 10.2 %slice-start = ((s8[5767168]{0:T(1024)(128)(4,1)}), s8[4194304]{0:T(1024)(128)(4,1)S(1)}, s32[]{:S(2)}) async-start(s8[5767168]{0:T(1024)(128)(4,1)} %bitcast.74), calls=%async_computation | async-start | bytes 8388608
  190.9 3.5 slice-start.1
  190.9 3.5 copy-start.6
  190.9 7.7 %slice-start.2 = ((s8[5767168]{0:T(1024)(128)(4,1)}), s8[4194304]{0:T(1024)(128)(4,1)S(1)}, s32[]{:S(2)}) async-start(s8[5767168]{0:T(1024)(128)(4,1)} %bitcast.80), calls=%async_computation.2 | async-start | bytes 8388608
  194.4 4.3 slice-start.3
  440.0 6.0 %copy-start.3 = (bf16[64,2048]{1,0:T(8,128)(2,1)S(1)}, bf16[64,2048]{1,0:T(8,128)(2,1)}, u32[]{:S(2)}) copy-start(bf16[64,2048]{1,0:T(8,128)(2,1)} %get-tuple-element.53) | copy-start | bytes 786436
  440.0 6.8 %copy-start = (bf16[3,4,64,1408]{3,2,1,0:T(8,128)(2,1)S(1)}, bf16[3,4,64,1408]{3,2,1,0:T(8,128)(2,1)}, u32[]{:S(2)}) copy-start(bf16[3,4,64,1408]{3,2,1,0:T(8,128)(2,1)} %get-tuple-element.54) | copy-start | bytes 6488068
  449.7 1.7 copy-start.2
  449.7 2.6 copy-start.1

commit v4 on v3

--- a/solution.py
+++ b/solution.py
@@ -421,11 +421,17 @@
     return ((ids % own_rows) // tok_rows) * (group * tok_rows) + (ids // own_rows) * tok_rows + ids % tok_rows
 
 
+def row_positions(window, dim, group, tok_rows, first_len, both_len):
+    shape = (window, 1) if dim == 0 else (1, window)
+    place = row_places(shape, dim, group, tok_rows)
+    anchor = jnp.where(place < first_len, 0, jnp.where(place < both_len, first_len, both_len))
+    return place, place - anchor
+
+
 def pair_bias(window, group, tok_rows, first_len, both_len):
-    place = row_places((1, window), 1, group, tok_rows)
+    place, position = row_positions(window, 1, group, tok_rows, first_len, both_len)
     key_place = row_places((window, 1), 0, group, tok_rows)
-    anchor = jnp.where(place < first_len, 0, jnp.where(place < both_len, first_len, both_len))
-    return jnp.where((key_place <= place) & (key_place >= anchor), 0.0, -1e30)
+    return jnp.where((key_place <= place) & (key_place >= place - position), 0.0, -1e30)
 
 
 def front_kernel(
@@ -434,15 +440,16 @@
     cotangent,
     seq_len,
     slot_order,
-    gains,
+    norm1_gain,
+    norm2_gain,
+    inverse,
+    key_in,
+    value_in,
     wq_in,
-    wkv_in,
     wo_in,
     wg_in,
     wu_in,
     wd_in,
-    cosine,
-    sine,
     xs,
     upstream,
     normed,
@@ -459,6 +466,10 @@
     wu,
     wd,
     gains_all,
+    cosine,
+    sine,
+    gains,
+    wkv_in,
     gs,
     sent,
     got,
@@ -496,6 +507,8 @@
     swap_g = send(1, cotangent.at[1 - micro], gs.at[micro], partner)
     own_x = move(0, tokens.at[micro], xs.at[micro])
     own_g = move(1, cotangent.at[micro], gs.at[micro])
+    gains[0:1, :] = norm1_gain[...].astype(jnp.float32)
+    gains[1:2, :] = norm2_gain[...].astype(jnp.float32)
     gain_sends = [
         send(2 + i, gains, gains_all.at[shard], device) for i, device in enumerate((core_mate, chip_mate, far_mate))
     ]
@@ -503,15 +516,22 @@
 
     def columns(ref, width):
         return ref.at[:, pl.ds(pl.multiple_of(member * width, 128), width)]
+
+    own_pair = pl.ds(pl.multiple_of(member // 2 * 128, 128), 128)
+    key_pair = key_in[:, own_pair].astype(jnp.float32)
+    value_pair = value_in[:, own_pair].astype(jnp.float32)
+    key_pair = jnp.where(member % 2 == 0, key_pair, pltpu.roll(key_pair, HDIM, 1))
+    value_pair = jnp.where(member % 2 == 0, pltpu.roll(value_pair, HDIM, 1), value_pair)
+    wkv_in[...] = jnp.where(lane_ids(key_pair.shape) < HDIM, key_pair, value_pair).astype(jnp.bfloat16)
 
     chip_shard = (1 - shard // 2) * 2 + shard % 2
     width_q, width_f = wq.shape[2], wg.shape[2]
     parts = (
         (columns(wq_in, width_q), wq),
         (wkv_in, wkv),
+        (columns(wd_in, width_f), wd),
         (columns(wg_in, width_f), wg),
         (columns(wu_in, width_f), wu),
-        (columns(wd_in, width_f), wd),
     )
 
     def weight_out(i):
@@ -548,8 +568,15 @@
         wo_copy(wo_core, wo_in, core_mate).start()
         wo_here.start()
 
+    for i in (2, 3, 4):
+        started[i] = weight_out(i)
+
     first_len = seq_len[slot_order[2 * (shard * MB + micro)]]
     both_len = first_len + seq_len[slot_order[2 * (shard * MB + micro) + 1]]
+    angles = row_positions(window, 0, group, tok_rows, first_len, both_len)[1].astype(jnp.float32) * inverse[...]
+    cosine[...] = jnp.cos(angles)
+    sine[...] = jnp.sin(angles)
+    bias[...] = pair_bias(window, group, tok_rows, first_len, both_len)
 
     own_gain.wait()
     for copy in gain_sends:
@@ -573,8 +600,6 @@
     for i in (0, 1):
         started[i][0].wait()
         on.append(weight_on(i))
-    for i in (2, 3, 4):
-        started[i] = weight_out(i)
     for i in (0, 1):
         started[i][1].wait()
         started[i][2].wait()
@@ -608,7 +633,6 @@
         project(members[i])
     gather_g = [send(26 + i, upstream.at[member], upstream.at[member], device) for i, device in enumerate(peers)]
 
-    bias[...] = pair_bias(window, group, tok_rows, first_len, both_len)
     key_twice = keys[...]
     value_twice = values[...]
     lower = lane_ids(value_twice.shape) < HDIM
@@ -624,6 +648,12 @@
         total += plain_dot(value_high, softmax_columns(key_high, pair, bias[...]).astype(jnp.bfloat16))
         attended[:, lanes] = total.T.astype(jnp.bfloat16)
 
+    on = []
+
+    def pass_on(i):
+        started[i][0].wait()
+        on.append(weight_on(i))
+
     @pl.when(same_chip & same_core)
     def _():
         wo_copy(wo_x, wo_in, chip_mate).wait_send()
@@ -654,6 +684,7 @@
         sent[i] = project_out(members[i]).astype(jnp.bfloat16)
         sums[i] = send(29 + i, sent.at[i], got.at[i], peers[i])
     total = inputs + project_out(member)
+    pass_on(2)
     for i in (0, 1, 2):
         sums[i].wait()
         total += got[i].astype(jnp.float32)
@@ -662,10 +693,9 @@
     gather_two = [
         send(32 + i, normed_two.at[member], normed_two.at[member], device) for i, device in enumerate(peers)
     ]
-    on = []
+    for i in (3, 4):
+        pass_on(i)
     for i in (2, 3, 4):
-        started[i][0].wait()
-        on.append(weight_on(i))
         started[i][1].wait()
         started[i][2].wait()
     for copy in (*on, *gather_g, *gather_two):
@@ -702,10 +732,14 @@
             shape((KV, D // KV, width_f), low),
             shape((KV, D // KV, width_f), low),
             shape((KV, 8, D // KV), jnp.float32),
+            shape((window, 2 * HDIM), jnp.float32),
+            shape((window, 2 * HDIM), jnp.float32),
         ),
-        in_specs=[anywhere, anywhere, smem, smem, vmem, anywhere, anywhere, anywhere, anywhere, anywhere, anywhere, vmem, vmem],
-        out_specs=tuple([vmem] * 12 + [anywhere] * 3 + [vmem]),
+        in_specs=[anywhere] * 2 + [smem] * 2 + [vmem] * 5 + [anywhere] * 5,
+        out_specs=tuple([vmem] * 12 + [anywhere] * 3 + [vmem] * 3),
         scratch_shapes=[
+            pltpu.VMEM((8, D // KV), jnp.float32),
+            pltpu.VMEM((D // KV, 2 * HDIM), low),
             pltpu.VMEM((MB, tok_rows, D), low),
             pltpu.VMEM((group - 1, own_rows, D), low),
             pltpu.VMEM((group - 1, own_rows, D), low),
@@ -827,6 +861,8 @@
         return copy
 
     ffn_parts = (gate_part, up_part, down_part)
+    width_f = from_half.shape[-1]
+    own_ffn = pl.ds(pl.multiple_of(member * width_f, 128), width_f)
     sums_two = {i: send(6 + i, d_two_part.at[members[i]], got_two.at[i], peers[i]) for i in (2, 0, 1)}
     own_load = move(0, d_two_part.at[member], own_two)
     core_copies = {}
@@ -850,16 +886,10 @@
     )
     kept = [move(4 + i, source, target) for i, (source, target) in enumerate(inputs_in)]
 
-    units = []
-    for w in range(3):
-        units.append((w, 1 - chip, 1 - micro))
-    for w in (0, 1):
-        units.append((w, chip, 1 - micro))
-        units.append((w, 1 - chip, micro))
-    units.append((2, chip, 1 - micro))
-    units.append((2, 1 - chip, micro))
-    for w in range(3):
-        units.append((w, chip, micro))
+    units = [(w, 1 - chip, 1 - micro) for w in range(3)]
+    units += [(w, chip, 1 - micro) for w in range(3)]
+    units += [(w, 1 - chip, micro) for w in range(3)]
+    units += [(w, chip, micro) for w in range(3)]
     turn_of = {"next": 0, "load": None}
 
     def load_unit(number):
@@ -918,12 +948,12 @@
 
         for i in range(group - 1):
             last_copies.append(
-                send(18 + 3 * w + i, from_chip.at[w, micro, members[i]], ffn_grad.at[w, member], peers[i])
+                send(18 + 3 * w + i, from_chip.at[w, micro, members[i]], ffn_grad.at[w, :, own_ffn], peers[i])
             )
-        here_copies.append(move(17 + w, from_chip.at[w, micro, member], ffn_grad.at[w, member]))
-
-    chip_unit(0, 1 - micro, 0)
-    chip_unit(1, 1 - micro, 0)
+        here_copies.append(move(17 + w, from_chip.at[w, micro, member], ffn_grad.at[w, :, own_ffn]))
+
+    for w in range(3):
+        chip_unit(w, 1 - micro, 0)
 
     kept[0].wait()
     kept[1].wait()
@@ -945,7 +975,7 @@
     first_len = seq_len[slot_order[2 * (shard * MB + micro)]]
     both_len = first_len + seq_len[slot_order[2 * (shard * MB + micro) + 1]]
     bias[...] = pair_bias(window, group, tok_rows, first_len, both_len)
-    chip_unit(2, 1 - micro, 0)
+    half_unit(0)
 
     for i in (2, 3, 4, 5, 6):
         kept[i].wait()
@@ -955,6 +985,7 @@
         d_attended[place_rows, :] = contract_cols(d_full[rows], wo[...]).astype(jnp.bfloat16)
 
     attention_grad(member)
+    half_unit(1)
     for i, copy in enumerate(gather):
         copy.wait()
         attention_grad(members[i])
@@ -976,11 +1007,6 @@
     def _():
         out_by_core.start()
 
-    half_unit(0)
-    chip_unit(0, micro, 1)
-    half_unit(1)
-    chip_unit(1, micro, 1)
-
     @pl.when(jnp.logical_not(same_core))
     def _():
         out_by_core.wait_send()
@@ -997,6 +1023,10 @@
     @pl.when(same_core & jnp.logical_not(same_chip))
     def _():
         out_by_chip.start()
+
+    half_unit(2)
+    for w in range(3):
+        chip_unit(w, micro, 1)
 
     key_twice, value_twice = keys[...], values[...]
     lower = lane_ids(key_twice.shape) < HDIM
@@ -1024,10 +1054,7 @@
         grad_rot = total.T * HDIM**-0.5
         d_query[:, lanes] = (grad_rot * cosine[...] + turn_back(grad_rot * sine[...])).astype(jnp.bfloat16)
 
-    pl.loop(0, width_q // 256)(attention_pair)
-    half_unit(2)
-    chip_unit(2, micro, 1)
-    pl.loop(width_q // 256, width_q // 128)(attention_pair)
+    pl.loop(0, width_q // 128)(attention_pair)
 
     fold = lambda sums: jnp.where(lower, sums[0] + pltpu.roll(sums[1], HDIM, 1), 0.0)
     key_grad, value_grad = fold(key_sum), fold(value_sum)
@@ -1180,9 +1207,10 @@
         total += late_chip[micro, t].astype(jnp.float32) + late_half[t].astype(jnp.float32)
         late_chip[micro, t] = total.astype(jnp.bfloat16)
 
+    own_late = pl.ds(pl.multiple_of(member * d_all.shape[1], 128), d_all.shape[1])
     for i in range(group - 1):
-        last_copies.append(send(54 + i, late_chip.at[micro, members[i]], qkv_grad.at[member], peers[i]))
-    here_copies.append(move(25, late_chip.at[micro, member], qkv_grad.at[member]))
+        last_copies.append(send(54 + i, late_chip.at[micro, members[i]], qkv_grad.at[:, own_late], peers[i]))
+    here_copies.append(move(25, late_chip.at[micro, member], qkv_grad.at[:, own_late]))
     take(1, give_grad, input_grad)
     for copy in gain_all:
         copy.wait()
@@ -1219,8 +1247,8 @@
         out_shape=(
             shape((MB, tok_rows, D), full),
             shape((MB, tok_rows, D), full),
-            shape((3, group, tok_rows, width_f), low),
-            shape((group, tok_rows, width_l), low),
+            shape((3, tok_rows, FF), low),
+            shape((tok_rows, group * width_l), low),
             shape((tok_rows, D), low),
             shape((8, D), full),
         ),
@@ -1305,22 +1333,7 @@
     tok_rows = tokens.shape[1]
     window = n_sp * tok_rows
     own_rows = MB * tok_rows
-    first_len = seq_len[slot_order[2 * (shard * MB + micro)]]
-    second_len = seq_len[slot_order[2 * (shard * MB + micro) + 1]]
-    place = row_places((window,), 0, group, tok_rows)
-    anchor = jnp.where(place < first_len, 0, jnp.where(place < first_len + second_len, first_len, first_len + second_len))
-    inverse = ROPE_BASE ** (-2.0 * jnp.arange(HDIM // 2, dtype=jnp.float32) / HDIM)
-    angles = (place - anchor).astype(jnp.float32)[:, None] * jnp.tile(inverse, 4)[None, :]
-    cosine, sine = jnp.cos(angles), jnp.sin(angles)
-
-    def columns(weight):
-        width = weight.shape[1] // group
-        return lax.dynamic_slice_in_dim(weight, member * width, width, 1)
-
-    gains = jnp.concatenate(
-        [norm1_gain[None], norm2_gain[None], jnp.zeros((6, norm1_gain.shape[0]), jnp.bfloat16)]
-    ).astype(jnp.float32)
-    kv_weight = jnp.concatenate([columns(key_weight), columns(value_weight)], axis=1)
+    inverse = np.float32(ROPE_BASE) ** (np.arange(HDIM // 2, dtype=np.float32) * np.float32(-2.0 / HDIM))
     heads = HEADS // group
     (
         own_tokens,
@@ -1339,10 +1352,13 @@
         w_up,
         w_down,
         gains,
+        cosine,
+        sine,
     ) = front(
         n_sp, tok_rows, heads,
-        tokens, cotangent, seq_len, slot_order, gains,
-        query_weight, kv_weight, output_weight, gate_weight, up_weight, down_weight, cosine, sine,
+        tokens, cotangent, seq_len, slot_order, norm1_gain[None], norm2_gain[None],
+        jnp.asarray(np.tile(inverse, 4)[None]), key_weight, value_weight,
+        query_weight, output_weight, gate_weight, up_weight, down_weight,
     )
     upstream_rows, normed_rows = upstream_low.reshape(window, D), normed_two.reshape(window, D)
     gate_full, up_full, down_full = (w.reshape(D, -1) for w in (w_gate, w_up, w_down))
@@ -1369,22 +1385,23 @@
     )
     gain_own = lax.dynamic_slice_in_dim(gain_sum, (shard * n_sp + rank) * tok_rows, tok_rows, 1)
 
-    def side_by_side(pieces):
-        return jnp.swapaxes(pieces, 0, 1).reshape(tok_rows, -1).astype(jnp.float32)
+    def part_of(first, width):
+        pieces = qkv_grad.reshape(tok_rows, group, -1)[:, :, first : first + width]
+        return pieces.reshape(tok_rows, group * width).astype(jnp.float32)
 
     width_q = heads * HDIM
     return (
         block,
         d_inputs,
         gain_own[0],
-        side_by_side(qkv_grad[:, :, :width_q]),
-        side_by_side(qkv_grad[:, :, width_q : width_q + HDIM]),
-        side_by_side(qkv_grad[:, :, width_q + HDIM :]),
+        part_of(0, width_q),
+        part_of(width_q, HDIM),
+        part_of(width_q + HDIM, HDIM),
         output_grad.astype(jnp.float32),
         gain_own[1],
-        side_by_side(ffn_grad[0]),
-        side_by_side(ffn_grad[1]),
-        side_by_side(ffn_grad[2]),
+        ffn_grad[0].astype(jnp.float32),
+        ffn_grad[1].astype(jnp.float32),
+        ffn_grad[2].astype(jnp.float32),
     )
 
 

time: 462 us -> 430 us (0.931)
  Pallas kernels: 382 us -> 361 us
  between operations: 6.55 us -> 1.02 us
  local copies, waits for them, and re-layouts: 15.3 us -> 10.1 us
    pallas_call x1, Pallas kernels: 169 us -> 144 us  [front(): pl.pallas_call(functools.partial(front_kernel, n_sp), out_shape=(shape((M...]
    convert_element_type x8 -> x2, local copies, waits for them, and re-layouts: 6.2 us -> 1.53 us  [part_of(): return pieces.reshape(tok_rows, group * width).astype(jnp.float32)]
where the time goes in v4:
time: 430 us; the launch traced here: 422 us
  Pallas kernels  361 us (84%)
  matrix products  46.2 us (11%)
  local copies, waits for them, and re-layouts  10.1 us (2%)
    pallas_call x1, Pallas kernels, back(): pl.pallas_call(functools.partial(back_kernel, n_sp), out_shape=(shape((MB...  217 us
    pallas_call x1, Pallas kernels, front(): pl.pallas_call(functools.partial(front_kernel, n_sp), out_shape=(shape((M...  144 us
    dot_general x3, matrix products, plain_dot(): return jnp.dot(left_side, right_side, preferred_element_type=jnp.float32)  17.6 us
    dot_general x3, matrix products, contract_rows(): lax.dot_general(left_side, right_side, (((0,), (0,)), ((), ())), preferre...  15.8 us
    dot_general x3, matrix products, contract_cols(): lax.dot_general(left_side, right_side, (((1,), (1,)), ((), ())), preferre...  12.8 us

profile of v4, /device:TPU:0, one launch (start us, length us, event | category | flops | bytes accessed | tf_op | source)
XLA Modules:
  0.0 421.9 jit_solution(4837089048905001734)
XLA Ops:
  0.6 1.3 broadcast_in_dim.6.norm1_gain
  1.9 1.3 broadcast_in_dim.7.norm2_gain
  3.2 144.4 %front.1 = (bf16[2,64,2048]{2,1,0:T(8,128)(2,1)}, bf16[4,128,2048]{2,1,0:T(8,128)(2,1)}, bf16[4,128,2048]{2,1,0:T(8,128)(2,1)}, bf16[512,512]{1,0:T(8,128)(2,1)}...) custom-call(bf16[2,64,2048]{2,1,0:T(8,128)(2,1)} %tokens.1, ...), custom_call_target="tpu_custom_call" | custom-call | flops 8000000000 | bytes 40000000 | tf_op jit(solution)/shard_map/front/pallas_call | solution.py:716
  147.6 0.0 slice-start
  147.6 6.5 %fusion.2 = f32[512,1408]{1,0:T(8,128)S(1)} fusion(bf16[512,2048]{1,0:T(8,128)(2,1)} %bitcast.62, bf16[2048,1408]{1,0:T(8,128)(2,1)} %bitcast.53), kind=kOutput, calls=%fused_computation.20 | convolution fusion | flops 2952790016 | bytes 10747904 | tf_op jit(solution)/shard_map/dot_general | solution.py:26
  154.1 0.0 slice-start.1
  154.2 0.0 slice-start.2
  154.2 5.1 %fusion.1 = f32[512,1408]{1,0:T(8,128)} fusion(bf16[512,2048]{1,0:T(8,128)(2,1)S(1)} %bitcast.60, bf16[2048,1408]{1,0:T(8,128)(2,1)S(1)} %bitcast.47), kind=kOutput, calls=%fused_computation.19 | convolution fusion | flops 2952790016 | bytes 10747904 | tf_op jit(solution)/shard_map/dot_general | solution.py:26
  159.3 0.0 copy-done.6
  159.3 0.0 slice-start.3
  159.3 6.0 %multiply_convert_fusion = (bf16[512,1408]{1,0:T(8,128)(2,1)S(1)}, bf16[512,1408]{1,0:T(8,128)(2,1)S(1)}, bf16[512,1408]{1,0:T(8,128)(2,1)S(1)}) fusion(f32[512,1408]{1,0:T(8,128)S(1)} %fusion.2, f32[512,1408]{1,0:T(8,128)} %fusion.1, bf16[512,2048]{1,0:T(8,128)(2,1)S(1)} %bitcast.63, bf16[2048,1408]{1,0:T(8,128)(2,1)S(1)} %bitcast.51), kind=kOutput, calls=%fused_computation.5 | convolution fusion | flops 2963603456 | bytes 17956864 | tf_op jit(solution)/shard_map/dot_general | solution.py:26
  165.3 3.4 fusion.3
  168.8 4.7 %add_convert_fusion = bf16[512,2048]{1,0:T(8,128)(2,1)} fusion(f32[512,2048]{1,0:T(8,128)S(1)} %fusion.3, bf16[512,1408]{1,0:T(8,128)(2,1)S(1)} %get-tuple-element.61, bf16[2048,1408]{1,0:T(8,128)(2,1)S(1)} %bitcast.52), kind=kOutput, calls=%fused_computation.3 | convolution fusion | flops 2954887168 | bytes 13500416 | tf_op jit(solution)/shard_map/dot_general | solution.py:36
  173.5 4.7 %convolution_convert_fusion.3.block_part = bf16[4,128,2048]{2,1,0:T(8,128)(2,1)} fusion(bf16[4,128,1408]{2,1,0:T(8,128)(2,1)S(1)} %bitcast.67, bf16[2048,1408,1]{1,0,2:T(8,128)(2,1)S(1)} %bitcast.48), kind=kOutput, calls=%fused_computation.4 | convolution fusion | flops 2953838592 | bytes 9306112 | tf_op jit(solution)/shard_map/dot_general | solution.py:36
  178.2 5.3 %convolution_convert_fusion.2 = bf16[2048,1408]{1,0:T(8,128)(2,1)} fusion(bf16[512,2048]{1,0:T(8,128)(2,1)S(1)} %bitcast.64, bf16[512,1408]{1,0:T(8,128)(2,1)S(1)} %get-tuple-element.60), kind=kOutput, calls=%fused_computation.2 | convolution fusion | flops 2955673600 | bytes 9306112 | tf_op jit(solution)/shard_map/dot_general | solution.py:30
  183.4 5.3 %convolution_convert_fusion.1 = bf16[2048,1408]{1,0:T(8,128)(2,1)} fusion(bf16[512,2048]{1,0:T(8,128)(2,1)S(1)} %bitcast.65, bf16[512,1408]{1,0:T(8,128)(2,1)S(1)} %get-tuple-element.61), kind=kOutput, calls=%fused_computation.1 | convolution fusion | flops 2955673600 | bytes 9306112 | tf_op jit(solution)/shard_map/dot_general | solution.py:30
  188.7 5.2 %convolution_convert_fusion = bf16[2048,1408]{1,0:T(8,128)(2,1)} fusion(bf16[512,2048]{1,0:T(8,128)(2,1)S(1)} %bitcast.61, bf16[512,1408]{1,0:T(8,128)(2,1)S(1)} %get-tuple-element.59), kind=kOutput, calls=%fused_computation | convolution fusion | flops 2955673600 | bytes 9306112 | tf_op jit(solution)/shard_map/dot_general | solution.py:30
  193.9 217.0 %back.1 = (f32[2,64,2048]{2,1,0:T(8,128)}, f32[2,64,2048]{2,1,0:T(8,128)}, bf16[3,64,5632]{2,1,0:T(8,128)(2,1)}, bf16[64,2560]{1,0:T(8,128)(2,1)}, bf16[64,2048]{1,0:T(8,128)(2,1)}, /*index=5*/f32[8,2048]{1,0:T(8,128)}) custom-call(bf16[4,128,2048]{2,1,0:T(8,128)(2,1)} %bitcast.66, bf16[4,128,2048]{2,1,0:T(8,128)(2,1)} %convolution_convert_fusion.3.block_part, ...), custom_call_target="tpu_custom_call" | custom-call | flops 14000000000 | bytes 60000000 | tf_op jit(solution)/shard_map/back/pallas_call | solution.py:1245
  411.0 0.0 copy-start.3
  411.0 0.0 copy-start
  411.0 0.9 constant_dynamic-slice_fusion
  411.9 0.5 slice_bitcast_fusion
  412.4 1.0 reshape.78
  413.5 1.0 copy.25
  414.5 0.1 slice_convert_fusion.1
  414.6 0.8 reshape.80
  415.4 0.8 reshape.81
  416.1 0.8 convert_element_type.80
  417.0 2.1 bitcast_convert_fusion
  419.1 1.0 copy.28
  420.1 0.6 copy-done.1
  420.7 1.0 copy.29
  (17 shorter events, 0.1 us)
Async XLA Ops:
  147.6 6.6 %copy-start.4 = (bf16[4,512,1408]{2,1,0:T(8,128)(2,1)S(1)}, bf16[4,512,1408]{2,1,0:T(8,128)(2,1)}, u32[]{:S(2)}) copy-start(bf16[4,512,1408]{2,1,0:T(8,128)(2,1)} %get-tuple-element.36) | copy-start | bytes 17301508
  147.6 6.6 %copy-start.5 = (bf16[4,128,2048]{2,1,0:T(8,128)(2,1)S(1)}, bf16[4,128,2048]{2,1,0:T(8,128)(2,1)}, u32[]{:S(2)}) copy-start(bf16[4,128,2048]{2,1,0:T(8,128)(2,1)} %get-tuple-element.35.upstream_in) | copy-start | bytes 6291460
  147.6 11.7 %slice-start = ((s8[5767168]{0:T(1024)(128)(4,1)}), s8[4194304]{0:T(1024)(128)(4,1)S(1)}, s32[]{:S(2)}) async-start(s8[5767168]{0:T(1024)(128)(4,1)} %bitcast.49), calls=%async_computation | async-start | bytes 8388608
  154.1 5.1 %slice-start.1 = ((s8[5767168]{0:T(1024)(128)(4,1)}), s8[1572864]{0:T(1024)(128)(4,1)S(1)}, s32[]{:S(2)}) async-start(s8[5767168]{0:T(1024)(128)(4,1)} %bitcast.49), calls=%async_computation.1 | async-start | bytes 3145728
  154.2 5.1 %copy-start.6 = (bf16[4,128,2048]{2,1,0:T(8,128)(2,1)S(1)}, bf16[4,128,2048]{2,1,0:T(8,128)(2,1)}, u32[]{:S(2)}) copy-start(bf16[4,128,2048]{2,1,0:T(8,128)(2,1)} %get-tuple-element.37) | copy-start | bytes 6291460
  154.2 11.1 %slice-start.2 = ((s8[5767168]{0:T(1024)(128)(4,1)}), s8[4194304]{0:T(1024)(128)(4,1)S(1)}, s32[]{:S(2)}) async-start(s8[5767168]{0:T(1024)(128)(4,1)} %bitcast.54), calls=%async_computation.2 | async-start | bytes 8388608
  159.3 6.0 %slice-start.3 = ((s8[5767168]{0:T(1024)(128)(4,1)}), s8[1572864]{0:T(1024)(128)(4,1)S(1)}, s32[]{:S(2)}) async-start(s8[5767168]{0:T(1024)(128)(4,1)} %bitcast.54), calls=%async_computation.3 | async-start | bytes 3145728
  411.0 5.2 %copy-start.3 = (bf16[64,2048]{1,0:T(8,128)(2,1)S(1)}, bf16[64,2048]{1,0:T(8,128)(2,1)}, u32[]{:S(2)}) copy-start(bf16[64,2048]{1,0:T(8,128)(2,1)} %get-tuple-element.57) | copy-start | bytes 786436
  411.0 6.0 %copy-start = (bf16[3,64,5632]{2,1,0:T(8,128)(2,1)S(1)}, bf16[3,64,5632]{2,1,0:T(8,128)(2,1)}, u32[]{:S(2)}) copy-start(bf16[3,64,5632]{2,1,0:T(8,128)(2,1)} %get-tuple-element.58) | copy-start | bytes 6488068
  417.0 2.2 copy-start.2
  419.1 1.6 copy-start.1
